TPU v7x, 32 devices: a whole 2x2x4 slice. The times are simulated.
32 devices in a mesh: hop: 2 (over x), batch: 16 (over z, y, core).
Axes of the slice: x: 2, y: 2, z: 4, core: 2. Of those that a mesh axis runs over, the one named last changes fastest.
Arguments:
- section_rows: bfloat16 [2, 2048, 2048], P('hop', 'batch'), may hold values from -6 to 6
- weights: bfloat16 [2, 2048, 2048], P('hop'), may hold values from -0.125 to 0.125
- relation_table: bfloat16 [256, 2048], replicated, may hold values from -4 to 4
- relation_ids: int32 [2048], P('batch'), may hold values from 0 to 255
Outputs:
- weight_grad: float32 [2, 2048, 2048], P('hop', 'batch')
- relation_grad: float32 [256, 2048], P(('hop', 'batch'))
- query_grad: bfloat16 [2048, 2048], P('batch')
Inputs may be any that keep to these rules, and one draw needn't show every extreme that they name: `relation_ids`: relation index of each query.
All inputs are finite; a program needn't handle non-finite values.
Results may differ from a plain program's by a relative error of at most 0.0064.
Values may be sent and summed in bfloat16 or wider, within the bound.
No kernel may reach another device: no remote copies, remote signals or barrier semaphores. Data moves between devices by JAX's collectives and lax.ppermute only.
A program may use at most 128 MiB of HBM per device.

v0:
```python
import jax
import jax.numpy as jnp
from jax import lax
from jax.experimental import pallas as pl
from jax.experimental.pallas import tpu as pltpu
from jax.sharding import Mesh
from jax.sharding import PartitionSpec as P

F32 = jnp.float32
BF16 = jnp.bfloat16
TILE = 256
GRANT = 16 * 1024 * 1024


def dot(a, b, ca, cb):
    return lax.dot_general(a, b, (((ca,), (cb,)), ((), ())), preferred_element_type=F32)


def swap_core(block):
    return lax.ppermute(block, "core", [(0, 1), (1, 0)])


def mix(q_re, q_im, r_re, r_im):
    return (q_re * r_re - q_im * r_im).astype(BF16), (q_re * r_im + q_im * r_re).astype(BF16)


def at(step, base=0):
    return pl.ds(pl.multiple_of(base + step * TILE, TILE), TILE)


def lead_body(rows, weight, onehot, table, query, rel):
    half = weight.shape[0] // 2
    steps = half // TILE
    for step in range(steps):
        span = pl.ds(step * TILE, TILE)
        r_re = dot(onehot[...], table[:, at(step)], 1, 0)
        r_im = dot(onehot[...], table[:, at(step, half)], 1, 0)
        q_re = dot(rows[...], weight[at(step)], 1, 1).astype(BF16)
        q_im = dot(rows[...], weight[at(step, half)], 1, 1).astype(BF16)
        query[0, :, span], query[1, :, span] = q_re, q_im
        rel[0, :, span], rel[1, :, span] = r_re.astype(BF16), r_im.astype(BF16)


def lead(rows, weight, onehot, table):
    rows_dev, hidden = rows.shape
    width = weight.shape[0]
    half = width // 2
    count_rel = table.shape[0]
    vmem = pl.BlockSpec(memory_space=pltpu.VMEM)
    pair = jax.ShapeDtypeStruct((2, rows_dev, half), BF16)
    return pl.pallas_call(
        lead_body,
        out_shape=(pair, pair),
        in_specs=[vmem] * 4,
        out_specs=(vmem,) * 2,
        compiler_params=pltpu.CompilerParams(vmem_limit_bytes=GRANT),
        cost_estimate=pl.CostEstimate(
            flops=2 * rows_dev * width * (hidden + count_rel), bytes_accessed=2 * width * hidden, transcendentals=0
        ),
    )(rows, weight, onehot, table)


def trail_body(first, query, rows, weight, rel, onehot, right, query_grad, give, keep, mixed, hidden):
    width = weight.shape[0]
    half = width // 2
    is_first = first[0] == 1
    owned = give.shape[0]

    def make_mixed(step, carry):
        mixed[:, at(step)], mixed[:, at(step, half)] = mix(
            query[0, :, at(step)].astype(F32), query[1, :, at(step)].astype(F32),
            rel[0, :, at(step)].astype(F32), rel[1, :, at(step)].astype(F32),
        )
        return carry

    lax.fori_loop(0, half // TILE, make_mixed, 0)

    def make_hidden(step, carry):
        pre = dot(mixed[...], weight[:, at(step)], 1, 0)
        sig = jax.nn.sigmoid(pre)
        cot = rows[:, at(step)]
        grad = (cot.astype(F32) * (sig * (1.0 + pre * (1.0 - sig)))).astype(BF16)
        hidden[:, at(step)] = grad
        right[:, at(step)] = jnp.where(is_first, cot, grad)
        return carry

    lax.fori_loop(0, weight.shape[1] // TILE, make_hidden, 0)

    def make_query(step, carry):
        gz_re = dot(hidden[...], weight[at(step), :], 1, 1)
        gz_im = dot(hidden[...], weight[at(step, half), :], 1, 1)
        r_re, r_im = rel[0, :, at(step)].astype(F32), rel[1, :, at(step)].astype(F32)
        query_grad[:, at(step)] = (gz_re * r_re + gz_im * r_im).astype(BF16)
        query_grad[:, at(step, half)] = (gz_im * r_re - gz_re * r_im).astype(BF16)
        a, b = query[0, :, at(step)].astype(F32), query[1, :, at(step)].astype(F32)
        for base, grad in ((0, gz_re * a + gz_im * b), (half, gz_im * a - gz_re * b)):
            head = grad.astype(BF16)
            rest = (grad - head.astype(F32)).astype(BF16)
            total = dot(onehot[...], head, 1, 0) + dot(onehot[...], rest, 1, 0)
            give[:, at(step, base)] = total[:owned]
            keep[:, at(step, base)] = total[owned:]
        return carry

    lax.fori_loop(0, half // TILE, make_query, 0)


def trail(first, query, rows, weight, rel, onehot):
    rows_dev, hidden = rows.shape
    width = weight.shape[0]
    count_rel = onehot.shape[0]
    vmem = pl.BlockSpec(memory_space=pltpu.VMEM)
    flops = 4 * rows_dev * width * hidden + 4 * rows_dev * count_rel * width
    return pl.pallas_call(
        trail_body,
        out_shape=(
            jax.ShapeDtypeStruct((rows_dev, hidden), BF16),
            jax.ShapeDtypeStruct((rows_dev, width), BF16),
            jax.ShapeDtypeStruct((count_rel // 2, width), F32),
            jax.ShapeDtypeStruct((count_rel // 2, width), F32),
            jax.ShapeDtypeStruct((rows_dev, width), BF16),
        ),
        in_specs=[pl.BlockSpec(memory_space=pltpu.SMEM)] + [vmem] * 5,
        out_specs=(vmem,) * 5,
        scratch_shapes=[pltpu.VMEM((rows_dev, hidden), BF16)],
        compiler_params=pltpu.CompilerParams(vmem_limit_bytes=GRANT),
        cost_estimate=pl.CostEstimate(
            flops=flops, bytes_accessed=4 * width * hidden, transcendentals=rows_dev * hidden
        ),
    )(first, query, rows, weight, rel, onehot)


def local(section_rows, weights, relation_table, relation_ids):
    rows = section_rows[0]
    weight = weights[0]
    rows_dev, width = rows.shape
    half = width // 2
    count_rel = relation_table.shape[0]
    chips = lax.axis_size("chip")
    first = lax.axis_index("hop") == 0
    core = lax.axis_index("core")
    chip = lax.axis_index("chip")
    total_rows = rows_dev * chips * 2
    cols = width // chips
    owned = count_rel // (4 * chips)

    def columns(left):
        return left.reshape(left.shape[0], chips, cols).transpose(1, 0, 2)

    onehot = (relation_ids[:, None] == lax.iota(jnp.int32, count_rel)[None, :]).astype(BF16)
    number = lax.iota(jnp.int32, count_rel)
    side = number // (count_rel // 2)
    dest = number % (count_rel // 2) // (2 * owned)
    hop = number % (2 * owned) // owned
    which_core = jnp.where(side == 1, core, 1 - core)
    relation = ((hop * chips + dest) * 2 + which_core) * owned + number % owned
    onehot_t = (relation[:, None] == relation_ids[None, :]).astype(BF16)

    own_query, rel = lead(rows, weight, onehot, relation_table)
    query = lax.ppermute(own_query, "hop", [(0, 1)])
    right, grad_query, rel_give, rel_keep, mixed = trail(
        first.astype(jnp.int32).reshape(1), query, rows, weight, rel, onehot_t
    )
    query_back = lax.ppermute(grad_query, "hop", [(1, 0)])
    query_grad = jnp.where(first, query_back, grad_query)
    rel_chip = (rel_keep + swap_core(rel_give)).astype(BF16).reshape(chips, 2, owned, width)
    rel_back = lax.ppermute(rel_chip[:, 0], "hop", [(1, 0)])

    def chip_at(place):
        place = lax.rem(place, chips)
        return jnp.where(place < (chips + 1) // 2, 2 * place, 2 * (chips - place) - 1)

    ring = list(range(0, chips, 2)) + list(range(1, chips, 2))[::-1]
    place = jnp.where(lax.rem(chip, 2) == 0, chip // 2, chips - 1 - chip // 2)
    up = [(ring[i], ring[(i + 1) % chips]) for i in range(chips)]
    down = [(b, a) for a, b in up]
    blocks = [(right, 0, 0)]
    fwd = bwd = right
    for s in range(1, (chips + 1) // 2):
        fwd = lax.ppermute(fwd, "chip", up)
        bwd = lax.ppermute(bwd, "chip", down)
        blocks += [(fwd, chips - s, 0), (bwd, s, 0)]
    if chips % 2 == 0:
        mid = rows_dev // 2
        blocks.append((lax.ppermute(fwd[:mid], "chip", up), chips // 2, 0))
        blocks.append((lax.ppermute(bwd[mid:], "chip", down), chips // 2, mid))

    rel_own = jnp.where(first, rel_back, rel_chip[:, 1]).reshape(chips, owned, chips, cols)
    rel_own = rel_own.transpose(0, 2, 1, 3).reshape(chips, owned * chips, cols)
    left = columns(jnp.where(first, query_back, mixed))
    sent = jnp.concatenate([left, rel_own], axis=1)
    sent, _ = lax.optimization_barrier((sent, (blocks[3][0], blocks[4][0])))
    received = lax.all_to_all(sent, "chip", 0, 0, tiled=True)
    left_cols, rel_rows = received[:, :rows_dev], received[:, rows_dev:]
    rel_sum = jnp.sum(rel_rows.astype(F32), axis=0) * jnp.sqrt(F32(count_rel) / F32(total_rows))
    relation_grad = rel_sum.reshape(chips, owned, cols).transpose(1, 0, 2).reshape(owned, width)

    partial = jnp.zeros((cols, width), F32)
    for block, step, base in blocks:
        left = lax.dynamic_index_in_dim(left_cols, chip_at(place + step), 0, keepdims=False)
        partial = partial + dot(left[base:base + block.shape[0]], block, 0, 0)
    partial = partial.reshape(2, cols // 2, width)
    keep = lax.dynamic_index_in_dim(partial, core, 0, keepdims=False)
    give = lax.dynamic_index_in_dim(partial, 1 - core, 0, keepdims=False)
    weight_grad = (keep + swap_core(give)) * (1.0 / jnp.sqrt(F32(total_rows)))
    return weight_grad[None], relation_grad, query_grad


def solution(mesh):
    hops, batch = mesh.devices.shape
    fine = Mesh(mesh.devices.reshape(hops, batch // 2, 2), ("hop", "chip", "core"))
    rows = ("chip", "core")
    return jax.shard_map(
        local,
        mesh=fine,
        in_specs=(P("hop", rows, None), P("hop", None, None), P(), P(rows)),
        out_specs=(P("hop", rows, None), P(("hop", "chip", "core"), None), P(rows, None)),
        check_vma=False,
    )
```

profile of v0, /device:TPU:9, one launch (start us, length us, event | category | flops | bytes accessed | tf_op | source)
XLA Modules:
  0.0 120.1 jit_solution(7908758156848112952)
XLA Ops:
  0.6 0.7 fusion.8.onehot
  1.4 0.0 copy-start
  1.4 3.4 %copy-done = bf16[1,2048,2048]{2,1,0:T(8,128)(2,1)S(1)} copy-done((bf16[1,2048,2048]{2,1,0:T(8,128)(2,1)S(1)}, bf16[1,2048,2048]{2,1,0:T(8,128)(2,1)}, u32[]{:S(2)}) %copy-start) | copy-done | bytes 8388632
  4.8 1.0 copy-done.2
  5.8 1.2 %copy-done.4 = bf16[256,2048]{1,0:T(8,128)(2,1)S(1)} copy-done((bf16[256,2048]{1,0:T(8,128)(2,1)S(1)}, bf16[256,2048]{1,0:T(8,128)(2,1)}, u32[]{:S(2)}) %copy-start.4) | copy-done | bytes 1048600
  7.0 3.1 %shard_map.67 = (bf16[2,128,1024]{2,1,0:T(8,128)(2,1)S(1)}, bf16[2,128,1024]{2,1,0:T(8,128)(2,1)S(1)}) custom-call(bf16[128,2048]{1,0:T(8,128)(2,1)S(1)} %bitcast.78, bf16[2048,2048]{1,0:T(8,128)(2,1)S(1)} %bitcast.76, bf16[128,256]{1,0:T(8,128)(2,1)S(1)} %fusion.8.onehot, bf16[256,2048]{1,0:T(8,128)(2,1)S(1)} %copy-done.4), custom_call_target="tpu_custom_call" | custom-call | flops 1207959552 | bytes 8388608 | tf_op jit(solution)/shard_map/pallas_call | solution.py:51
  10.1 3.2 %collective-permute-start = (bf16[2,128,1024]{2,1,0:T(8,128)(2,1)S(1)}, bf16[2,128,1024]{2,1,0:T(8,128)(2,1)S(1)}, u32[]{:S(2)}, u32[]{:S(2)}) collective-permute-start(bf16[2,128,1024]{2,1,0:T(8,128)(2,1)S(1)} %get-tuple-element.11), channel_id=1, source_target_pairs={{0,16},{1,17},{2,18},{3,19},{4,20},{5,21},{6,22},{7,23},{8,24},{9,... | collective-permute-start | bytes 1572872 | tf_op jit(solution)/shard_map/ppermute | solution.py:159
  13.3 0.1 compare_convert_fusion.onehot
  13.4 10.4 %collective-permute-done.query = bf16[2,128,1024]{2,1,0:T(8,128)(2,1)S(1)} collective-permute-done((bf16[2,128,1024]{2,1,0:T(8,128)(2,1)S(1)}, bf16[2,128,1024]{2,1,0:T(8,128)(2,1)S(1)}, u32[]{:S(2)}, u32[]{:S(2)}) %collective-permute-start) | collective-permute-done | bytes 524320 | tf_op jit(solution)/shard_map/ppermute | solution.py:159
  23.8 3.4 %copy-done.1 = bf16[1,2048,2048]{2,1,0:T(8,128)(2,1)S(1)} copy-done((bf16[1,2048,2048]{2,1,0:T(8,128)(2,1)S(1)}, bf16[1,2048,2048]{2,1,0:T(8,128)(2,1)}, u32[]{:S(2)}) %copy-start.1) | copy-done | bytes 8388632
  27.2 7.8 %shard_map.68 = (bf16[128,2048]{1,0:T(8,128)(2,1)S(1)}, bf16[128,2048]{1,0:T(8,128)(2,1)S(1)}, f32[128,2048]{1,0:T(8,128)S(1)}, f32[128,2048]{1,0:T(8,128)S(1)}, bf16[128,2048]{1,0:T(8,128)(2,1)S(1)}) custom-call(s32[1]{0:T(128)} %bitcast.first, bf16[2,128,1024]{2,1,0:T(8,128)(2,1)S(1)} %collective-permute-done.query, bf16[128,2048]{1,0:T(8,128)(2,1)S(1)} %bitcast.79, ...), custom_call_target="tpu_custom_call" | custom-call | flops 2415919104 | bytes 16777216 | tf_op jit(solution)/shard_map/pallas_call | solution.py:113
  35.0 1.6 %collective-permute-start.2 = (f32[128,2048]{1,0:T(8,128)S(1)}, f32[128,2048]{1,0:T(8,128)S(1)}, u32[]{:S(2)}, u32[]{:S(2)}) collective-permute-start(f32[128,2048]{1,0:T(8,128)S(1)} %get-tuple-element.16), channel_id=1, source_target_pairs={{0,1},{1,0},{2,3},{3,2},{4,5},{5,4},{6,7},{7,6},{8,9},{9,8},{10,11... | collective-permute-start | bytes 3145736 | tf_op jit(solution)/shard_map/ppermute | solution.py:20
  36.6 1.3 %collective-permute-start.4 = (bf16[128,2048]{1,0:T(8,128)(2,1)S(1)}, bf16[128,2048]{1,0:T(8,128)(2,1)S(1)}, u32[]{:S(2)}, u32[]{:S(2)}) collective-permute-start(bf16[128,2048]{1,0:T(8,128)(2,1)S(1)} %get-tuple-element.17), channel_id=1, source_target_pairs={{0,4},{4,8},{8,12},{12,14},{14,10},{10,6},{6,2},{2,0},{1,5},{5,9},... | collective-permute-start | bytes 1572872 | tf_op jit(solution)/shard_map/ppermute | solution.py:179
  37.9 0.2 collective-permute-start.6
  38.1 1.3 %collective-permute-start.1 = (bf16[128,2048]{1,0:T(8,128)(2,1)S(1)}, bf16[128,2048]{1,0:T(8,128)(2,1)S(1)}, u32[]{:S(2)}, u32[]{:S(2)}) collective-permute-start(bf16[128,2048]{1,0:T(8,128)(2,1)S(1)} %get-tuple-element.13), channel_id=1, source_target_pairs={{16,0},{17,1},{18,2},{19,3},{20,4},{21,5},{22,6},{23,7},{24,8},{25... | collective-permute-start | bytes 1572872 | tf_op jit(solution)/shard_map/ppermute | solution.py:163
  39.4 0.1 add_convert_fusion
  39.5 1.3 %collective-permute-start.3 = (bf16[8,8,2048]{2,1,0:T(8,128)(2,1)S(1)}, bf16[8,8,2048]{2,1,0:T(8,128)(2,1)S(1)}, u32[]{:S(2)}, u32[]{:S(2)}) collective-permute-start(bf16[8,8,2048]{2,1,0:T(8,128)(2,1)S(1)} %slice_bitcast_fusion.1), channel_id=1, source_target_pairs={{16,0},{17,1},{18,2},{19,3},{20,4},{21,5},{22,6},{23,7},{24,8},{25... | collective-permute-start | bytes 786440 | tf_op jit(solution)/shard_map/ppermute | solution.py:166
  40.8 12.2 %collective-permute-done.1 = bf16[128,2048]{1,0:T(8,128)(2,1)S(1)} collective-permute-done((bf16[128,2048]{1,0:T(8,128)(2,1)S(1)}, bf16[128,2048]{1,0:T(8,128)(2,1)S(1)}, u32[]{:S(2)}, u32[]{:S(2)}) %collective-permute-start.1) | collective-permute-done | bytes 524320 | tf_op jit(solution)/shard_map/ppermute | solution.py:163
  53.1 0.9 broadcast_select_fusion
  54.0 0.0 collective-permute-done.4
  54.0 1.4 %collective-permute-start.5 = (bf16[128,2048]{1,0:T(8,128)(2,1)S(1)}, bf16[128,2048]{1,0:T(8,128)(2,1)}, u32[]{:S(2)}, u32[]{:S(2)}) collective-permute-start(bf16[128,2048]{1,0:T(8,128)(2,1)S(1)} %collective-permute-done.4), channel_id=1, source_target_pairs={{0,4},{4,8},{8,12},{12,14},{14,10},{10,6},{6,2},{2,0},{1,5},{5,9},... | collective-permute-start | bytes 1572872 | tf_op jit(solution)/shard_map/ppermute | solution.py:179
  55.4 0.2 collective-permute-start.7
  55.5 3.2 %collective-permute-done.3 = bf16[8,8,2048]{2,1,0:T(8,128)(2,1)S(1)} collective-permute-done((bf16[8,8,2048]{2,1,0:T(8,128)(2,1)S(1)}, bf16[8,8,2048]{2,1,0:T(8,128)(2,1)S(1)}, u32[]{:S(2)}, u32[]{:S(2)}) %collective-permute-start.3) | collective-permute-done | bytes 262176 | tf_op jit(solution)/shard_map/ppermute | solution.py:166
  58.7 0.9 pad_maximum_fusion
  59.7 5.6 %collective-permute-done.5 = bf16[128,2048]{1,0:T(8,128)(2,1)} collective-permute-done((bf16[128,2048]{1,0:T(8,128)(2,1)S(1)}, bf16[128,2048]{1,0:T(8,128)(2,1)}, u32[]{:S(2)}, u32[]{:S(2)}) %collective-permute-start.5) | collective-permute-done | bytes 524320 | tf_op jit(solution)/shard_map/ppermute | solution.py:179
  65.3 1.0 collective-permute-done.7
  66.3 4.7 %all-to-all-start = ((bf16[8,192,256]{2,1,0:T(8,128)(2,1)}), bf16[8,192,256]{2,1,0:T(8,128)(2,1)S(1)}, u32[]{:S(2)}, u32[]{:S(2)}) async-start(bf16[8,192,256]{2,1,0:T(8,128)(2,1)} %pad_maximum_fusion), calls=%async_computation | async-start | bytes 1572864 | tf_op jit(solution)/shard_map/all_to_all | solution.py:192
  71.0 1.2 collective-permute-start.8
  72.2 0.3 collective-permute-start.9
  72.5 25.0 %collective-permute-done.8 = bf16[128,2048]{1,0:T(8,128)(2,1)S(1)} collective-permute-done((bf16[128,2048]{1,0:T(8,128)(2,1)}, bf16[128,2048]{1,0:T(8,128)(2,1)S(1)}, u32[]{:S(2)}, u32[]{:S(2)}) %collective-permute-start.8) | collective-permute-done | bytes 524320 | tf_op jit(solution)/shard_map/ppermute | solution.py:179
  97.5 0.7 slice.43
  98.2 2.1 %collective-permute-start.10 = (bf16[64,2048]{1,0:T(8,128)(2,1)}, bf16[64,2048]{1,0:T(8,128)(2,1)}, u32[]{:S(2)}, u32[]{:S(2)}) collective-permute-start(bf16[64,2048]{1,0:T(8,128)(2,1)} %slice.43), channel_id=1, source_target_pairs={{0,4},{4,8},{8,12},{12,14},{14,10},{10,6},{6,2},{2,0},{1,5},{5,9},... | collective-permute-start | bytes 786440 | tf_op jit(solution)/shard_map/ppermute | solution.py:184
  100.3 0.7 slice.44
  101.1 0.5 fusion.17
  101.5 0.5 fusion.15
  102.0 0.5 fusion.4
  102.5 1.5 %fusion.12 = f32[256,2048]{1,0:T(8,128)S(1)} fusion(bf16[128,2048]{1,0:T(8,128)(2,1)} %collective-permute-done.7, bf16[8,128,256]{2,1,0:T(8,128)(2,1)S(1)} %slice.42, s32[]{:T(128)S(6)} %select_n.166), kind=kOutput, calls=%fused_computation.27 | convolution fusion | flops 134217728 | bytes 2686980 | tf_op jit(solution)/shard_map/dot_general | solution.py:16
  104.0 0.5 fusion.9
  104.5 1.4 %fusion.28 = f32[256,2048]{1,0:T(8,128)S(1)} fusion(bf16[64,2048]{1,0:T(8,128)(2,1)} %collective-permute-done.10, bf16[8,128,256]{2,1,0:T(8,128)(2,1)S(1)} %slice.42, s32[]{:T(128)S(6)} %select_n.172), kind=kOutput, calls=%fused_computation.45 | convolution fusion | flops 67108864 | bytes 2392068 | tf_op jit(solution)/shard_map/dot_general | solution.py:16
  105.9 1.0 collective-permute-done.11
  106.9 1.4 %fusion.27 = f32[256,2048]{1,0:T(8,128)S(1)} fusion(bf16[64,2048]{1,0:T(8,128)(2,1)} %collective-permute-done.11, bf16[8,128,256]{2,1,0:T(8,128)(2,1)S(1)} %slice.42, s32[]{:T(128)S(6)} %select_n.172, s32[]{:T(128)S(6)} %add.190), kind=kOutput, calls=%fused_computation.43 | convolution fusion | flops 67108864 | bytes 2392072 | tf_op jit(solution)/shard_map/dot_general | solution.py:16
  108.3 1.5 %fusion.3 = f32[256,2048]{1,0:T(8,128)S(1)} fusion(f32[256,2048]{1,0:T(8,128)S(1)} %fusion.12, f32[256,2048]{1,0:T(8,128)S(1)} %fusion.4, bf16[128,2048]{1,0:T(8,128)(2,1)} %collective-permute-done.5, bf16[8,128,256]{2,1,0:T(8,128)(2,1)S(1)} %slice.42, s32[]{:T(128)S(6)} %select_n.164), kind=kOutput, calls=%fused_computation.5 | convolution fusion | flops 135266304 | bytes 6881284 | tf_op jit(solution)/shard_map/dot_general | solution.py:16
  109.8 0.6 fusion.2
  110.4 1.1 dynamic-slice_bitcast_fusion
  111.4 3.7 %collective-permute-start.12 = (f32[128,2048]{1,0:T(8,128)}, f32[128,2048]{1,0:T(8,128)}, u32[]{:S(2)}, u32[]{:S(2)}) collective-permute-start(f32[128,2048]{1,0:T(8,128)} %dynamic-slice_bitcast_fusion), channel_id=1, source_target_pairs={{0,1},{1,0},{2,3},{3,2},{4,5},{5,4},{6,7},{7,6},{8,9},{9,8},{10,11... | collective-permute-start | bytes 3145736 | tf_op jit(solution)/shard_map/ppermute | solution.py:20
  115.2 0.6 broadcast_multiply_fusion
  115.8 2.0 %collective-permute-done.12 = f32[128,2048]{1,0:T(8,128)} collective-permute-done((f32[128,2048]{1,0:T(8,128)}, f32[128,2048]{1,0:T(8,128)}, u32[]{:S(2)}, u32[]{:S(2)}) %collective-permute-start.12) | collective-permute-done | bytes 1048608 | tf_op jit(solution)/shard_map/ppermute | solution.py:20
  117.8 2.3 %fusion.6 = f32[1,128,2048]{2,1,0:T(8,128)} fusion(f32[128,2048]{1,0:T(8,128)} %collective-permute-done.12, f32[2,128,2048]{2,1,0:T(8,128)S(1)} %bitcast.81, s32[]{:T(128)S(6)} %select_n.173), kind=kLoop, calls=%fused_computation.10 | loop fusion | flops 524288 | bytes 3145732 | tf_op jit(solution)/shard_map/broadcast_in_dim | solution.py:205
  (19 shorter events, 0.2 us)
Async XLA Ops:
  1.4 3.4 %copy-start = (bf16[1,2048,2048]{2,1,0:T(8,128)(2,1)S(1)}, bf16[1,2048,2048]{2,1,0:T(8,128)(2,1)}, u32[]{:S(2)}) copy-start(bf16[1,2048,2048]{2,1,0:T(8,128)(2,1)} %param.5) | copy-start | bytes 25165828
  4.8 1.0 copy-start.2
  5.8 1.2 %copy-start.4 = (bf16[256,2048]{1,0:T(8,128)(2,1)S(1)}, bf16[256,2048]{1,0:T(8,128)(2,1)}, u32[]{:S(2)}) copy-start(bf16[256,2048]{1,0:T(8,128)(2,1)} %table.1) | copy-start | bytes 3145732
  7.0 6.3 %copy-start.5 = (s32[128]{0:T(128)S(1)}, s32[128]{0:T(128)}, u32[]{:S(2)}) copy-start(s32[128]{0:T(128)} %param.7) | copy-start | bytes 1540
  7.0 16.8 %copy-start.3 = (bf16[1,128,2048]{2,1,0:T(8,128)(2,1)S(1)}, bf16[1,128,2048]{2,1,0:T(8,128)(2,1)}, u32[]{:S(2)}) copy-start(bf16[1,128,2048]{2,1,0:T(8,128)(2,1)} %param.4) | copy-start | bytes 1572868
  10.1 13.7 %collective-permute-start = (bf16[2,128,1024]{2,1,0:T(8,128)(2,1)S(1)}, bf16[2,128,1024]{2,1,0:T(8,128)(2,1)S(1)}, u32[]{:S(2)}, u32[]{:S(2)}) collective-permute-start(bf16[2,128,1024]{2,1,0:T(8,128)(2,1)S(1)} %get-tuple-element.11), channel_id=1, source_target_pairs={{0,16},{1,17},{2,18},{3,19},{4,20},{5,21},{6,22},{7,23},{8,24},{9,... | collective-permute-start | bytes 1572872 | tf_op jit(solution)/shard_map/ppermute | solution.py:159
  23.8 3.4 %copy-start.1 = (bf16[1,2048,2048]{2,1,0:T(8,128)(2,1)S(1)}, bf16[1,2048,2048]{2,1,0:T(8,128)(2,1)}, u32[]{:S(2)}) copy-start(bf16[1,2048,2048]{2,1,0:T(8,128)(2,1)} %param.5) | copy-start | bytes 25165828
  35.0 4.4 %collective-permute-start.2 = (f32[128,2048]{1,0:T(8,128)S(1)}, f32[128,2048]{1,0:T(8,128)S(1)}, u32[]{:S(2)}, u32[]{:S(2)}) collective-permute-start(f32[128,2048]{1,0:T(8,128)S(1)} %get-tuple-element.16), channel_id=1, source_target_pairs={{0,1},{1,0},{2,3},{3,2},{4,5},{5,4},{6,7},{7,6},{8,9},{9,8},{10,11... | collective-permute-start | bytes 3145736 | tf_op jit(solution)/shard_map/ppermute | solution.py:20
  36.6 17.4 %collective-permute-start.4 = (bf16[128,2048]{1,0:T(8,128)(2,1)S(1)}, bf16[128,2048]{1,0:T(8,128)(2,1)S(1)}, u32[]{:S(2)}, u32[]{:S(2)}) collective-permute-start(bf16[128,2048]{1,0:T(8,128)(2,1)S(1)} %get-tuple-element.17), channel_id=1, source_target_pairs={{0,4},{4,8},{8,12},{12,14},{14,10},{10,6},{6,2},{2,0},{1,5},{5,9},... | collective-permute-start | bytes 1572872 | tf_op jit(solution)/shard_map/ppermute | solution.py:179
  37.9 17.4 %collective-permute-start.6 = (bf16[128,2048]{1,0:T(8,128)(2,1)S(1)}, bf16[128,2048]{1,0:T(8,128)(2,1)S(1)}, u32[]{:S(2)}, u32[]{:S(2)}) collective-permute-start(bf16[128,2048]{1,0:T(8,128)(2,1)S(1)} %get-tuple-element.17), channel_id=1, source_target_pairs={{4,0},{8,4},{12,8},{14,12},{10,14},{6,10},{2,6},{0,2},{5,1},{9,5},... | collective-permute-start | bytes 1572872 | tf_op jit(solution)/shard_map/ppermute | solution.py:180
  38.1 15.0 %collective-permute-start.1 = (bf16[128,2048]{1,0:T(8,128)(2,1)S(1)}, bf16[128,2048]{1,0:T(8,128)(2,1)S(1)}, u32[]{:S(2)}, u32[]{:S(2)}) collective-permute-start(bf16[128,2048]{1,0:T(8,128)(2,1)S(1)} %get-tuple-element.13), channel_id=1, source_target_pairs={{16,0},{17,1},{18,2},{19,3},{20,4},{21,5},{22,6},{23,7},{24,8},{25... | collective-permute-start | bytes 1572872 | tf_op jit(solution)/shard_map/ppermute | solution.py:163
  39.5 19.2 %collective-permute-start.3 = (bf16[8,8,2048]{2,1,0:T(8,128)(2,1)S(1)}, bf16[8,8,2048]{2,1,0:T(8,128)(2,1)S(1)}, u32[]{:S(2)}, u32[]{:S(2)}) collective-permute-start(bf16[8,8,2048]{2,1,0:T(8,128)(2,1)S(1)} %slice_bitcast_fusion.1), channel_id=1, source_target_pairs={{16,0},{17,1},{18,2},{19,3},{20,4},{21,5},{22,6},{23,7},{24,8},{25... | collective-permute-start | bytes 786440 | tf_op jit(solution)/shard_map/ppermute | solution.py:166
  54.0 11.3 %collective-permute-start.5 = (bf16[128,2048]{1,0:T(8,128)(2,1)S(1)}, bf16[128,2048]{1,0:T(8,128)(2,1)}, u32[]{:S(2)}, u32[]{:S(2)}) collective-permute-start(bf16[128,2048]{1,0:T(8,128)(2,1)S(1)} %collective-permute-done.4), channel_id=1, source_target_pairs={{0,4},{4,8},{8,12},{12,14},{14,10},{10,6},{6,2},{2,0},{1,5},{5,9},... | collective-permute-start | bytes 1572872 | tf_op jit(solution)/shard_map/ppermute | solution.py:179
  55.4 10.9 %collective-permute-start.7 = (bf16[128,2048]{1,0:T(8,128)(2,1)S(1)}, bf16[128,2048]{1,0:T(8,128)(2,1)}, u32[]{:S(2)}, u32[]{:S(2)}) collective-permute-start(bf16[128,2048]{1,0:T(8,128)(2,1)S(1)} %collective-permute-done.6), channel_id=1, source_target_pairs={{4,0},{8,4},{12,8},{14,12},{10,14},{6,10},{2,6},{0,2},{5,1},{9,5},... | collective-permute-start | bytes 1572872 | tf_op jit(solution)/shard_map/ppermute | solution.py:180
  66.3 34.7 %all-to-all-start = ((bf16[8,192,256]{2,1,0:T(8,128)(2,1)}), bf16[8,192,256]{2,1,0:T(8,128)(2,1)S(1)}, u32[]{:S(2)}, u32[]{:S(2)}) async-start(bf16[8,192,256]{2,1,0:T(8,128)(2,1)} %pad_maximum_fusion), calls=%async_computation | async-start | bytes 1572864 | tf_op jit(solution)/shard_map/all_to_all | solution.py:192
  71.0 26.5 %collective-permute-start.8 = (bf16[128,2048]{1,0:T(8,128)(2,1)}, bf16[128,2048]{1,0:T(8,128)(2,1)S(1)}, u32[]{:S(2)}, u32[]{:S(2)}) collective-permute-start(bf16[128,2048]{1,0:T(8,128)(2,1)} %collective-permute-done.5), channel_id=1, source_target_pairs={{0,4},{4,8},{8,12},{12,14},{14,10},{10,6},{6,2},{2,0},{1,5},{5,9},... | collective-permute-start | bytes 1572872 | tf_op jit(solution)/shard_map/ppermute | solution.py:179
  72.2 28.1 %collective-permute-start.9 = (bf16[128,2048]{1,0:T(8,128)(2,1)}, bf16[128,2048]{1,0:T(8,128)(2,1)S(1)}, u32[]{:S(2)}, u32[]{:S(2)}) collective-permute-start(bf16[128,2048]{1,0:T(8,128)(2,1)} %collective-permute-done.7), channel_id=1, source_target_pairs={{4,0},{8,4},{12,8},{14,12},{10,14},{6,10},{2,6},{0,2},{5,1},{9,5},... | collective-permute-start | bytes 1572872 | tf_op jit(solution)/shard_map/ppermute | solution.py:180
  98.2 6.2 %collective-permute-start.10 = (bf16[64,2048]{1,0:T(8,128)(2,1)}, bf16[64,2048]{1,0:T(8,128)(2,1)}, u32[]{:S(2)}, u32[]{:S(2)}) collective-permute-start(bf16[64,2048]{1,0:T(8,128)(2,1)} %slice.43), channel_id=1, source_target_pairs={{0,4},{4,8},{8,12},{12,14},{14,10},{10,6},{6,2},{2,0},{1,5},{5,9},... | collective-permute-start | bytes 786440 | tf_op jit(solution)/shard_map/ppermute | solution.py:184
  101.0 5.8 %collective-permute-start.11 = (bf16[64,2048]{1,0:T(8,128)(2,1)}, bf16[64,2048]{1,0:T(8,128)(2,1)}, u32[]{:S(2)}, u32[]{:S(2)}) collective-permute-start(bf16[64,2048]{1,0:T(8,128)(2,1)} %slice.44), channel_id=1, source_target_pairs={{4,0},{8,4},{12,8},{14,12},{10,14},{6,10},{2,6},{0,2},{5,1},{9,5},... | collective-permute-start | bytes 786440 | tf_op jit(solution)/shard_map/ppermute | solution.py:185
  111.4 6.4 %collective-permute-start.12 = (f32[128,2048]{1,0:T(8,128)}, f32[128,2048]{1,0:T(8,128)}, u32[]{:S(2)}, u32[]{:S(2)}) collective-permute-start(f32[128,2048]{1,0:T(8,128)} %dynamic-slice_bitcast_fusion), channel_id=1, source_target_pairs={{0,1},{1,0},{2,3},{3,2},{4,5},{5,4},{6,7},{7,6},{8,9},{9,8},{10,11... | collective-permute-start | bytes 3145736 | tf_op jit(solution)/shard_map/ppermute | solution.py:20
where the time goes:
time: 121 us; the launch traced here: 120 us
  waiting for transfers between devices  60.4 us (50%)
  starting transfers between devices  22.3 us (18%)
  local copies, waits for them, and re-layouts  11.6 us (10%)
  Pallas kernels  10.9 us (9%)
  matrix products  8.27 us (7%)
  other arithmetic  5.8 us (5%)
    ppermute x3, waiting for transfers between devices, local(): fwd = lax.ppermute(fwd, 'chip', up)  30.6 us
    ppermute x1, waiting for transfers between devices, local(): query_back = lax.ppermute(grad_query, 'hop', [(1, 0)])  12.2 us
    ppermute x1, waiting for transfers between devices, local(): query = lax.ppermute(own_query, 'hop', [(0, 1)])  10.4 us
    unnamed x12, local copies, waits for them, and re-layouts  9.03 us
    dot_general x9, matrix products, dot(): lax.dot_general(a, b, (((ca,), (cb,)), ((), ())), preferred_element_type=...  8.27 us
    pallas_call x1, Pallas kernels, trail(): pl.pallas_call(trail_body, out_shape=(jax.ShapeDtypeStruct((rows_dev, hid...  7.81 us
    ppermute x2, starting transfers between devices, swap_core(): return lax.ppermute(block, 'core', [(0, 1), (1, 0)])  5.34 us
    all_to_all x1, starting transfers between devices, local(): received = lax.all_to_all(sent, 'chip', 0, 0, tiled=True)  4.71 us
  transfers between devices with their start and end apart: 14, of which 8 were waited for; matrix products, arithmetic and copies ran while one was open for 8% of the time, Pallas kernels for 0%

commit v1 on v0

--- a/solution.py
+++ b/solution.py
@@ -28,36 +28,28 @@
     return pl.ds(pl.multiple_of(base + step * TILE, TILE), TILE)
 
 
-def lead_body(rows, weight, onehot, table, query, rel):
+def lead_body(rows, weight, query):
     half = weight.shape[0] // 2
-    steps = half // TILE
-    for step in range(steps):
+    for step in range(half // TILE):
         span = pl.ds(step * TILE, TILE)
-        r_re = dot(onehot[...], table[:, at(step)], 1, 0)
-        r_im = dot(onehot[...], table[:, at(step, half)], 1, 0)
-        q_re = dot(rows[...], weight[at(step)], 1, 1).astype(BF16)
-        q_im = dot(rows[...], weight[at(step, half)], 1, 1).astype(BF16)
-        query[0, :, span], query[1, :, span] = q_re, q_im
-        rel[0, :, span], rel[1, :, span] = r_re.astype(BF16), r_im.astype(BF16)
-
-
-def lead(rows, weight, onehot, table):
+        query[0, :, span] = dot(rows[...], weight[at(step)], 1, 1).astype(BF16)
+        query[1, :, span] = dot(rows[...], weight[at(step, half)], 1, 1).astype(BF16)
+
+
+def lead(rows, weight):
     rows_dev, hidden = rows.shape
     width = weight.shape[0]
-    half = width // 2
-    count_rel = table.shape[0]
     vmem = pl.BlockSpec(memory_space=pltpu.VMEM)
-    pair = jax.ShapeDtypeStruct((2, rows_dev, half), BF16)
     return pl.pallas_call(
         lead_body,
-        out_shape=(pair, pair),
-        in_specs=[vmem] * 4,
-        out_specs=(vmem,) * 2,
+        out_shape=jax.ShapeDtypeStruct((2, rows_dev, width // 2), BF16),
+        in_specs=[vmem] * 2,
+        out_specs=vmem,
         compiler_params=pltpu.CompilerParams(vmem_limit_bytes=GRANT),
         cost_estimate=pl.CostEstimate(
-            flops=2 * rows_dev * width * (hidden + count_rel), bytes_accessed=2 * width * hidden, transcendentals=0
+            flops=2 * rows_dev * width * hidden, bytes_accessed=2 * width * hidden, transcendentals=0
         ),
-    )(rows, weight, onehot, table)
+    )(rows, weight)
 
 
 def trail_body(first, query, rows, weight, rel, onehot, right, query_grad, give, keep, mixed, hidden):
@@ -155,8 +147,10 @@
     relation = ((hop * chips + dest) * 2 + which_core) * owned + number % owned
     onehot_t = (relation[:, None] == relation_ids[None, :]).astype(BF16)
 
-    own_query, rel = lead(rows, weight, onehot, relation_table)
+    own_query = lead(rows, weight)
     query = lax.ppermute(own_query, "hop", [(0, 1)])
+    rel = dot(onehot, relation_table, 1, 0).astype(BF16)
+    rel = rel.reshape(rows_dev, 2, half).transpose(1, 0, 2)
     right, grad_query, rel_give, rel_keep, mixed = trail(
         first.astype(jnp.int32).reshape(1), query, rows, weight, rel, onehot_t
     )
@@ -179,10 +173,6 @@
         fwd = lax.ppermute(fwd, "chip", up)
         bwd = lax.ppermute(bwd, "chip", down)
         blocks += [(fwd, chips - s, 0), (bwd, s, 0)]
-    if chips % 2 == 0:
-        mid = rows_dev // 2
-        blocks.append((lax.ppermute(fwd[:mid], "chip", up), chips // 2, 0))
-        blocks.append((lax.ppermute(bwd[mid:], "chip", down), chips // 2, mid))
 
     rel_own = jnp.where(first, rel_back, rel_chip[:, 1]).reshape(chips, owned, chips, cols)
     rel_own = rel_own.transpose(0, 2, 1, 3).reshape(chips, owned * chips, cols)
@@ -194,10 +184,19 @@
     rel_sum = jnp.sum(rel_rows.astype(F32), axis=0) * jnp.sqrt(F32(count_rel) / F32(total_rows))
     relation_grad = rel_sum.reshape(chips, owned, cols).transpose(1, 0, 2).reshape(owned, width)
 
-    partial = jnp.zeros((cols, width), F32)
-    for block, step, base in blocks:
-        left = lax.dynamic_index_in_dim(left_cols, chip_at(place + step), 0, keepdims=False)
-        partial = partial + dot(left[base:base + block.shape[0]], block, 0, 0)
+    def add(partial, blocks):
+        for block, step, base in blocks:
+            left = lax.dynamic_index_in_dim(left_cols, chip_at(place + step), 0, keepdims=False)
+            partial = partial + dot(left[base:base + block.shape[0]], block, 0, 0)
+        return partial
+
+    partial = add(jnp.zeros((cols, width), F32), blocks[:5])
+    if chips % 2 == 0:
+        mid = rows_dev // 2
+        top, bottom, partial = lax.optimization_barrier((fwd[:mid], bwd[mid:], partial))
+        blocks.append((lax.ppermute(top, "chip", up), chips // 2, 0))
+        blocks.append((lax.ppermute(bottom, "chip", down), chips // 2, mid))
+    partial = add(partial, blocks[5:])
     partial = partial.reshape(2, cols // 2, width)
     keep = lax.dynamic_index_in_dim(partial, core, 0, keepdims=False)
     give = lax.dynamic_index_in_dim(partial, 1 - core, 0, keepdims=False)

time: 121 us -> 124 us (1.025)
  local copies, waits for them, and re-layouts: 11.6 us -> 13.1 us
    ppermute x1, waiting for transfers between devices: 10.4 us -> 7.77 us  [local(): query = lax.ppermute(own_query, 'hop', [(0, 1)])]
    ppermute x2, waiting for transfers between devices: 1 us -> 3.55 us  [the longest x1 1.81 us: local(): blocks.append((lax.ppermute(top, 'chip', up), chips // 2, 0))]
    reshape x0 -> x1, local copies, waits for them, and re-layouts: none -> 1.24 us  [local(): rel = rel.reshape(rows_dev, 2, half).transpose(1, 0, 2)]
    dot_general x9 -> x10, matrix products: 8.27 us -> 9.26 us  [dot(): lax.dot_general(a, b, (((ca,), (cb,)), ((), ())), preferred_element_type=...]
    unnamed x12 -> x26, local copies, waits for them, and re-layouts: 9.03 us -> 8.74 us
  transfers between devices with their start and end apart: 14 -> 14, of which waited for: 8 -> 10; matrix products, arithmetic and copies ran while one was open for 8% -> 8% of each run, Pallas kernels for 0% -> 0%
where the time goes in v1:
time: 124 us; the launch traced here: 122 us
  waiting for transfers between devices  59.2 us (48%)
  starting transfers between devices  22.8 us (18%)
  local copies, waits for them, and re-layouts  13.1 us (11%)
  Pallas kernels  10.7 us (9%)
  matrix products  9.26 us (7%)
  other arithmetic  6.09 us (5%)
    ppermute x3, waiting for transfers between devices, local(): fwd = lax.ppermute(fwd, 'chip', up)  31.1 us
    ppermute x1, waiting for transfers between devices, local(): query_back = lax.ppermute(grad_query, 'hop', [(1, 0)])  12.2 us
    dot_general x10, matrix products, dot(): lax.dot_general(a, b, (((ca,), (cb,)), ((), ())), preferred_element_type=...  9.26 us
    unnamed x26, local copies, waits for them, and re-layouts  8.74 us
    pallas_call x1, Pallas kernels, trail(): pl.pallas_call(trail_body, out_shape=(jax.ShapeDtypeStruct((rows_dev, hid...  7.81 us
    ppermute x1, waiting for transfers between devices, local(): query = lax.ppermute(own_query, 'hop', [(0, 1)])  7.77 us
    all_to_all x1, starting transfers between devices, local(): received = lax.all_to_all(sent, 'chip', 0, 0, tiled=True)  5.51 us
    ppermute x2, starting transfers between devices, swap_core(): return lax.ppermute(block, 'core', [(0, 1), (1, 0)])  4.96 us
  transfers between devices with their start and end apart: 14, of which 10 were waited for; matrix products, arithmetic and copies ran while one was open for 8% of the time, Pallas kernels for 0%

profile of v1, /device:TPU:9, one launch (start us, length us, event | category | flops | bytes accessed | tf_op | source)
XLA Modules:
  0.0 122.0 jit_solution(345111147057195083)
XLA Ops:
  0.7 3.5 %copy-done.1 = bf16[1,2048,2048]{2,1,0:T(8,128)(2,1)S(1)} copy-done((bf16[1,2048,2048]{2,1,0:T(8,128)(2,1)S(1)}, bf16[1,2048,2048]{2,1,0:T(8,128)(2,1)}, u32[]{:S(2)}) %copy-start.1) | copy-done | bytes 8388632
  4.1 1.0 copy-done.3
  5.2 2.9 %shard_map.67 = bf16[2,128,1024]{2,1,0:T(8,128)(2,1)S(1)} custom-call(bf16[128,2048]{1,0:T(8,128)(2,1)S(1)} %bitcast.83, bf16[2048,2048]{1,0:T(8,128)(2,1)S(1)} %bitcast.81), custom_call_target="tpu_custom_call" | custom-call | flops 1073741824 | bytes 8388608 | tf_op jit(solution)/shard_map/pallas_call | solution.py:43
  8.1 3.3 %collective-permute-start = (bf16[2,128,1024]{2,1,0:T(8,128)(2,1)S(1)}, bf16[2,128,1024]{2,1,0:T(8,128)(2,1)S(1)}, u32[]{:S(2)}, u32[]{:S(2)}) collective-permute-start(bf16[2,128,1024]{2,1,0:T(8,128)(2,1)S(1)} %shard_map.67), channel_id=1, source_target_pairs={{0,16},{1,17},{2,18},{3,19},{4,20},{5,21},{6,22},{7,23},{8,24},{9,... | collective-permute-start | bytes 1572872 | tf_op jit(solution)/shard_map/ppermute | solution.py:151
  11.4 0.3 convolution_convert_fusion
  11.7 1.0 copy.9
  12.7 1.2 %copy.10 = bf16[128,2,1024]{2,0,1:T(8,128)(2,1)S(1)} copy(bf16[128,2,1024]{0,2,1:T(8,128)(2,1)} %bitcast.91) | data formatting | bytes 1048576 | tf_op jit(solution)/shard_map/reshape | solution.py:153
  14.1 7.8 %collective-permute-done.query = bf16[2,128,1024]{2,1,0:T(8,128)(2,1)S(1)} collective-permute-done((bf16[2,128,1024]{2,1,0:T(8,128)(2,1)S(1)}, bf16[2,128,1024]{2,1,0:T(8,128)(2,1)S(1)}, u32[]{:S(2)}, u32[]{:S(2)}) %collective-permute-start) | collective-permute-done | bytes 524320 | tf_op jit(solution)/shard_map/ppermute | solution.py:151
  21.9 3.4 %copy-done.2 = bf16[1,2048,2048]{2,1,0:T(8,128)(2,1)S(1)} copy-done((bf16[1,2048,2048]{2,1,0:T(8,128)(2,1)S(1)}, bf16[1,2048,2048]{2,1,0:T(8,128)(2,1)}, u32[]{:S(2)}) %copy-start.2) | copy-done | bytes 8388632
  25.3 7.8 %shard_map.68 = (bf16[128,2048]{1,0:T(8,128)(2,1)S(1)}, bf16[128,2048]{1,0:T(8,128)(2,1)S(1)}, f32[128,2048]{1,0:T(8,128)S(1)}, f32[128,2048]{1,0:T(8,128)S(1)}, bf16[128,2048]{1,0:T(8,128)(2,1)S(1)}) custom-call(s32[1]{0:T(128)} %bitcast.first, bf16[2,128,1024]{2,1,0:T(8,128)(2,1)S(1)} %collective-permute-done.query, bf16[128,2048]{1,0:T(8,128)(2,1)S(1)} %bitcast.84, ...), custom_call_target="tpu_custom_call" | custom-call | flops 2415919104 | bytes 16777216 | tf_op jit(solution)/shard_map/pallas_call | solution.py:105
  33.1 1.6 %collective-permute-start.8 = (f32[128,2048]{1,0:T(8,128)S(1)}, f32[128,2048]{1,0:T(8,128)S(1)}, u32[]{:S(2)}, u32[]{:S(2)}) collective-permute-start(f32[128,2048]{1,0:T(8,128)S(1)} %get-tuple-element.16), channel_id=1, source_target_pairs={{0,1},{1,0},{2,3},{3,2},{4,5},{5,4},{6,7},{7,6},{8,9},{9,8},{10,11... | collective-permute-start | bytes 3145736 | tf_op jit(solution)/shard_map/ppermute | solution.py:20
  34.7 1.3 %collective-permute-start.1 = (bf16[128,2048]{1,0:T(8,128)(2,1)S(1)}, bf16[128,2048]{1,0:T(8,128)(2,1)S(1)}, u32[]{:S(2)}, u32[]{:S(2)}) collective-permute-start(bf16[128,2048]{1,0:T(8,128)(2,1)S(1)} %get-tuple-element.12), channel_id=1, source_target_pairs={{0,4},{4,8},{8,12},{12,14},{14,10},{10,6},{6,2},{2,0},{1,5},{5,9},... | collective-permute-start | bytes 1572872 | tf_op jit(solution)/shard_map/ppermute | solution.py:173
  36.0 0.2 collective-permute-start.4
  36.2 1.3 %collective-permute-start.7 = (bf16[128,2048]{1,0:T(8,128)(2,1)S(1)}, bf16[128,2048]{1,0:T(8,128)(2,1)S(1)}, u32[]{:S(2)}, u32[]{:S(2)}) collective-permute-start(bf16[128,2048]{1,0:T(8,128)(2,1)S(1)} %get-tuple-element.13), channel_id=1, source_target_pairs={{16,0},{17,1},{18,2},{19,3},{20,4},{21,5},{22,6},{23,7},{24,8},{25... | collective-permute-start | bytes 1572872 | tf_op jit(solution)/shard_map/ppermute | solution.py:157
  37.6 1.3 %collective-permute-start.9 = (bf16[8,8,2048]{2,1,0:T(8,128)(2,1)S(1)}, bf16[8,8,2048]{2,1,0:T(8,128)(2,1)S(1)}, u32[]{:S(2)}, u32[]{:S(2)}) collective-permute-start(bf16[8,8,2048]{2,1,0:T(8,128)(2,1)S(1)} %slice_bitcast_fusion.1), channel_id=1, source_target_pairs={{16,0},{17,1},{18,2},{19,3},{20,4},{21,5},{22,6},{23,7},{24,8},{25... | collective-permute-start | bytes 786440 | tf_op jit(solution)/shard_map/ppermute | solution.py:160
  38.9 12.2 %collective-permute-done.7 = bf16[128,2048]{1,0:T(8,128)(2,1)S(1)} collective-permute-done((bf16[128,2048]{1,0:T(8,128)(2,1)S(1)}, bf16[128,2048]{1,0:T(8,128)(2,1)S(1)}, u32[]{:S(2)}, u32[]{:S(2)}) %collective-permute-start.7) | collective-permute-done | bytes 524320 | tf_op jit(solution)/shard_map/ppermute | solution.py:157
  51.2 0.9 broadcast_select_fusion
  52.2 1.3 %collective-permute-start.2 = (bf16[128,2048]{1,0:T(8,128)(2,1)S(1)}, bf16[128,2048]{1,0:T(8,128)(2,1)S(1)}, u32[]{:S(2)}, u32[]{:S(2)}) collective-permute-start(bf16[128,2048]{1,0:T(8,128)(2,1)S(1)} %collective-permute-done.1), channel_id=1, source_target_pairs={{0,4},{4,8},{8,12},{12,14},{14,10},{10,6},{6,2},{2,0},{1,5},{5,9},... | collective-permute-start | bytes 1572872 | tf_op jit(solution)/shard_map/ppermute | solution.py:173
  53.5 0.2 collective-permute-start.5
  53.7 3.1 %collective-permute-done.9 = bf16[8,8,2048]{2,1,0:T(8,128)(2,1)S(1)} collective-permute-done((bf16[8,8,2048]{2,1,0:T(8,128)(2,1)S(1)}, bf16[8,8,2048]{2,1,0:T(8,128)(2,1)S(1)}, u32[]{:S(2)}, u32[]{:S(2)}) %collective-permute-start.9) | collective-permute-done | bytes 262176 | tf_op jit(solution)/shard_map/ppermute | solution.py:160
  56.8 0.9 pad_maximum_fusion
  57.8 5.7 %collective-permute-done.2 = bf16[128,2048]{1,0:T(8,128)(2,1)S(1)} collective-permute-done((bf16[128,2048]{1,0:T(8,128)(2,1)S(1)}, bf16[128,2048]{1,0:T(8,128)(2,1)S(1)}, u32[]{:S(2)}, u32[]{:S(2)}) %collective-permute-start.2) | collective-permute-done | bytes 524320 | tf_op jit(solution)/shard_map/ppermute | solution.py:173
  63.4 0.8 copy-done.10
  64.2 0.2 collective-permute-done.5
  64.4 5.5 %all-to-all-start = ((bf16[8,192,256]{2,1,0:T(8,128)(2,1)}), bf16[8,192,256]{2,1,0:T(8,128)(2,1)S(1)}, u32[]{:S(2)}, u32[]{:S(2)}) async-start(bf16[8,192,256]{2,1,0:T(8,128)(2,1)} %pad_maximum_fusion), calls=%async_computation | async-start | bytes 1572864 | tf_op jit(solution)/shard_map/all_to_all | solution.py:182
  69.9 1.2 collective-permute-start.3
  71.1 0.3 collective-permute-start.6
  71.4 25.4 %collective-permute-done.3 = bf16[128,2048]{1,0:T(8,128)(2,1)} collective-permute-done((bf16[128,2048]{1,0:T(8,128)(2,1)}, bf16[128,2048]{1,0:T(8,128)(2,1)}, u32[]{:S(2)}, u32[]{:S(2)}) %collective-permute-start.3) | collective-permute-done | bytes 524320 | tf_op jit(solution)/shard_map/ppermute | solution.py:173
  96.8 1.0 slice.40
  97.8 0.3 collective-permute-done.6
  98.1 1.9 %fusion.16 = f32[256,2048]{1,0:T(8,128)S(1)} fusion(bf16[128,2048]{1,0:T(8,128)(2,1)} %copy-done.8, bf16[8,128,256]{2,1,0:T(8,128)(2,1)S(1)} %slice.44, s32[]{:T(128)S(6)} %select_n.160), kind=kOutput, calls=%fused_computation.30 | convolution fusion | flops 134217728 | bytes 2686980 | tf_op jit(solution)/shard_map/dot_general | solution.py:16
  100.1 1.5 %fusion.14 = f32[256,2048]{1,0:T(8,128)S(1)} fusion(bf16[128,2048]{1,0:T(8,128)(2,1)} %copy-done.9, bf16[8,128,256]{2,1,0:T(8,128)(2,1)S(1)} %slice.44, s32[]{:T(128)S(6)} %select_n.162), kind=kOutput, calls=%fused_computation.28 | convolution fusion | flops 134217728 | bytes 2686980 | tf_op jit(solution)/shard_map/dot_general | solution.py:16
  101.6 0.5 fusion.1
  102.1 1.6 %fusion.11 = f32[256,2048]{1,0:T(8,128)S(1)} fusion(bf16[128,2048]{1,0:T(8,128)(2,1)} %collective-permute-done.5, bf16[8,128,256]{2,1,0:T(8,128)(2,1)S(1)} %slice.44, s32[]{:T(128)S(6)} %select_n.166), kind=kOutput, calls=%fused_computation.25 | convolution fusion | flops 134217728 | bytes 2686980 | tf_op jit(solution)/shard_map/dot_general | solution.py:16
  103.6 0.5 fusion
  104.1 2.0 %collective-permute-start.10 = (bf16[64,2048]{1,0:T(8,128)(2,1)S(1)}, bf16[64,2048]{1,0:T(8,128)(2,1)S(1)}, u32[]{:S(2)}, u32[]{:S(2)}) collective-permute-start(bf16[64,2048]{1,0:T(8,128)(2,1)S(1)} %slice.40), channel_id=1, source_target_pairs={{0,4},{4,8},{8,12},{12,14},{14,10},{10,6},{6,2},{2,0},{1,5},{5,9},... | collective-permute-start | bytes 786440 | tf_op jit(solution)/shard_map/ppermute | solution.py:197
  106.1 1.5 %fusion.9 = f32[256,2048]{1,0:T(8,128)S(1)} fusion(bf16[128,2048]{1,0:T(8,128)(2,1)} %collective-permute-done.3, bf16[8,128,256]{2,1,0:T(8,128)(2,1)S(1)} %slice.44, s32[]{:T(128)S(6)} %select_n.168), kind=kOutput, calls=%fused_computation.23 | convolution fusion | flops 134217728 | bytes 2686980 | tf_op jit(solution)/shard_map/dot_general | solution.py:16
  107.6 1.8 %collective-permute-done.10 = bf16[64,2048]{1,0:T(8,128)(2,1)S(1)} collective-permute-done((bf16[64,2048]{1,0:T(8,128)(2,1)S(1)}, bf16[64,2048]{1,0:T(8,128)(2,1)S(1)}, u32[]{:S(2)}, u32[]{:S(2)}) %collective-permute-start.10) | collective-permute-done | bytes 262176 | tf_op jit(solution)/shard_map/ppermute | solution.py:197
  109.4 0.5 fusion.28
  109.9 1.7 %collective-permute-done.11 = bf16[64,2048]{1,0:T(8,128)(2,1)S(1)} collective-permute-done((bf16[64,2048]{1,0:T(8,128)(2,1)S(1)}, bf16[64,2048]{1,0:T(8,128)(2,1)S(1)}, u32[]{:S(2)}, u32[]{:S(2)}) %collective-permute-start.11) | collective-permute-done | bytes 262176 | tf_op jit(solution)/shard_map/ppermute | solution.py:198
  111.6 0.5 fusion.27
  112.1 0.6 add_add_fusion
  112.7 1.1 dynamic-slice_bitcast_fusion
  113.7 3.3 %collective-permute-start.12 = (f32[128,2048]{1,0:T(8,128)}, f32[128,2048]{1,0:T(8,128)}, u32[]{:S(2)}, u32[]{:S(2)}) collective-permute-start(f32[128,2048]{1,0:T(8,128)} %dynamic-slice_bitcast_fusion), channel_id=1, source_target_pairs={{0,1},{1,0},{2,3},{3,2},{4,5},{5,4},{6,7},{7,6},{8,9},{9,8},{10,11... | collective-permute-start | bytes 3145736 | tf_op jit(solution)/shard_map/ppermute | solution.py:20
  117.1 1.0 convert_reduce_fusion
  118.1 0.6 broadcast_multiply_fusion
  118.7 1.0 collective-permute-done.12
  119.7 2.3 %fusion.3 = f32[1,128,2048]{2,1,0:T(8,128)} fusion(f32[128,2048]{1,0:T(8,128)} %collective-permute-done.12, f32[2,128,2048]{2,1,0:T(8,128)S(1)} %bitcast.87, s32[]{:T(128)S(6)} %select_n.173), kind=kLoop, calls=%fused_computation.8 | loop fusion | flops 524288 | bytes 3145732 | tf_op jit(solution)/shard_map/broadcast_in_dim | solution.py:204
  (35 shorter events, 0.5 us)
Async XLA Ops:
  0.6 10.7 %copy-start = (bf16[256,2048]{1,0:T(8,128)(2,1)S(1)}, bf16[256,2048]{1,0:T(8,128)(2,1)}, u32[]{:S(2)}) copy-start(bf16[256,2048]{1,0:T(8,128)(2,1)} %param.6) | copy-start | bytes 3145732
  0.6 3.5 %copy-start.1 = (bf16[1,2048,2048]{2,1,0:T(8,128)(2,1)S(1)}, bf16[1,2048,2048]{2,1,0:T(8,128)(2,1)}, u32[]{:S(2)}) copy-start(bf16[1,2048,2048]{2,1,0:T(8,128)(2,1)} %param.5) | copy-start | bytes 25165828
  4.1 1.0 copy-start.3
  5.2 6.2 %copy-start.12 = (s32[128]{0:T(128)S(1)}, s32[128]{0:T(128)}, u32[]{:S(2)}) copy-start(s32[128]{0:T(128)} %param.7) | copy-start | bytes 1540
  8.1 13.8 %copy-start.4 = (bf16[1,128,2048]{2,1,0:T(8,128)(2,1)S(1)}, bf16[1,128,2048]{2,1,0:T(8,128)(2,1)}, u32[]{:S(2)}) copy-start(bf16[1,128,2048]{2,1,0:T(8,128)(2,1)} %param.4) | copy-start | bytes 1572868
  8.1 13.8 %collective-permute-start = (bf16[2,128,1024]{2,1,0:T(8,128)(2,1)S(1)}, bf16[2,128,1024]{2,1,0:T(8,128)(2,1)S(1)}, u32[]{:S(2)}, u32[]{:S(2)}) collective-permute-start(bf16[2,128,1024]{2,1,0:T(8,128)(2,1)S(1)} %shard_map.67), channel_id=1, source_target_pairs={{0,16},{1,17},{2,18},{3,19},{4,20},{5,21},{6,22},{7,23},{8,24},{9,... | collective-permute-start | bytes 1572872 | tf_op jit(solution)/shard_map/ppermute | solution.py:151
  21.9 3.4 %copy-start.2 = (bf16[1,2048,2048]{2,1,0:T(8,128)(2,1)S(1)}, bf16[1,2048,2048]{2,1,0:T(8,128)(2,1)}, u32[]{:S(2)}) copy-start(bf16[1,2048,2048]{2,1,0:T(8,128)(2,1)} %param.5) | copy-start | bytes 25165828
  33.1 4.4 %collective-permute-start.8 = (f32[128,2048]{1,0:T(8,128)S(1)}, f32[128,2048]{1,0:T(8,128)S(1)}, u32[]{:S(2)}, u32[]{:S(2)}) collective-permute-start(f32[128,2048]{1,0:T(8,128)S(1)} %get-tuple-element.16), channel_id=1, source_target_pairs={{0,1},{1,0},{2,3},{3,2},{4,5},{5,4},{6,7},{7,6},{8,9},{9,8},{10,11... | collective-permute-start | bytes 3145736 | tf_op jit(solution)/shard_map/ppermute | solution.py:20
  34.7 17.4 %collective-permute-start.1 = (bf16[128,2048]{1,0:T(8,128)(2,1)S(1)}, bf16[128,2048]{1,0:T(8,128)(2,1)S(1)}, u32[]{:S(2)}, u32[]{:S(2)}) collective-permute-start(bf16[128,2048]{1,0:T(8,128)(2,1)S(1)} %get-tuple-element.12), channel_id=1, source_target_pairs={{0,4},{4,8},{8,12},{12,14},{14,10},{10,6},{6,2},{2,0},{1,5},{5,9},... | collective-permute-start | bytes 1572872 | tf_op jit(solution)/shard_map/ppermute | solution.py:173
  36.0 17.5 %collective-permute-start.4 = (bf16[128,2048]{1,0:T(8,128)(2,1)S(1)}, bf16[128,2048]{1,0:T(8,128)(2,1)S(1)}, u32[]{:S(2)}, u32[]{:S(2)}) collective-permute-start(bf16[128,2048]{1,0:T(8,128)(2,1)S(1)} %get-tuple-element.12), channel_id=1, source_target_pairs={{4,0},{8,4},{12,8},{14,12},{10,14},{6,10},{2,6},{0,2},{5,1},{9,5},... | collective-permute-start | bytes 1572872 | tf_op jit(solution)/shard_map/ppermute | solution.py:174
  36.2 15.0 %collective-permute-start.7 = (bf16[128,2048]{1,0:T(8,128)(2,1)S(1)}, bf16[128,2048]{1,0:T(8,128)(2,1)S(1)}, u32[]{:S(2)}, u32[]{:S(2)}) collective-permute-start(bf16[128,2048]{1,0:T(8,128)(2,1)S(1)} %get-tuple-element.13), channel_id=1, source_target_pairs={{16,0},{17,1},{18,2},{19,3},{20,4},{21,5},{22,6},{23,7},{24,8},{25... | collective-permute-start | bytes 1572872 | tf_op jit(solution)/shard_map/ppermute | solution.py:157
  37.6 19.1 %collective-permute-start.9 = (bf16[8,8,2048]{2,1,0:T(8,128)(2,1)S(1)}, bf16[8,8,2048]{2,1,0:T(8,128)(2,1)S(1)}, u32[]{:S(2)}, u32[]{:S(2)}) collective-permute-start(bf16[8,8,2048]{2,1,0:T(8,128)(2,1)S(1)} %slice_bitcast_fusion.1), channel_id=1, source_target_pairs={{16,0},{17,1},{18,2},{19,3},{20,4},{21,5},{22,6},{23,7},{24,8},{25... | collective-permute-start | bytes 786440 | tf_op jit(solution)/shard_map/ppermute | solution.py:160
  52.1 17.8 %copy-start.8 = (bf16[128,2048]{1,0:T(8,128)(2,1)}, bf16[128,2048]{1,0:T(8,128)(2,1)S(1)}, u32[]{:S(2)}) copy-start(bf16[128,2048]{1,0:T(8,128)(2,1)S(1)} %collective-permute-done.1) | copy-start | bytes 1572868
  52.2 11.3 %collective-permute-start.2 = (bf16[128,2048]{1,0:T(8,128)(2,1)S(1)}, bf16[128,2048]{1,0:T(8,128)(2,1)S(1)}, u32[]{:S(2)}, u32[]{:S(2)}) collective-permute-start(bf16[128,2048]{1,0:T(8,128)(2,1)S(1)} %collective-permute-done.1), channel_id=1, source_target_pairs={{0,4},{4,8},{8,12},{12,14},{14,10},{10,6},{6,2},{2,0},{1,5},{5,9},... | collective-permute-start | bytes 1572872 | tf_op jit(solution)/shard_map/ppermute | solution.py:173
  53.5 9.9 %copy-start.9 = (bf16[128,2048]{1,0:T(8,128)(2,1)}, bf16[128,2048]{1,0:T(8,128)(2,1)S(1)}, u32[]{:S(2)}) copy-start(bf16[128,2048]{1,0:T(8,128)(2,1)S(1)} %collective-permute-done.4) | copy-start | bytes 1572868
  53.5 10.9 %collective-permute-start.5 = (bf16[128,2048]{1,0:T(8,128)(2,1)S(1)}, bf16[128,2048]{1,0:T(8,128)(2,1)}, u32[]{:S(2)}, u32[]{:S(2)}) collective-permute-start(bf16[128,2048]{1,0:T(8,128)(2,1)S(1)} %collective-permute-done.4), channel_id=1, source_target_pairs={{4,0},{8,4},{12,8},{14,12},{10,14},{6,10},{2,6},{0,2},{5,1},{9,5},... | collective-permute-start | bytes 1572872 | tf_op jit(solution)/shard_map/ppermute | solution.py:174
  63.4 0.8 copy-start.10
  64.4 33.7 %all-to-all-start = ((bf16[8,192,256]{2,1,0:T(8,128)(2,1)}), bf16[8,192,256]{2,1,0:T(8,128)(2,1)S(1)}, u32[]{:S(2)}, u32[]{:S(2)}) async-start(bf16[8,192,256]{2,1,0:T(8,128)(2,1)} %pad_maximum_fusion), calls=%async_computation | async-start | bytes 1572864 | tf_op jit(solution)/shard_map/all_to_all | solution.py:182
  69.9 26.9 %collective-permute-start.3 = (bf16[128,2048]{1,0:T(8,128)(2,1)}, bf16[128,2048]{1,0:T(8,128)(2,1)}, u32[]{:S(2)}, u32[]{:S(2)}) collective-permute-start(bf16[128,2048]{1,0:T(8,128)(2,1)} %copy-done.10), channel_id=1, source_target_pairs={{0,4},{4,8},{8,12},{12,14},{14,10},{10,6},{6,2},{2,0},{1,5},{5,9},... | collective-permute-start | bytes 1572872 | tf_op jit(solution)/shard_map/ppermute | solution.py:173
  71.1 26.9 %collective-permute-start.6 = (bf16[128,2048]{1,0:T(8,128)(2,1)}, bf16[128,2048]{1,0:T(8,128)(2,1)S(1)}, u32[]{:S(2)}, u32[]{:S(2)}) collective-permute-start(bf16[128,2048]{1,0:T(8,128)(2,1)} %collective-permute-done.5), channel_id=1, source_target_pairs={{4,0},{8,4},{12,8},{14,12},{10,14},{6,10},{2,6},{0,2},{5,1},{9,5},... | collective-permute-start | bytes 1572872 | tf_op jit(solution)/shard_map/ppermute | solution.py:174
  98.1 2.0 %copy-start.6 = (bf16[128,2048]{1,0:T(8,128)(2,1)}, bf16[128,2048]{1,0:T(8,128)(2,1)S(1)}, u32[]{:S(2)}) copy-start(bf16[128,2048]{1,0:T(8,128)(2,1)S(1)} %collective-permute-done.6) | copy-start | bytes 1572868
  98.1 4.0 %copy-start.5 = (bf16[8,192,256]{2,1,0:T(8,128)(2,1)}, bf16[8,192,256]{2,1,0:T(8,128)(2,1)S(1)}, u32[]{:S(2)}) copy-start(bf16[8,192,256]{2,1,0:T(8,128)(2,1)S(1)} %all-to-all-done) | copy-start | bytes 2359300
  102.1 1.6 %copy-start.11 = (bf16[128,2048]{1,0:T(8,128)(2,1)S(1)}, bf16[128,2048]{1,0:T(8,128)(2,1)}, u32[]{:S(2)}) copy-start(bf16[128,2048]{1,0:T(8,128)(2,1)} %copy-done.10) | copy-start | bytes 1572868
  104.1 5.3 %collective-permute-start.10 = (bf16[64,2048]{1,0:T(8,128)(2,1)S(1)}, bf16[64,2048]{1,0:T(8,128)(2,1)S(1)}, u32[]{:S(2)}, u32[]{:S(2)}) collective-permute-start(bf16[64,2048]{1,0:T(8,128)(2,1)S(1)} %slice.40), channel_id=1, source_target_pairs={{0,4},{4,8},{8,12},{12,14},{14,10},{10,6},{6,2},{2,0},{1,5},{5,9},... | collective-permute-start | bytes 786440 | tf_op jit(solution)/shard_map/ppermute | solution.py:197
  106.1 5.5 %collective-permute-start.11 = (bf16[64,2048]{1,0:T(8,128)(2,1)S(1)}, bf16[64,2048]{1,0:T(8,128)(2,1)S(1)}, u32[]{:S(2)}, u32[]{:S(2)}) collective-permute-start(bf16[64,2048]{1,0:T(8,128)(2,1)S(1)} %slice.41), channel_id=1, source_target_pairs={{4,0},{8,4},{12,8},{14,12},{10,14},{6,10},{2,6},{0,2},{5,1},{9,5},... | collective-permute-start | bytes 786440 | tf_op jit(solution)/shard_map/ppermute | solution.py:198
  107.6 4.5 %copy-start.7 = (bf16[128,2048]{1,0:T(8,128)(2,1)S(1)}, bf16[128,2048]{1,0:T(8,128)(2,1)}, u32[]{:S(2)}) copy-start(bf16[128,2048]{1,0:T(8,128)(2,1)} %copy-done.6) | copy-start | bytes 1572868
  113.7 6.0 %collective-permute-start.12 = (f32[128,2048]{1,0:T(8,128)}, f32[128,2048]{1,0:T(8,128)}, u32[]{:S(2)}, u32[]{:S(2)}) collective-permute-start(f32[128,2048]{1,0:T(8,128)} %dynamic-slice_bitcast_fusion), channel_id=1, source_target_pairs={{0,1},{1,0},{2,3},{3,2},{4,5},{5,4},{6,7},{7,6},{8,9},{9,8},{10,11... | collective-permute-start | bytes 3145736 | tf_op jit(solution)/shard_map/ppermute | solution.py:20

commit v2 on v1

--- a/solution.py
+++ b/solution.py
@@ -178,25 +178,21 @@
     rel_own = rel_own.transpose(0, 2, 1, 3).reshape(chips, owned * chips, cols)
     left = columns(jnp.where(first, query_back, mixed))
     sent = jnp.concatenate([left, rel_own], axis=1)
-    sent, _ = lax.optimization_barrier((sent, (blocks[3][0], blocks[4][0])))
+    sent, _ = lax.optimization_barrier((sent, (blocks[-2][0], blocks[-1][0])))
     received = lax.all_to_all(sent, "chip", 0, 0, tiled=True)
     left_cols, rel_rows = received[:, :rows_dev], received[:, rows_dev:]
     rel_sum = jnp.sum(rel_rows.astype(F32), axis=0) * jnp.sqrt(F32(count_rel) / F32(total_rows))
     relation_grad = rel_sum.reshape(chips, owned, cols).transpose(1, 0, 2).reshape(owned, width)
 
-    def add(partial, blocks):
-        for block, step, base in blocks:
-            left = lax.dynamic_index_in_dim(left_cols, chip_at(place + step), 0, keepdims=False)
-            partial = partial + dot(left[base:base + block.shape[0]], block, 0, 0)
-        return partial
-
-    partial = add(jnp.zeros((cols, width), F32), blocks[:5])
     if chips % 2 == 0:
         mid = rows_dev // 2
-        top, bottom, partial = lax.optimization_barrier((fwd[:mid], bwd[mid:], partial))
-        blocks.append((lax.ppermute(top, "chip", up), chips // 2, 0))
-        blocks.append((lax.ppermute(bottom, "chip", down), chips // 2, mid))
-    partial = add(partial, blocks[5:])
+        blocks.append((lax.ppermute(fwd[:mid], "chip", up), chips // 2, 0))
+        blocks.append((lax.ppermute(bwd[mid:], "chip", down), chips // 2, mid))
+    right_all = jnp.zeros((chips * rows_dev, width), BF16)
+    for block, step, base in blocks:
+        start = chip_at(place + step) * rows_dev + base
+        right_all = lax.dynamic_update_slice_in_dim(right_all, block, start, 0)
+    partial = dot(left_cols.reshape(chips * rows_dev, cols), right_all, 0, 0)
     partial = partial.reshape(2, cols // 2, width)
     keep = lax.dynamic_index_in_dim(partial, core, 0, keepdims=False)
     give = lax.dynamic_index_in_dim(partial, 1 - core, 0, keepdims=False)

time: 124 us -> 122 us (0.984)
  local copies, waits for them, and re-layouts: 13.1 us -> 30.8 us
  waiting for transfers between devices: 59.2 us -> 42.8 us
  matrix products: 9.26 us -> 3.95 us
  other arithmetic: 6.09 us -> 8.29 us
  starting transfers between devices: 22.8 us -> 20.8 us
    ppermute x3, waiting for transfers between devices: 31.1 us -> 15.7 us  [local(): fwd = lax.ppermute(fwd, 'chip', up)]
    dynamic_update_slice x0 -> x9, local copies, waits for them, and re-layouts: none -> 12.6 us  [local(): right_all = lax.dynamic_update_slice_in_dim(right_all, block, start, 0)]
    ppermute x2, waiting for transfers between devices: 3.55 us -> 15 us  [the longest x1 14.3 us: local(): blocks.append((lax.ppermute(fwd[:mid], 'chip', up), chips // 2, 0))]
    ppermute x1, waiting for transfers between devices: 12.2 us -> 1.39 us  [local(): query_back = lax.ppermute(grad_query, 'hop', [(1, 0)])]
    dot_general x10 -> x2, matrix products: 9.26 us -> 3.95 us  [dot(): lax.dot_general(a, b, (((ca,), (cb,)), ((), ())), preferred_element_type=...]
    unnamed x26 -> x28, local copies, waits for them, and re-layouts: 8.74 us -> 11.3 us
    broadcast_in_dim x0 -> x1, local copies, waits for them, and re-layouts: none -> 2.47 us  [local(): right_all = jnp.zeros((chips * rows_dev, width), BF16)]
    ppermute x1, waiting for transfers between devices: 3.11 us -> 1.01 us  [local(): rel_back = lax.ppermute(rel_chip[:, 0], 'hop', [(1, 0)])]
  transfers between devices with their start and end apart: 14 -> 14, of which waited for: 10 -> 10; matrix products, arithmetic and copies ran while one was open for 8% -> 20% of each run, Pallas kernels for 0% -> 0%
where the time goes in v2:
time: 122 us; the launch traced here: 119 us
  waiting for transfers between devices  42.8 us (35%)
  local copies, waits for them, and re-layouts  30.8 us (25%)
  starting transfers between devices  20.8 us (17%)
  Pallas kernels  11.6 us (10%)
  other arithmetic  8.29 us (7%)
  matrix products  3.95 us (3%)
    ppermute x3, waiting for transfers between devices, local(): fwd = lax.ppermute(fwd, 'chip', up)  15.7 us
    ppermute x1, waiting for transfers between devices, local(): blocks.append((lax.ppermute(fwd[:mid], 'chip', up), chips // 2, 0))  14.3 us
    dynamic_update_slice x9, local copies, waits for them, and re-layouts, local(): right_all = lax.dynamic_update_slice_in_dim(right_all, block, start, 0)  12.6 us
    unnamed x28, local copies, waits for them, and re-layouts  11.3 us
    pallas_call x1, Pallas kernels, trail(): pl.pallas_call(trail_body, out_shape=(jax.ShapeDtypeStruct((rows_dev, hid...  8.76 us
    ppermute x1, waiting for transfers between devices, local(): query = lax.ppermute(own_query, 'hop', [(0, 1)])  7.79 us
    all_to_all x1, starting transfers between devices, local(): received = lax.all_to_all(sent, 'chip', 0, 0, tiled=True)  4.72 us
    ppermute x2, starting transfers between devices, swap_core(): return lax.ppermute(block, 'core', [(0, 1), (1, 0)])  4.41 us
  transfers between devices with their start and end apart: 14, of which 10 were waited for; matrix products, arithmetic and copies ran while one was open for 20% of the time, Pallas kernels for 0%

profile of v2, /device:TPU:9, one launch (start us, length us, event | category | flops | bytes accessed | tf_op | source)
XLA Modules:
  0.0 119.4 jit_solution(9987109510737780358)
XLA Ops:
  0.7 3.5 %copy-done.1 = bf16[1,2048,2048]{2,1,0:T(8,128)(2,1)S(1)} copy-done((bf16[1,2048,2048]{2,1,0:T(8,128)(2,1)S(1)}, bf16[1,2048,2048]{2,1,0:T(8,128)(2,1)}, u32[]{:S(2)}) %copy-start.1) | copy-done | bytes 8388632
  4.1 1.0 copy-done.3
  5.2 2.9 %shard_map.67 = bf16[2,128,1024]{2,1,0:T(8,128)(2,1)S(1)} custom-call(bf16[128,2048]{1,0:T(8,128)(2,1)S(1)} %bitcast.52, bf16[2048,2048]{1,0:T(8,128)(2,1)S(1)} %bitcast.50), custom_call_target="tpu_custom_call" | custom-call | flops 1073741824 | bytes 8388608 | tf_op jit(solution)/shard_map/pallas_call | solution.py:43
  8.1 3.2 %collective-permute-start = (bf16[2,128,1024]{2,1,0:T(8,128)(2,1)S(1)}, bf16[2,128,1024]{2,1,0:T(8,128)(2,1)S(1)}, u32[]{:S(2)}, u32[]{:S(2)}) collective-permute-start(bf16[2,128,1024]{2,1,0:T(8,128)(2,1)S(1)} %shard_map.67), channel_id=1, source_target_pairs={{0,16},{1,17},{2,18},{3,19},{4,20},{5,21},{6,22},{7,23},{8,24},{9,... | collective-permute-start | bytes 1572872 | tf_op jit(solution)/shard_map/ppermute | solution.py:151
  11.6 1.0 copy.9
  12.6 1.2 %copy.10 = bf16[128,2,1024]{2,0,1:T(8,128)(2,1)S(1)} copy(bf16[128,2,1024]{0,2,1:T(8,128)(2,1)} %bitcast.58) | data formatting | bytes 1048576 | tf_op jit(solution)/shard_map/reshape | solution.py:153
  14.0 7.8 %collective-permute-done.query = bf16[2,128,1024]{2,1,0:T(8,128)(2,1)S(1)} collective-permute-done((bf16[2,128,1024]{2,1,0:T(8,128)(2,1)S(1)}, bf16[2,128,1024]{2,1,0:T(8,128)(2,1)S(1)}, u32[]{:S(2)}, u32[]{:S(2)}) %collective-permute-start) | collective-permute-done | bytes 524320 | tf_op jit(solution)/shard_map/ppermute | solution.py:151
  21.8 0.8 copy-done.5
  22.6 3.4 %copy-done.2 = bf16[1,2048,2048]{2,1,0:T(8,128)(2,1)S(1)} copy-done((bf16[1,2048,2048]{2,1,0:T(8,128)(2,1)S(1)}, bf16[1,2048,2048]{2,1,0:T(8,128)(2,1)}, u32[]{:S(2)}) %copy-start.2) | copy-done | bytes 8388632
  26.0 1.0 copy-done.6
  27.0 8.8 %shard_map.68 = (bf16[128,2048]{1,0:T(8,128)(2,1)}, bf16[128,2048]{1,0:T(8,128)(2,1)}, f32[128,2048]{1,0:T(8,128)}, f32[128,2048]{1,0:T(8,128)S(1)}, bf16[128,2048]{1,0:T(8,128)(2,1)S(1)}) custom-call(s32[1]{0:T(128)} %bitcast.first, bf16[2,128,1024]{2,1,0:T(8,128)(2,1)S(1)} %copy-done.6, bf16[128,2048]{1,0:T(8,128)(2,1)S(1)} %bitcast.53, ...), custom_call_target="tpu_custom_call" | custom-call | flops 2415919104 | bytes 16777216 | tf_op jit(solution)/shard_map/pallas_call | solution.py:105
  35.8 0.8 copy-done.7
  36.6 1.5 %collective-permute-start.2 = (f32[128,2048]{1,0:T(8,128)}, f32[128,2048]{1,0:T(8,128)}, u32[]{:S(2)}, u32[]{:S(2)}) collective-permute-start(f32[128,2048]{1,0:T(8,128)} %get-tuple-element.12), channel_id=1, source_target_pairs={{0,1},{1,0},{2,3},{3,2},{4,5},{5,4},{6,7},{7,6},{8,9},{9,8},{10,11... | collective-permute-start | bytes 3145736 | tf_op jit(solution)/shard_map/ppermute | solution.py:20
  38.1 1.3 %collective-permute-start.4 = (bf16[128,2048]{1,0:T(8,128)(2,1)}, bf16[128,2048]{1,0:T(8,128)(2,1)}, u32[]{:S(2)}, u32[]{:S(2)}) collective-permute-start(bf16[128,2048]{1,0:T(8,128)(2,1)} %get-tuple-element.13), channel_id=1, source_target_pairs={{0,4},{4,8},{8,12},{12,14},{14,10},{10,6},{6,2},{2,0},{1,5},{5,9},... | collective-permute-start | bytes 1572872 | tf_op jit(solution)/shard_map/ppermute | solution.py:173
  39.6 1.3 %collective-permute-start.1 = (bf16[128,2048]{1,0:T(8,128)(2,1)}, bf16[128,2048]{1,0:T(8,128)(2,1)S(1)}, u32[]{:S(2)}, u32[]{:S(2)}) collective-permute-start(bf16[128,2048]{1,0:T(8,128)(2,1)} %get-tuple-element.9), channel_id=1, source_target_pairs={{16,0},{17,1},{18,2},{19,3},{20,4},{21,5},{22,6},{23,7},{24,8},{25... | collective-permute-start | bytes 1572872 | tf_op jit(solution)/shard_map/ppermute | solution.py:157
  41.0 2.5 %broadcast_in_dim.20 = bf16[1024,2048]{1,0:T(8,128)(2,1)} broadcast(bf16[]{:T(256)} %constant.145.clone.1), dimensions={} | broadcast | bytes 4194306 | tf_op jit(solution)/shard_map/broadcast_in_dim | solution.py:191
  43.5 1.9 %constant_dynamic-update-slice_fusion.8 = bf16[1024,2048]{1,0:T(8,128)(2,1)} fusion(bf16[1024,2048]{1,0:T(8,128)(2,1)} %broadcast_in_dim.20, bf16[128,2048]{1,0:T(8,128)(2,1)} %get-tuple-element.13, s32[]{:T(128)S(6)} %select_n.159), kind=kLoop, calls=%fused_computation.28 | loop fusion | bytes 1048580 | tf_op jit(solution)/shard_map/dynamic_update_slice | solution.py:194
  45.4 6.6 %collective-permute-done.4 = bf16[128,2048]{1,0:T(8,128)(2,1)} collective-permute-done((bf16[128,2048]{1,0:T(8,128)(2,1)}, bf16[128,2048]{1,0:T(8,128)(2,1)}, u32[]{:S(2)}, u32[]{:S(2)}) %collective-permute-start.4) | collective-permute-done | bytes 524320 | tf_op jit(solution)/shard_map/ppermute | solution.py:173
  52.0 1.3 %collective-permute-start.5 = (bf16[128,2048]{1,0:T(8,128)(2,1)}, bf16[128,2048]{1,0:T(8,128)(2,1)S(1)}, u32[]{:S(2)}, u32[]{:S(2)}) collective-permute-start(bf16[128,2048]{1,0:T(8,128)(2,1)} %collective-permute-done.4), channel_id=1, source_target_pairs={{0,4},{4,8},{8,12},{12,14},{14,10},{10,6},{6,2},{2,0},{1,5},{5,9},... | collective-permute-start | bytes 1572872 | tf_op jit(solution)/shard_map/ppermute | solution.py:173
  53.4 1.4 %collective-permute-done.1 = bf16[128,2048]{1,0:T(8,128)(2,1)S(1)} collective-permute-done((bf16[128,2048]{1,0:T(8,128)(2,1)}, bf16[128,2048]{1,0:T(8,128)(2,1)S(1)}, u32[]{:S(2)}, u32[]{:S(2)}) %collective-permute-start.1) | collective-permute-done | bytes 524320 | tf_op jit(solution)/shard_map/ppermute | solution.py:157
  54.8 0.8 copy-done.12
  55.6 1.9 %broadcast_select_fusion = (bf16[128,2048]{1,0:T(8,128)(2,1)}, bf16[128,2048]{1,0:T(8,128)(2,1)S(1)}) fusion(bf16[128,2048]{1,0:T(8,128)(2,1)} %copy-done.12, bf16[128,2048]{1,0:T(8,128)(2,1)} %get-tuple-element.9, pred[]{:T(512)S(6)} %eq.44, bf16[128,2048]{1,0:T(8,128)(2,1)S(1)} %copy-done.8), kind=kLoop, calls=%fused_computation.11 | loop fusion | flops 524288 | bytes 2621441 | tf_op jit(solution)/shard_map/jit(_where)/select_n | solution.py:158
  57.6 1.3 %add_convert_fusion = bf16[128,2048]{1,0:T(8,128)(2,1)S(1)} fusion(f32[128,2048]{1,0:T(8,128)S(1)} %get-tuple-element.11, f32[128,2048]{1,0:T(8,128)} %collective-permute-done.2), kind=kLoop, calls=%fused_computation.7 | loop fusion | flops 524288 | bytes 2621440 | tf_op jit(solution)/shard_map/convert_element_type | solution.py:159
  58.9 1.3 %collective-permute-start.3 = (bf16[8,8,2048]{2,1,0:T(8,128)(2,1)S(1)}, bf16[8,8,2048]{2,1,0:T(8,128)(2,1)S(1)}, u32[]{:S(2)}, u32[]{:S(2)}) collective-permute-start(bf16[8,8,2048]{2,1,0:T(8,128)(2,1)S(1)} %slice_bitcast_fusion.1), channel_id=1, source_target_pairs={{16,0},{17,1},{18,2},{19,3},{20,4},{21,5},{22,6},{23,7},{24,8},{25... | collective-permute-start | bytes 786440 | tf_op jit(solution)/shard_map/ppermute | solution.py:160
  60.2 1.9 %constant_dynamic-update-slice_fusion.7 = bf16[1024,2048]{1,0:T(8,128)(2,1)} fusion(bf16[1024,2048]{1,0:T(8,128)(2,1)} %constant_dynamic-update-slice_fusion.8, bf16[128,2048]{1,0:T(8,128)(2,1)} %collective-permute-done.4, s32[]{:T(128)S(6)} %select_n.161), kind=kLoop, calls=%fused_computation.27 | loop fusion | bytes 1048580 | tf_op jit(solution)/shard_map/dynamic_update_slice | solution.py:194
  62.2 1.9 %constant_dynamic-update-slice_fusion.6 = bf16[1024,2048]{1,0:T(8,128)(2,1)} fusion(bf16[1024,2048]{1,0:T(8,128)(2,1)} %constant_dynamic-update-slice_fusion.7, bf16[128,2048]{1,0:T(8,128)(2,1)} %collective-permute-done.7, s32[]{:T(128)S(6)} %select_n.163), kind=kLoop, calls=%fused_computation.26 | loop fusion | bytes 1048580 | tf_op jit(solution)/shard_map/dynamic_update_slice | solution.py:194
  64.1 0.8 collective-permute-done.5
  64.8 1.3 %collective-permute-start.6 = (bf16[128,2048]{1,0:T(8,128)(2,1)S(1)}, bf16[128,2048]{1,0:T(8,128)(2,1)S(1)}, u32[]{:S(2)}, u32[]{:S(2)}) collective-permute-start(bf16[128,2048]{1,0:T(8,128)(2,1)S(1)} %collective-permute-done.5), channel_id=1, source_target_pairs={{0,4},{4,8},{8,12},{12,14},{14,10},{10,6},{6,2},{2,0},{1,5},{5,9},... | collective-permute-start | bytes 1572872 | tf_op jit(solution)/shard_map/ppermute | solution.py:173
  66.3 1.0 collective-permute-done.3
  67.4 0.9 pad_maximum_fusion
  68.3 8.3 %collective-permute-done.6 = bf16[128,2048]{1,0:T(8,128)(2,1)S(1)} collective-permute-done((bf16[128,2048]{1,0:T(8,128)(2,1)S(1)}, bf16[128,2048]{1,0:T(8,128)(2,1)S(1)}, u32[]{:S(2)}, u32[]{:S(2)}) %collective-permute-start.6) | collective-permute-done | bytes 524320 | tf_op jit(solution)/shard_map/ppermute | solution.py:173
  76.6 1.0 collective-permute-done.9
  77.6 4.7 %all-to-all-start = ((bf16[8,192,256]{2,1,0:T(8,128)(2,1)}), bf16[8,192,256]{2,1,0:T(8,128)(2,1)S(1)}, u32[]{:S(2)}, u32[]{:S(2)}) async-start(bf16[8,192,256]{2,1,0:T(8,128)(2,1)} %pad_maximum_fusion), calls=%async_computation | async-start | bytes 1572864 | tf_op jit(solution)/shard_map/all_to_all | solution.py:182
  82.3 1.9 %constant_dynamic-update-slice_fusion.5 = bf16[1024,2048]{1,0:T(8,128)(2,1)} fusion(bf16[1024,2048]{1,0:T(8,128)(2,1)} %constant_dynamic-update-slice_fusion.6, bf16[128,2048]{1,0:T(8,128)(2,1)} %copy-done.10, s32[]{:T(128)S(6)} %select_n.165), kind=kLoop, calls=%fused_computation.25 | loop fusion | bytes 1048580 | tf_op jit(solution)/shard_map/dynamic_update_slice | solution.py:194
  84.2 1.9 %constant_dynamic-update-slice_fusion.4 = bf16[1024,2048]{1,0:T(8,128)(2,1)} fusion(bf16[1024,2048]{1,0:T(8,128)(2,1)} %constant_dynamic-update-slice_fusion.5, bf16[128,2048]{1,0:T(8,128)(2,1)} %copy-done.11, s32[]{:T(128)S(6)} %select_n.167), kind=kLoop, calls=%fused_computation.24 | loop fusion | bytes 1048580 | tf_op jit(solution)/shard_map/dynamic_update_slice | solution.py:194
  86.1 1.2 %collective-permute-start.10 = (bf16[64,2048]{1,0:T(8,128)(2,1)S(1)}, bf16[64,2048]{1,0:T(8,128)(2,1)S(1)}, u32[]{:S(2)}, u32[]{:S(2)}) collective-permute-start(bf16[64,2048]{1,0:T(8,128)(2,1)S(1)} %slice.27), channel_id=1, source_target_pairs={{0,4},{4,8},{8,12},{12,14},{14,10},{10,6},{6,2},{2,0},{1,5},{5,9},... | collective-permute-start | bytes 786440 | tf_op jit(solution)/shard_map/ppermute | solution.py:189
  87.7 0.8 constant_dynamic-update-slice_fusion.3
  88.6 0.8 constant_dynamic-update-slice_fusion.2
  89.4 14.3 %collective-permute-done.10 = bf16[64,2048]{1,0:T(8,128)(2,1)S(1)} collective-permute-done((bf16[64,2048]{1,0:T(8,128)(2,1)S(1)}, bf16[64,2048]{1,0:T(8,128)(2,1)S(1)}, u32[]{:S(2)}, u32[]{:S(2)}) %collective-permute-start.10) | collective-permute-done | bytes 262176 | tf_op jit(solution)/shard_map/ppermute | solution.py:189
  103.7 0.8 constant_dynamic-update-slice_fusion.1
  105.1 0.7 constant_dynamic-update-slice_fusion
  105.9 1.0 copy.13
  106.9 3.6 %fusion = f32[2,128,2048]{2,1,0:T(8,128)S(1)} fusion(bf16[2,128,1024]{2,1,0:T(8,128)(2,1)} %bitcast.61, bf16[1024,2048]{1,0:T(8,128)(2,1)} %constant_dynamic-update-slice_fusion), kind=kOutput, calls=%fused_computation | convolution fusion | flops 1073741824 | bytes 6815744 | tf_op jit(solution)/shard_map/dot_general | solution.py:16
  110.5 1.1 dynamic-slice_bitcast_fusion
  111.5 2.9 %collective-permute-start.12 = (f32[128,2048]{1,0:T(8,128)}, f32[128,2048]{1,0:T(8,128)}, u32[]{:S(2)}, u32[]{:S(2)}) collective-permute-start(f32[128,2048]{1,0:T(8,128)} %dynamic-slice_bitcast_fusion), channel_id=1, source_target_pairs={{0,1},{1,0},{2,3},{3,2},{4,5},{5,4},{6,7},{7,6},{8,9},{9,8},{10,11... | collective-permute-start | bytes 3145736 | tf_op jit(solution)/shard_map/ppermute | solution.py:20
  114.4 1.0 convert_reduce_fusion
  116.0 1.0 collective-permute-done.12
  117.0 2.3 %fusion.3 = f32[1,128,2048]{2,1,0:T(8,128)} fusion(f32[128,2048]{1,0:T(8,128)} %collective-permute-done.12, f32[2,128,2048]{2,1,0:T(8,128)S(1)} %fusion, s32[]{:T(128)S(6)} %select_n.175), kind=kLoop, calls=%fused_computation.5 | loop fusion | flops 524288 | bytes 3145732 | tf_op jit(solution)/shard_map/broadcast_in_dim | solution.py:200
  (40 shorter events, 2.8 us)
Async XLA Ops:
  0.6 10.6 %copy-start = (bf16[256,2048]{1,0:T(8,128)(2,1)S(1)}, bf16[256,2048]{1,0:T(8,128)(2,1)}, u32[]{:S(2)}) copy-start(bf16[256,2048]{1,0:T(8,128)(2,1)} %param.6) | copy-start | bytes 3145732
  0.6 3.5 %copy-start.1 = (bf16[1,2048,2048]{2,1,0:T(8,128)(2,1)S(1)}, bf16[1,2048,2048]{2,1,0:T(8,128)(2,1)}, u32[]{:S(2)}) copy-start(bf16[1,2048,2048]{2,1,0:T(8,128)(2,1)} %param.5) | copy-start | bytes 25165828
  4.1 1.0 copy-start.3
  5.2 6.1 %copy-start.13 = (s32[128]{0:T(128)S(1)}, s32[128]{0:T(128)}, u32[]{:S(2)}) copy-start(s32[128]{0:T(128)} %param.7) | copy-start | bytes 1540
  5.2 17.4 %copy-start.4 = (bf16[1,128,2048]{2,1,0:T(8,128)(2,1)S(1)}, bf16[1,128,2048]{2,1,0:T(8,128)(2,1)}, u32[]{:S(2)}) copy-start(bf16[1,128,2048]{2,1,0:T(8,128)(2,1)} %param.4) | copy-start | bytes 1572868
  8.1 13.7 %collective-permute-start = (bf16[2,128,1024]{2,1,0:T(8,128)(2,1)S(1)}, bf16[2,128,1024]{2,1,0:T(8,128)(2,1)S(1)}, u32[]{:S(2)}, u32[]{:S(2)}) collective-permute-start(bf16[2,128,1024]{2,1,0:T(8,128)(2,1)S(1)} %shard_map.67), channel_id=1, source_target_pairs={{0,16},{1,17},{2,18},{3,19},{4,20},{5,21},{6,22},{7,23},{8,24},{9,... | collective-permute-start | bytes 1572872 | tf_op jit(solution)/shard_map/ppermute | solution.py:151
  21.8 0.8 copy-start.5
  22.6 3.4 %copy-start.2 = (bf16[1,2048,2048]{2,1,0:T(8,128)(2,1)S(1)}, bf16[1,2048,2048]{2,1,0:T(8,128)(2,1)}, u32[]{:S(2)}) copy-start(bf16[1,2048,2048]{2,1,0:T(8,128)(2,1)} %param.5) | copy-start | bytes 25165828
  25.9 1.0 copy-start.6
  35.8 0.8 copy-start.7
  36.6 19.1 %copy-start.8 = (bf16[128,2048]{1,0:T(8,128)(2,1)S(1)}, bf16[128,2048]{1,0:T(8,128)(2,1)}, u32[]{:S(2)}) copy-start(bf16[128,2048]{1,0:T(8,128)(2,1)} %copy-done.7) | copy-start | bytes 1572868
  36.6 21.0 %collective-permute-start.2 = (f32[128,2048]{1,0:T(8,128)}, f32[128,2048]{1,0:T(8,128)}, u32[]{:S(2)}, u32[]{:S(2)}) collective-permute-start(f32[128,2048]{1,0:T(8,128)} %get-tuple-element.12), channel_id=1, source_target_pairs={{0,1},{1,0},{2,3},{3,2},{4,5},{5,4},{6,7},{7,6},{8,9},{9,8},{10,11... | collective-permute-start | bytes 3145736 | tf_op jit(solution)/shard_map/ppermute | solution.py:20
  38.1 13.9 %collective-permute-start.4 = (bf16[128,2048]{1,0:T(8,128)(2,1)}, bf16[128,2048]{1,0:T(8,128)(2,1)}, u32[]{:S(2)}, u32[]{:S(2)}) collective-permute-start(bf16[128,2048]{1,0:T(8,128)(2,1)} %get-tuple-element.13), channel_id=1, source_target_pairs={{0,4},{4,8},{8,12},{12,14},{14,10},{10,6},{6,2},{2,0},{1,5},{5,9},... | collective-permute-start | bytes 1572872 | tf_op jit(solution)/shard_map/ppermute | solution.py:173
  39.4 13.9 %collective-permute-start.7 = (bf16[128,2048]{1,0:T(8,128)(2,1)}, bf16[128,2048]{1,0:T(8,128)(2,1)}, u32[]{:S(2)}, u32[]{:S(2)}) collective-permute-start(bf16[128,2048]{1,0:T(8,128)(2,1)} %get-tuple-element.13), channel_id=1, source_target_pairs={{4,0},{8,4},{12,8},{14,12},{10,14},{6,10},{2,6},{0,2},{5,1},{9,5},... | collective-permute-start | bytes 1572872 | tf_op jit(solution)/shard_map/ppermute | solution.py:174
  39.6 15.3 %collective-permute-start.1 = (bf16[128,2048]{1,0:T(8,128)(2,1)}, bf16[128,2048]{1,0:T(8,128)(2,1)S(1)}, u32[]{:S(2)}, u32[]{:S(2)}) collective-permute-start(bf16[128,2048]{1,0:T(8,128)(2,1)} %get-tuple-element.9), channel_id=1, source_target_pairs={{16,0},{17,1},{18,2},{19,3},{20,4},{21,5},{22,6},{23,7},{24,8},{25... | collective-permute-start | bytes 1572872 | tf_op jit(solution)/shard_map/ppermute | solution.py:157
  52.0 12.9 %collective-permute-start.5 = (bf16[128,2048]{1,0:T(8,128)(2,1)}, bf16[128,2048]{1,0:T(8,128)(2,1)S(1)}, u32[]{:S(2)}, u32[]{:S(2)}) collective-permute-start(bf16[128,2048]{1,0:T(8,128)(2,1)} %collective-permute-done.4), channel_id=1, source_target_pairs={{0,4},{4,8},{8,12},{12,14},{14,10},{10,6},{6,2},{2,0},{1,5},{5,9},... | collective-permute-start | bytes 1572872 | tf_op jit(solution)/shard_map/ppermute | solution.py:173
  53.3 12.9 %collective-permute-start.8 = (bf16[128,2048]{1,0:T(8,128)(2,1)}, bf16[128,2048]{1,0:T(8,128)(2,1)S(1)}, u32[]{:S(2)}, u32[]{:S(2)}) collective-permute-start(bf16[128,2048]{1,0:T(8,128)(2,1)} %collective-permute-done.7), channel_id=1, source_target_pairs={{4,0},{8,4},{12,8},{14,12},{10,14},{6,10},{2,6},{0,2},{5,1},{9,5},... | collective-permute-start | bytes 1572872 | tf_op jit(solution)/shard_map/ppermute | solution.py:174
  54.8 0.8 copy-start.12
  58.9 8.4 %collective-permute-start.3 = (bf16[8,8,2048]{2,1,0:T(8,128)(2,1)S(1)}, bf16[8,8,2048]{2,1,0:T(8,128)(2,1)S(1)}, u32[]{:S(2)}, u32[]{:S(2)}) collective-permute-start(bf16[8,8,2048]{2,1,0:T(8,128)(2,1)S(1)} %slice_bitcast_fusion.1), channel_id=1, source_target_pairs={{16,0},{17,1},{18,2},{19,3},{20,4},{21,5},{22,6},{23,7},{24,8},{25... | collective-permute-start | bytes 786440 | tf_op jit(solution)/shard_map/ppermute | solution.py:160
  64.8 11.7 %copy-start.10 = (bf16[128,2048]{1,0:T(8,128)(2,1)}, bf16[128,2048]{1,0:T(8,128)(2,1)S(1)}, u32[]{:S(2)}) copy-start(bf16[128,2048]{1,0:T(8,128)(2,1)S(1)} %collective-permute-done.5) | copy-start | bytes 1572868
  64.8 11.7 %collective-permute-start.6 = (bf16[128,2048]{1,0:T(8,128)(2,1)S(1)}, bf16[128,2048]{1,0:T(8,128)(2,1)S(1)}, u32[]{:S(2)}, u32[]{:S(2)}) collective-permute-start(bf16[128,2048]{1,0:T(8,128)(2,1)S(1)} %collective-permute-done.5), channel_id=1, source_target_pairs={{0,4},{4,8},{8,12},{12,14},{14,10},{10,6},{6,2},{2,0},{1,5},{5,9},... | collective-permute-start | bytes 1572872 | tf_op jit(solution)/shard_map/ppermute | solution.py:173
  66.1 10.5 %copy-start.11 = (bf16[128,2048]{1,0:T(8,128)(2,1)}, bf16[128,2048]{1,0:T(8,128)(2,1)S(1)}, u32[]{:S(2)}) copy-start(bf16[128,2048]{1,0:T(8,128)(2,1)S(1)} %collective-permute-done.8) | copy-start | bytes 1572868
  66.1 11.5 %collective-permute-start.9 = (bf16[128,2048]{1,0:T(8,128)(2,1)S(1)}, bf16[128,2048]{1,0:T(8,128)(2,1)S(1)}, u32[]{:S(2)}, u32[]{:S(2)}) collective-permute-start(bf16[128,2048]{1,0:T(8,128)(2,1)S(1)} %collective-permute-done.8), channel_id=1, source_target_pairs={{4,0},{8,4},{12,8},{14,12},{10,14},{6,10},{2,6},{0,2},{5,1},{9,5},... | collective-permute-start | bytes 1572872 | tf_op jit(solution)/shard_map/ppermute | solution.py:174
  77.6 28.2 %all-to-all-start = ((bf16[8,192,256]{2,1,0:T(8,128)(2,1)}), bf16[8,192,256]{2,1,0:T(8,128)(2,1)S(1)}, u32[]{:S(2)}, u32[]{:S(2)}) async-start(bf16[8,192,256]{2,1,0:T(8,128)(2,1)} %pad_maximum_fusion), calls=%async_computation | async-start | bytes 1572864 | tf_op jit(solution)/shard_map/all_to_all | solution.py:182
  86.1 17.6 %collective-permute-start.10 = (bf16[64,2048]{1,0:T(8,128)(2,1)S(1)}, bf16[64,2048]{1,0:T(8,128)(2,1)S(1)}, u32[]{:S(2)}, u32[]{:S(2)}) collective-permute-start(bf16[64,2048]{1,0:T(8,128)(2,1)S(1)} %slice.27), channel_id=1, source_target_pairs={{0,4},{4,8},{8,12},{12,14},{14,10},{10,6},{6,2},{2,0},{1,5},{5,9},... | collective-permute-start | bytes 786440 | tf_op jit(solution)/shard_map/ppermute | solution.py:189
  87.4 17.7 %collective-permute-start.11 = (bf16[64,2048]{1,0:T(8,128)(2,1)S(1)}, bf16[64,2048]{1,0:T(8,128)(2,1)S(1)}, u32[]{:S(2)}, u32[]{:S(2)}) collective-permute-start(bf16[64,2048]{1,0:T(8,128)(2,1)S(1)} %slice.28), channel_id=1, source_target_pairs={{4,0},{8,4},{12,8},{14,12},{10,14},{6,10},{2,6},{0,2},{5,1},{9,5},... | collective-permute-start | bytes 786440 | tf_op jit(solution)/shard_map/ppermute | solution.py:190
  105.8 1.1 copy-start.9
  111.5 5.5 %collective-permute-start.12 = (f32[128,2048]{1,0:T(8,128)}, f32[128,2048]{1,0:T(8,128)}, u32[]{:S(2)}, u32[]{:S(2)}) collective-permute-start(f32[128,2048]{1,0:T(8,128)} %dynamic-slice_bitcast_fusion), channel_id=1, source_target_pairs={{0,1},{1,0},{2,3},{3,2},{4,5},{5,4},{6,7},{7,6},{8,9},{9,8},{10,11... | collective-permute-start | bytes 3145736 | tf_op jit(solution)/shard_map/ppermute | solution.py:20

commit v3 on v2

--- a/solution.py
+++ b/solution.py
@@ -178,7 +178,7 @@
     rel_own = rel_own.transpose(0, 2, 1, 3).reshape(chips, owned * chips, cols)
     left = columns(jnp.where(first, query_back, mixed))
     sent = jnp.concatenate([left, rel_own], axis=1)
-    sent, _ = lax.optimization_barrier((sent, (blocks[-2][0], blocks[-1][0])))
+    sent, _ = lax.optimization_barrier((sent, (blocks[3][0], blocks[4][0])))
     received = lax.all_to_all(sent, "chip", 0, 0, tiled=True)
     left_cols, rel_rows = received[:, :rows_dev], received[:, rows_dev:]
     rel_sum = jnp.sum(rel_rows.astype(F32), axis=0) * jnp.sqrt(F32(count_rel) / F32(total_rows))

time: 122 us -> 116 us (0.951); the launches traced: 119 us -> 115 us
  waiting for transfers between devices: 42.8 us -> 38.1 us
    ppermute x3, waiting for transfers between devices: 15.7 us -> 8.18 us  [local(): fwd = lax.ppermute(fwd, 'chip', up)]
    ppermute x1, waiting for transfers between devices: 14.3 us -> 18.1 us  [local(): blocks.append((lax.ppermute(fwd[:mid], 'chip', up), chips // 2, 0))]
    unnamed x28 -> x22, local copies, waits for them, and re-layouts: 11.3 us -> 10.6 us
  transfers between devices with their start and end apart: 14 -> 14, of which waited for: 10 -> 8; matrix products, arithmetic and copies ran while one was open for 20% -> 21% of each run, Pallas kernels for 0% -> 0%
where the time goes in v3:
time: 116 us; the launch traced here: 115 us
  waiting for transfers between devices  38.1 us (33%)
  local copies, waits for them, and re-layouts  30 us (26%)
  starting transfers between devices  21.7 us (19%)
  Pallas kernels  11.6 us (10%)
  other arithmetic  8.29 us (7%)
  matrix products  3.95 us (3%)
    ppermute x1, waiting for transfers between devices, local(): blocks.append((lax.ppermute(fwd[:mid], 'chip', up), chips // 2, 0))  18.1 us
    dynamic_update_slice x9, local copies, waits for them, and re-layouts, local(): right_all = lax.dynamic_update_slice_in_dim(right_all, block, start, 0)  12.5 us
    unnamed x22, local copies, waits for them, and re-layouts  10.6 us
    pallas_call x1, Pallas kernels, trail(): pl.pallas_call(trail_body, out_shape=(jax.ShapeDtypeStruct((rows_dev, hid...  8.76 us
    ppermute x3, waiting for transfers between devices, local(): fwd = lax.ppermute(fwd, 'chip', up)  8.18 us
    ppermute x1, waiting for transfers between devices, local(): query = lax.ppermute(own_query, 'hop', [(0, 1)])  7.79 us
    all_to_all x1, starting transfers between devices, local(): received = lax.all_to_all(sent, 'chip', 0, 0, tiled=True)  5.61 us
    ppermute x2, starting transfers between devices, swap_core(): return lax.ppermute(block, 'core', [(0, 1), (1, 0)])  4.41 us
  transfers between devices with their start and end apart: 14, of which 8 were waited for; matrix products, arithmetic and copies ran while one was open for 21% of the time, Pallas kernels for 0%

profile of v3, /device:TPU:9, one launch (start us, length us, event | category | flops | bytes accessed | tf_op | source)
XLA Modules:
  0.0 114.7 jit_solution(4357182748050018945)
XLA Ops:
  0.7 3.5 %copy-done.1 = bf16[1,2048,2048]{2,1,0:T(8,128)(2,1)S(1)} copy-done((bf16[1,2048,2048]{2,1,0:T(8,128)(2,1)S(1)}, bf16[1,2048,2048]{2,1,0:T(8,128)(2,1)}, u32[]{:S(2)}) %copy-start.1) | copy-done | bytes 8388632
  4.1 1.0 copy-done.3
  5.2 2.9 %shard_map.67 = bf16[2,128,1024]{2,1,0:T(8,128)(2,1)S(1)} custom-call(bf16[128,2048]{1,0:T(8,128)(2,1)S(1)} %bitcast.52, bf16[2048,2048]{1,0:T(8,128)(2,1)S(1)} %bitcast.50), custom_call_target="tpu_custom_call" | custom-call | flops 1073741824 | bytes 8388608 | tf_op jit(solution)/shard_map/pallas_call | solution.py:43
  8.1 3.2 %collective-permute-start = (bf16[2,128,1024]{2,1,0:T(8,128)(2,1)S(1)}, bf16[2,128,1024]{2,1,0:T(8,128)(2,1)S(1)}, u32[]{:S(2)}, u32[]{:S(2)}) collective-permute-start(bf16[2,128,1024]{2,1,0:T(8,128)(2,1)S(1)} %shard_map.67), channel_id=1, source_target_pairs={{0,16},{1,17},{2,18},{3,19},{4,20},{5,21},{6,22},{7,23},{8,24},{9,... | collective-permute-start | bytes 1572872 | tf_op jit(solution)/shard_map/ppermute | solution.py:151
  11.2 0.3 convolution_convert_fusion
  11.6 1.0 copy.9
  12.6 1.2 %copy.10 = bf16[128,2,1024]{2,0,1:T(8,128)(2,1)S(1)} copy(bf16[128,2,1024]{0,2,1:T(8,128)(2,1)} %bitcast.58) | data formatting | bytes 1048576 | tf_op jit(solution)/shard_map/reshape | solution.py:153
  14.0 7.8 %collective-permute-done.query = bf16[2,128,1024]{2,1,0:T(8,128)(2,1)S(1)} collective-permute-done((bf16[2,128,1024]{2,1,0:T(8,128)(2,1)S(1)}, bf16[2,128,1024]{2,1,0:T(8,128)(2,1)S(1)}, u32[]{:S(2)}, u32[]{:S(2)}) %collective-permute-start) | collective-permute-done | bytes 524320 | tf_op jit(solution)/shard_map/ppermute | solution.py:151
  21.8 0.8 copy-done.5
  22.6 3.4 %copy-done.2 = bf16[1,2048,2048]{2,1,0:T(8,128)(2,1)S(1)} copy-done((bf16[1,2048,2048]{2,1,0:T(8,128)(2,1)S(1)}, bf16[1,2048,2048]{2,1,0:T(8,128)(2,1)}, u32[]{:S(2)}) %copy-start.2) | copy-done | bytes 8388632
  26.0 1.0 copy-done.6
  27.0 8.8 %shard_map.68 = (bf16[128,2048]{1,0:T(8,128)(2,1)}, bf16[128,2048]{1,0:T(8,128)(2,1)}, f32[128,2048]{1,0:T(8,128)}, f32[128,2048]{1,0:T(8,128)S(1)}, bf16[128,2048]{1,0:T(8,128)(2,1)S(1)}) custom-call(s32[1]{0:T(128)} %bitcast.first, bf16[2,128,1024]{2,1,0:T(8,128)(2,1)S(1)} %copy-done.6, bf16[128,2048]{1,0:T(8,128)(2,1)S(1)} %bitcast.53, ...), custom_call_target="tpu_custom_call" | custom-call | flops 2415919104 | bytes 16777216 | tf_op jit(solution)/shard_map/pallas_call | solution.py:105
  35.8 0.8 copy-done.7
  36.6 1.5 %collective-permute-start.2 = (f32[128,2048]{1,0:T(8,128)}, f32[128,2048]{1,0:T(8,128)}, u32[]{:S(2)}, u32[]{:S(2)}) collective-permute-start(f32[128,2048]{1,0:T(8,128)} %get-tuple-element.12), channel_id=1, source_target_pairs={{0,1},{1,0},{2,3},{3,2},{4,5},{5,4},{6,7},{7,6},{8,9},{9,8},{10,11... | collective-permute-start | bytes 3145736 | tf_op jit(solution)/shard_map/ppermute | solution.py:20
  38.1 1.3 %collective-permute-start.4 = (bf16[128,2048]{1,0:T(8,128)(2,1)}, bf16[128,2048]{1,0:T(8,128)(2,1)}, u32[]{:S(2)}, u32[]{:S(2)}) collective-permute-start(bf16[128,2048]{1,0:T(8,128)(2,1)} %get-tuple-element.13), channel_id=1, source_target_pairs={{0,4},{4,8},{8,12},{12,14},{14,10},{10,6},{6,2},{2,0},{1,5},{5,9},... | collective-permute-start | bytes 1572872 | tf_op jit(solution)/shard_map/ppermute | solution.py:173
  39.6 1.3 %collective-permute-start.1 = (bf16[128,2048]{1,0:T(8,128)(2,1)}, bf16[128,2048]{1,0:T(8,128)(2,1)}, u32[]{:S(2)}, u32[]{:S(2)}) collective-permute-start(bf16[128,2048]{1,0:T(8,128)(2,1)} %get-tuple-element.9), channel_id=1, source_target_pairs={{16,0},{17,1},{18,2},{19,3},{20,4},{21,5},{22,6},{23,7},{24,8},{25... | collective-permute-start | bytes 1572872 | tf_op jit(solution)/shard_map/ppermute | solution.py:157
  41.1 2.5 %broadcast_in_dim.20 = bf16[1024,2048]{1,0:T(8,128)(2,1)} broadcast(bf16[]{:T(256)} %constant.145.clone.1), dimensions={} | broadcast | bytes 4194306 | tf_op jit(solution)/shard_map/broadcast_in_dim | solution.py:191
  43.5 1.9 %constant_dynamic-update-slice_fusion.8 = bf16[1024,2048]{1,0:T(8,128)(2,1)} fusion(bf16[1024,2048]{1,0:T(8,128)(2,1)} %broadcast_in_dim.20, bf16[128,2048]{1,0:T(8,128)(2,1)} %get-tuple-element.13, s32[]{:T(128)S(6)} %select_n.159), kind=kLoop, calls=%fused_computation.28 | loop fusion | bytes 1048580 | tf_op jit(solution)/shard_map/dynamic_update_slice | solution.py:194
  45.4 6.6 %collective-permute-done.4 = bf16[128,2048]{1,0:T(8,128)(2,1)} collective-permute-done((bf16[128,2048]{1,0:T(8,128)(2,1)}, bf16[128,2048]{1,0:T(8,128)(2,1)}, u32[]{:S(2)}, u32[]{:S(2)}) %collective-permute-start.4) | collective-permute-done | bytes 524320 | tf_op jit(solution)/shard_map/ppermute | solution.py:173
  52.0 1.3 %collective-permute-start.5 = (bf16[128,2048]{1,0:T(8,128)(2,1)}, bf16[128,2048]{1,0:T(8,128)(2,1)}, u32[]{:S(2)}, u32[]{:S(2)}) collective-permute-start(bf16[128,2048]{1,0:T(8,128)(2,1)} %collective-permute-done.4), channel_id=1, source_target_pairs={{0,4},{4,8},{8,12},{12,14},{14,10},{10,6},{6,2},{2,0},{1,5},{5,9},... | collective-permute-start | bytes 1572872 | tf_op jit(solution)/shard_map/ppermute | solution.py:173
  53.5 1.5 %collective-permute-done.1 = bf16[128,2048]{1,0:T(8,128)(2,1)} collective-permute-done((bf16[128,2048]{1,0:T(8,128)(2,1)}, bf16[128,2048]{1,0:T(8,128)(2,1)}, u32[]{:S(2)}, u32[]{:S(2)}) %collective-permute-start.1) | collective-permute-done | bytes 524320 | tf_op jit(solution)/shard_map/ppermute | solution.py:157
  55.0 1.9 %broadcast_select_fusion = (bf16[128,2048]{1,0:T(8,128)(2,1)}, bf16[128,2048]{1,0:T(8,128)(2,1)S(1)}) fusion(bf16[128,2048]{1,0:T(8,128)(2,1)} %collective-permute-done.1, bf16[128,2048]{1,0:T(8,128)(2,1)} %get-tuple-element.9, pred[]{:T(512)S(6)} %eq.44, bf16[128,2048]{1,0:T(8,128)(2,1)S(1)} %copy-done.8), kind=kLoop, calls=%fused_computation.11 | loop fusion | flops 524288 | bytes 2621441 | tf_op jit(solution)/shard_map/jit(_where)/select_n | solution.py:158
  56.9 1.3 %add_convert_fusion = bf16[128,2048]{1,0:T(8,128)(2,1)S(1)} fusion(f32[128,2048]{1,0:T(8,128)S(1)} %get-tuple-element.11, f32[128,2048]{1,0:T(8,128)} %collective-permute-done.2), kind=kLoop, calls=%fused_computation.7 | loop fusion | flops 524288 | bytes 2621440 | tf_op jit(solution)/shard_map/convert_element_type | solution.py:159
  58.3 1.3 %collective-permute-start.3 = (bf16[8,8,2048]{2,1,0:T(8,128)(2,1)S(1)}, bf16[8,8,2048]{2,1,0:T(8,128)(2,1)S(1)}, u32[]{:S(2)}, u32[]{:S(2)}) collective-permute-start(bf16[8,8,2048]{2,1,0:T(8,128)(2,1)S(1)} %slice_bitcast_fusion.1), channel_id=1, source_target_pairs={{16,0},{17,1},{18,2},{19,3},{20,4},{21,5},{22,6},{23,7},{24,8},{25... | collective-permute-start | bytes 786440 | tf_op jit(solution)/shard_map/ppermute | solution.py:160
  59.6 1.9 %constant_dynamic-update-slice_fusion.7 = bf16[1024,2048]{1,0:T(8,128)(2,1)} fusion(bf16[1024,2048]{1,0:T(8,128)(2,1)} %constant_dynamic-update-slice_fusion.8, bf16[128,2048]{1,0:T(8,128)(2,1)} %collective-permute-done.4, s32[]{:T(128)S(6)} %select_n.161), kind=kLoop, calls=%fused_computation.27 | loop fusion | bytes 1048580 | tf_op jit(solution)/shard_map/dynamic_update_slice | solution.py:194
  61.5 1.9 %constant_dynamic-update-slice_fusion.6 = bf16[1024,2048]{1,0:T(8,128)(2,1)} fusion(bf16[1024,2048]{1,0:T(8,128)(2,1)} %constant_dynamic-update-slice_fusion.7, bf16[128,2048]{1,0:T(8,128)(2,1)} %collective-permute-done.6, s32[]{:T(128)S(6)} %select_n.163), kind=kLoop, calls=%fused_computation.26 | loop fusion | bytes 1048580 | tf_op jit(solution)/shard_map/dynamic_update_slice | solution.py:194
  63.4 1.6 %collective-permute-done.5 = bf16[128,2048]{1,0:T(8,128)(2,1)} collective-permute-done((bf16[128,2048]{1,0:T(8,128)(2,1)}, bf16[128,2048]{1,0:T(8,128)(2,1)}, u32[]{:S(2)}, u32[]{:S(2)}) %collective-permute-start.5) | collective-permute-done | bytes 524320 | tf_op jit(solution)/shard_map/ppermute | solution.py:173
  65.0 1.3 %collective-permute-start.8 = (bf16[128,2048]{1,0:T(8,128)(2,1)}, bf16[128,2048]{1,0:T(8,128)(2,1)S(1)}, u32[]{:S(2)}, u32[]{:S(2)}) collective-permute-start(bf16[128,2048]{1,0:T(8,128)(2,1)} %collective-permute-done.5), channel_id=1, source_target_pairs={{0,4},{4,8},{8,12},{12,14},{14,10},{10,6},{6,2},{2,0},{1,5},{5,9},... | collective-permute-start | bytes 1572872 | tf_op jit(solution)/shard_map/ppermute | solution.py:173
  66.5 0.3 collective-permute-done.3
  66.8 0.9 pad_maximum_fusion
  67.8 5.6 %all-to-all-start = ((bf16[8,192,256]{2,1,0:T(8,128)(2,1)}), bf16[8,192,256]{2,1,0:T(8,128)(2,1)S(1)}, u32[]{:S(2)}, u32[]{:S(2)}) async-start(bf16[8,192,256]{2,1,0:T(8,128)(2,1)} %pad_maximum_fusion), calls=%async_computation | async-start | bytes 1572864 | tf_op jit(solution)/shard_map/all_to_all | solution.py:182
  73.4 1.9 %constant_dynamic-update-slice_fusion.5 = bf16[1024,2048]{1,0:T(8,128)(2,1)} fusion(bf16[1024,2048]{1,0:T(8,128)(2,1)} %constant_dynamic-update-slice_fusion.6, bf16[128,2048]{1,0:T(8,128)(2,1)} %collective-permute-done.5, s32[]{:T(128)S(6)} %select_n.165), kind=kLoop, calls=%fused_computation.25 | loop fusion | bytes 1048580 | tf_op jit(solution)/shard_map/dynamic_update_slice | solution.py:194
  75.3 1.9 %constant_dynamic-update-slice_fusion.4 = bf16[1024,2048]{1,0:T(8,128)(2,1)} fusion(bf16[1024,2048]{1,0:T(8,128)(2,1)} %constant_dynamic-update-slice_fusion.5, bf16[128,2048]{1,0:T(8,128)(2,1)} %collective-permute-done.7, s32[]{:T(128)S(6)} %select_n.167), kind=kLoop, calls=%fused_computation.24 | loop fusion | bytes 1048580 | tf_op jit(solution)/shard_map/dynamic_update_slice | solution.py:194
  77.2 1.2 %collective-permute-start.10 = (bf16[64,2048]{1,0:T(8,128)(2,1)S(1)}, bf16[64,2048]{1,0:T(8,128)(2,1)S(1)}, u32[]{:S(2)}, u32[]{:S(2)}) collective-permute-start(bf16[64,2048]{1,0:T(8,128)(2,1)S(1)} %slice.27), channel_id=1, source_target_pairs={{0,4},{4,8},{8,12},{12,14},{14,10},{10,6},{6,2},{2,0},{1,5},{5,9},... | collective-permute-start | bytes 786440 | tf_op jit(solution)/shard_map/ppermute | solution.py:189
  78.8 0.8 constant_dynamic-update-slice_fusion.3
  79.6 0.8 constant_dynamic-update-slice_fusion.2
  80.4 18.1 %collective-permute-done.10 = bf16[64,2048]{1,0:T(8,128)(2,1)S(1)} collective-permute-done((bf16[64,2048]{1,0:T(8,128)(2,1)S(1)}, bf16[64,2048]{1,0:T(8,128)(2,1)S(1)}, u32[]{:S(2)}, u32[]{:S(2)}) %collective-permute-start.10) | collective-permute-done | bytes 262176 | tf_op jit(solution)/shard_map/ppermute | solution.py:189
  98.5 0.7 constant_dynamic-update-slice_fusion.1
  99.2 1.2 %collective-permute-done.11 = bf16[64,2048]{1,0:T(8,128)(2,1)S(1)} collective-permute-done((bf16[64,2048]{1,0:T(8,128)(2,1)S(1)}, bf16[64,2048]{1,0:T(8,128)(2,1)S(1)}, u32[]{:S(2)}, u32[]{:S(2)}) %collective-permute-start.11) | collective-permute-done | bytes 262176 | tf_op jit(solution)/shard_map/ppermute | solution.py:190
  100.4 0.7 constant_dynamic-update-slice_fusion
  101.2 1.0 copy.13
  102.2 3.6 %fusion = f32[2,128,2048]{2,1,0:T(8,128)S(1)} fusion(bf16[2,128,1024]{2,1,0:T(8,128)(2,1)} %bitcast.61, bf16[1024,2048]{1,0:T(8,128)(2,1)} %constant_dynamic-update-slice_fusion), kind=kOutput, calls=%fused_computation | convolution fusion | flops 1073741824 | bytes 6815744 | tf_op jit(solution)/shard_map/dot_general | solution.py:16
  105.8 1.1 dynamic-slice_bitcast_fusion
  106.9 2.9 %collective-permute-start.12 = (f32[128,2048]{1,0:T(8,128)}, f32[128,2048]{1,0:T(8,128)}, u32[]{:S(2)}, u32[]{:S(2)}) collective-permute-start(f32[128,2048]{1,0:T(8,128)} %dynamic-slice_bitcast_fusion), channel_id=1, source_target_pairs={{0,1},{1,0},{2,3},{3,2},{4,5},{5,4},{6,7},{7,6},{8,9},{9,8},{10,11... | collective-permute-start | bytes 3145736 | tf_op jit(solution)/shard_map/ppermute | solution.py:20
  109.8 1.0 convert_reduce_fusion
  110.7 0.6 broadcast_multiply_fusion
  111.4 1.0 collective-permute-done.12
  112.4 2.3 %fusion.3 = f32[1,128,2048]{2,1,0:T(8,128)} fusion(f32[128,2048]{1,0:T(8,128)} %collective-permute-done.12, f32[2,128,2048]{2,1,0:T(8,128)S(1)} %fusion, s32[]{:T(128)S(6)} %select_n.175), kind=kLoop, calls=%fused_computation.5 | loop fusion | flops 524288 | bytes 3145732 | tf_op jit(solution)/shard_map/broadcast_in_dim | solution.py:200
  (34 shorter events, 1.2 us)
Async XLA Ops:
  0.6 10.6 %copy-start = (bf16[256,2048]{1,0:T(8,128)(2,1)S(1)}, bf16[256,2048]{1,0:T(8,128)(2,1)}, u32[]{:S(2)}) copy-start(bf16[256,2048]{1,0:T(8,128)(2,1)} %param.6) | copy-start | bytes 3145732
  0.6 3.5 %copy-start.1 = (bf16[1,2048,2048]{2,1,0:T(8,128)(2,1)S(1)}, bf16[1,2048,2048]{2,1,0:T(8,128)(2,1)}, u32[]{:S(2)}) copy-start(bf16[1,2048,2048]{2,1,0:T(8,128)(2,1)} %param.5) | copy-start | bytes 25165828
  4.1 1.0 copy-start.3
  5.2 6.1 %copy-start.10 = (s32[128]{0:T(128)S(1)}, s32[128]{0:T(128)}, u32[]{:S(2)}) copy-start(s32[128]{0:T(128)} %param.7) | copy-start | bytes 1540
  5.2 17.4 %copy-start.4 = (bf16[1,128,2048]{2,1,0:T(8,128)(2,1)S(1)}, bf16[1,128,2048]{2,1,0:T(8,128)(2,1)}, u32[]{:S(2)}) copy-start(bf16[1,128,2048]{2,1,0:T(8,128)(2,1)} %param.4) | copy-start | bytes 1572868
  8.1 13.7 %collective-permute-start = (bf16[2,128,1024]{2,1,0:T(8,128)(2,1)S(1)}, bf16[2,128,1024]{2,1,0:T(8,128)(2,1)S(1)}, u32[]{:S(2)}, u32[]{:S(2)}) collective-permute-start(bf16[2,128,1024]{2,1,0:T(8,128)(2,1)S(1)} %shard_map.67), channel_id=1, source_target_pairs={{0,16},{1,17},{2,18},{3,19},{4,20},{5,21},{6,22},{7,23},{8,24},{9,... | collective-permute-start | bytes 1572872 | tf_op jit(solution)/shard_map/ppermute | solution.py:151
  21.8 0.8 copy-start.5
  22.6 3.4 %copy-start.2 = (bf16[1,2048,2048]{2,1,0:T(8,128)(2,1)S(1)}, bf16[1,2048,2048]{2,1,0:T(8,128)(2,1)}, u32[]{:S(2)}) copy-start(bf16[1,2048,2048]{2,1,0:T(8,128)(2,1)} %param.5) | copy-start | bytes 25165828
  25.9 1.0 copy-start.6
  35.8 0.9 copy-start.7
  36.6 18.4 %copy-start.8 = (bf16[128,2048]{1,0:T(8,128)(2,1)S(1)}, bf16[128,2048]{1,0:T(8,128)(2,1)}, u32[]{:S(2)}) copy-start(bf16[128,2048]{1,0:T(8,128)(2,1)} %copy-done.7) | copy-start | bytes 1572868
  36.6 20.3 %collective-permute-start.2 = (f32[128,2048]{1,0:T(8,128)}, f32[128,2048]{1,0:T(8,128)}, u32[]{:S(2)}, u32[]{:S(2)}) collective-permute-start(f32[128,2048]{1,0:T(8,128)} %get-tuple-element.12), channel_id=1, source_target_pairs={{0,1},{1,0},{2,3},{3,2},{4,5},{5,4},{6,7},{7,6},{8,9},{9,8},{10,11... | collective-permute-start | bytes 3145736 | tf_op jit(solution)/shard_map/ppermute | solution.py:20
  38.1 13.9 %collective-permute-start.4 = (bf16[128,2048]{1,0:T(8,128)(2,1)}, bf16[128,2048]{1,0:T(8,128)(2,1)}, u32[]{:S(2)}, u32[]{:S(2)}) collective-permute-start(bf16[128,2048]{1,0:T(8,128)(2,1)} %get-tuple-element.13), channel_id=1, source_target_pairs={{0,4},{4,8},{8,12},{12,14},{14,10},{10,6},{6,2},{2,0},{1,5},{5,9},... | collective-permute-start | bytes 1572872 | tf_op jit(solution)/shard_map/ppermute | solution.py:173
  39.4 13.9 %collective-permute-start.6 = (bf16[128,2048]{1,0:T(8,128)(2,1)}, bf16[128,2048]{1,0:T(8,128)(2,1)}, u32[]{:S(2)}, u32[]{:S(2)}) collective-permute-start(bf16[128,2048]{1,0:T(8,128)(2,1)} %get-tuple-element.13), channel_id=1, source_target_pairs={{4,0},{8,4},{12,8},{14,12},{10,14},{6,10},{2,6},{0,2},{5,1},{9,5},... | collective-permute-start | bytes 1572872 | tf_op jit(solution)/shard_map/ppermute | solution.py:174
  39.6 15.4 %collective-permute-start.1 = (bf16[128,2048]{1,0:T(8,128)(2,1)}, bf16[128,2048]{1,0:T(8,128)(2,1)}, u32[]{:S(2)}, u32[]{:S(2)}) collective-permute-start(bf16[128,2048]{1,0:T(8,128)(2,1)} %get-tuple-element.9), channel_id=1, source_target_pairs={{16,0},{17,1},{18,2},{19,3},{20,4},{21,5},{22,6},{23,7},{24,8},{25... | collective-permute-start | bytes 1572872 | tf_op jit(solution)/shard_map/ppermute | solution.py:157
  52.0 13.0 %collective-permute-start.5 = (bf16[128,2048]{1,0:T(8,128)(2,1)}, bf16[128,2048]{1,0:T(8,128)(2,1)}, u32[]{:S(2)}, u32[]{:S(2)}) collective-permute-start(bf16[128,2048]{1,0:T(8,128)(2,1)} %collective-permute-done.4), channel_id=1, source_target_pairs={{0,4},{4,8},{8,12},{12,14},{14,10},{10,6},{6,2},{2,0},{1,5},{5,9},... | collective-permute-start | bytes 1572872 | tf_op jit(solution)/shard_map/ppermute | solution.py:173
  53.3 13.0 %collective-permute-start.7 = (bf16[128,2048]{1,0:T(8,128)(2,1)}, bf16[128,2048]{1,0:T(8,128)(2,1)}, u32[]{:S(2)}, u32[]{:S(2)}) collective-permute-start(bf16[128,2048]{1,0:T(8,128)(2,1)} %collective-permute-done.6), channel_id=1, source_target_pairs={{4,0},{8,4},{12,8},{14,12},{10,14},{6,10},{2,6},{0,2},{5,1},{9,5},... | collective-permute-start | bytes 1572872 | tf_op jit(solution)/shard_map/ppermute | solution.py:174
  58.3 8.5 %collective-permute-start.3 = (bf16[8,8,2048]{2,1,0:T(8,128)(2,1)S(1)}, bf16[8,8,2048]{2,1,0:T(8,128)(2,1)S(1)}, u32[]{:S(2)}, u32[]{:S(2)}) collective-permute-start(bf16[8,8,2048]{2,1,0:T(8,128)(2,1)S(1)} %slice_bitcast_fusion.1), channel_id=1, source_target_pairs={{16,0},{17,1},{18,2},{19,3},{20,4},{21,5},{22,6},{23,7},{24,8},{25... | collective-permute-start | bytes 786440 | tf_op jit(solution)/shard_map/ppermute | solution.py:160
  65.0 12.1 %collective-permute-start.8 = (bf16[128,2048]{1,0:T(8,128)(2,1)}, bf16[128,2048]{1,0:T(8,128)(2,1)S(1)}, u32[]{:S(2)}, u32[]{:S(2)}) collective-permute-start(bf16[128,2048]{1,0:T(8,128)(2,1)} %collective-permute-done.5), channel_id=1, source_target_pairs={{0,4},{4,8},{8,12},{12,14},{14,10},{10,6},{6,2},{2,0},{1,5},{5,9},... | collective-permute-start | bytes 1572872 | tf_op jit(solution)/shard_map/ppermute | solution.py:173
  66.3 12.1 %collective-permute-start.9 = (bf16[128,2048]{1,0:T(8,128)(2,1)}, bf16[128,2048]{1,0:T(8,128)(2,1)S(1)}, u32[]{:S(2)}, u32[]{:S(2)}) collective-permute-start(bf16[128,2048]{1,0:T(8,128)(2,1)} %collective-permute-done.7), channel_id=1, source_target_pairs={{4,0},{8,4},{12,8},{14,12},{10,14},{6,10},{2,6},{0,2},{5,1},{9,5},... | collective-permute-start | bytes 1572872 | tf_op jit(solution)/shard_map/ppermute | solution.py:174
  67.8 33.4 %all-to-all-start = ((bf16[8,192,256]{2,1,0:T(8,128)(2,1)}), bf16[8,192,256]{2,1,0:T(8,128)(2,1)S(1)}, u32[]{:S(2)}, u32[]{:S(2)}) async-start(bf16[8,192,256]{2,1,0:T(8,128)(2,1)} %pad_maximum_fusion), calls=%async_computation | async-start | bytes 1572864 | tf_op jit(solution)/shard_map/all_to_all | solution.py:182
  77.2 21.3 %collective-permute-start.10 = (bf16[64,2048]{1,0:T(8,128)(2,1)S(1)}, bf16[64,2048]{1,0:T(8,128)(2,1)S(1)}, u32[]{:S(2)}, u32[]{:S(2)}) collective-permute-start(bf16[64,2048]{1,0:T(8,128)(2,1)S(1)} %slice.27), channel_id=1, source_target_pairs={{0,4},{4,8},{8,12},{12,14},{14,10},{10,6},{6,2},{2,0},{1,5},{5,9},... | collective-permute-start | bytes 786440 | tf_op jit(solution)/shard_map/ppermute | solution.py:189
  78.4 22.0 %collective-permute-start.11 = (bf16[64,2048]{1,0:T(8,128)(2,1)S(1)}, bf16[64,2048]{1,0:T(8,128)(2,1)S(1)}, u32[]{:S(2)}, u32[]{:S(2)}) collective-permute-start(bf16[64,2048]{1,0:T(8,128)(2,1)S(1)} %slice.28), channel_id=1, source_target_pairs={{4,0},{8,4},{12,8},{14,12},{10,14},{6,10},{2,6},{0,2},{5,1},{9,5},... | collective-permute-start | bytes 786440 | tf_op jit(solution)/shard_map/ppermute | solution.py:190
  101.2 1.1 copy-start.9
  106.9 5.5 %collective-permute-start.12 = (f32[128,2048]{1,0:T(8,128)}, f32[128,2048]{1,0:T(8,128)}, u32[]{:S(2)}, u32[]{:S(2)}) collective-permute-start(f32[128,2048]{1,0:T(8,128)} %dynamic-slice_bitcast_fusion), channel_id=1, source_target_pairs={{0,1},{1,0},{2,3},{3,2},{4,5},{5,4},{6,7},{7,6},{8,9},{9,8},{10,11... | collective-permute-start | bytes 3145736 | tf_op jit(solution)/shard_map/ppermute | solution.py:20

commit v4 on v3

--- a/solution.py
+++ b/solution.py
@@ -192,11 +192,11 @@
     for block, step, base in blocks:
         start = chip_at(place + step) * rows_dev + base
         right_all = lax.dynamic_update_slice_in_dim(right_all, block, start, 0)
-    partial = dot(left_cols.reshape(chips * rows_dev, cols), right_all, 0, 0)
-    partial = partial.reshape(2, cols // 2, width)
-    keep = lax.dynamic_index_in_dim(partial, core, 0, keepdims=False)
-    give = lax.dynamic_index_in_dim(partial, 1 - core, 0, keepdims=False)
-    weight_grad = (keep + swap_core(give)) * (1.0 / jnp.sqrt(F32(total_rows)))
+    lower, upper = left_cols[..., :cols // 2], left_cols[..., cols // 2:]
+    give = jnp.where(core == 0, upper, lower).reshape(chips * rows_dev, cols // 2)
+    keep = jnp.where(core == 0, lower, upper).reshape(chips * rows_dev, cols // 2)
+    got = swap_core(dot(give, right_all, 0, 0))
+    weight_grad = (dot(keep, right_all, 0, 0) + got) * (1.0 / jnp.sqrt(F32(total_rows)))
     return weight_grad[None], relation_grad, query_grad
 
 

time: 116 us -> 115 us (level)
  other arithmetic: 8.29 us -> 5.05 us
  matrix products: 3.95 us -> 7.17 us
  local copies, waits for them, and re-layouts: 30 us -> 28.8 us
    dot_general x2 -> x3, matrix products: 3.95 us -> 7.17 us  [dot(): lax.dot_general(a, b, (((ca,), (cb,)), ((), ())), preferred_element_type=...]
    broadcast_in_dim x1 -> x0, other arithmetic: 2.32 us -> none  [local(): return (weight_grad[None], relation_grad, query_grad)]
    ppermute x1, waiting for transfers between devices: 18.1 us -> 16.1 us  [local(): blocks.append((lax.ppermute(fwd[:mid], 'chip', up), chips // 2, 0))]
    unnamed x22 -> x20, local copies, waits for them, and re-layouts: 10.6 us -> 10.5 us
where the time goes in v4:
time: 115 us; the launch traced here: 113 us
  waiting for transfers between devices  37.8 us (33%)
  local copies, waits for them, and re-layouts  28.8 us (25%)
  starting transfers between devices  21.7 us (19%)
  Pallas kernels  11.6 us (10%)
  matrix products  7.17 us (6%)
  other arithmetic  5.05 us (4%)
    ppermute x1, waiting for transfers between devices, local(): blocks.append((lax.ppermute(fwd[:mid], 'chip', up), chips // 2, 0))  16.1 us
    dynamic_update_slice x9, local copies, waits for them, and re-layouts, local(): right_all = lax.dynamic_update_slice_in_dim(right_all, block, start, 0)  12.5 us
    unnamed x20, local copies, waits for them, and re-layouts  10.5 us
    ppermute x3, waiting for transfers between devices, local(): fwd = lax.ppermute(fwd, 'chip', up)  9.13 us
    pallas_call x1, Pallas kernels, trail(): pl.pallas_call(trail_body, out_shape=(jax.ShapeDtypeStruct((rows_dev, hid...  8.75 us
    ppermute x1, waiting for transfers between devices, local(): query = lax.ppermute(own_query, 'hop', [(0, 1)])  7.79 us
    dot_general x3, matrix products, dot(): lax.dot_general(a, b, (((ca,), (cb,)), ((), ())), preferred_element_type=...  7.17 us
    all_to_all x1, starting transfers between devices, local(): received = lax.all_to_all(sent, 'chip', 0, 0, tiled=True)  5.61 us
  transfers between devices with their start and end apart: 14, of which 8 were waited for; matrix products, arithmetic and copies ran while one was open for 21% of the time, Pallas kernels for 0%

profile of v4, /device:TPU:9, one launch (start us, length us, event | category | flops | bytes accessed | tf_op | source)
XLA Modules:
  0.0 113.1 jit_solution(13986629464258147641)
XLA Ops:
  0.7 3.5 %copy-done.1 = bf16[1,2048,2048]{2,1,0:T(8,128)(2,1)S(1)} copy-done((bf16[1,2048,2048]{2,1,0:T(8,128)(2,1)S(1)}, bf16[1,2048,2048]{2,1,0:T(8,128)(2,1)}, u32[]{:S(2)}) %copy-start.1) | copy-done | bytes 8388632
  4.1 1.0 copy-done.3
  5.2 2.9 %shard_map.67 = bf16[2,128,1024]{2,1,0:T(8,128)(2,1)S(1)} custom-call(bf16[128,2048]{1,0:T(8,128)(2,1)S(1)} %bitcast.42, bf16[2048,2048]{1,0:T(8,128)(2,1)S(1)} %bitcast.40), custom_call_target="tpu_custom_call" | custom-call | flops 1073741824 | bytes 8388608 | tf_op jit(solution)/shard_map/pallas_call | solution.py:43
  8.1 3.2 %collective-permute-start = (bf16[2,128,1024]{2,1,0:T(8,128)(2,1)S(1)}, bf16[2,128,1024]{2,1,0:T(8,128)(2,1)S(1)}, u32[]{:S(2)}, u32[]{:S(2)}) collective-permute-start(bf16[2,128,1024]{2,1,0:T(8,128)(2,1)S(1)} %shard_map.67), channel_id=1, source_target_pairs={{0,16},{1,17},{2,18},{3,19},{4,20},{5,21},{6,22},{7,23},{8,24},{9,... | collective-permute-start | bytes 1572872 | tf_op jit(solution)/shard_map/ppermute | solution.py:151
  11.2 0.3 convolution_convert_fusion
  11.6 1.0 copy.9
  12.6 1.2 %copy.10 = bf16[128,2,1024]{2,0,1:T(8,128)(2,1)S(1)} copy(bf16[128,2,1024]{0,2,1:T(8,128)(2,1)} %bitcast.48) | data formatting | bytes 1048576 | tf_op jit(solution)/shard_map/reshape | solution.py:153
  14.0 7.8 %collective-permute-done.query = bf16[2,128,1024]{2,1,0:T(8,128)(2,1)S(1)} collective-permute-done((bf16[2,128,1024]{2,1,0:T(8,128)(2,1)S(1)}, bf16[2,128,1024]{2,1,0:T(8,128)(2,1)S(1)}, u32[]{:S(2)}, u32[]{:S(2)}) %collective-permute-start) | collective-permute-done | bytes 524320 | tf_op jit(solution)/shard_map/ppermute | solution.py:151
  21.8 0.8 copy-done.5
  22.6 3.4 %copy-done.2 = bf16[1,2048,2048]{2,1,0:T(8,128)(2,1)S(1)} copy-done((bf16[1,2048,2048]{2,1,0:T(8,128)(2,1)S(1)}, bf16[1,2048,2048]{2,1,0:T(8,128)(2,1)}, u32[]{:S(2)}) %copy-start.2) | copy-done | bytes 8388632
  26.0 1.0 copy-done.6
  27.0 8.8 %shard_map.68 = (bf16[128,2048]{1,0:T(8,128)(2,1)}, bf16[128,2048]{1,0:T(8,128)(2,1)}, f32[128,2048]{1,0:T(8,128)}, f32[128,2048]{1,0:T(8,128)S(1)}, bf16[128,2048]{1,0:T(8,128)(2,1)S(1)}) custom-call(s32[1]{0:T(128)} %bitcast.first, bf16[2,128,1024]{2,1,0:T(8,128)(2,1)S(1)} %copy-done.6, bf16[128,2048]{1,0:T(8,128)(2,1)S(1)} %bitcast.43, ...), custom_call_target="tpu_custom_call" | custom-call | flops 2415919104 | bytes 16777216 | tf_op jit(solution)/shard_map/pallas_call | solution.py:105
  35.7 0.8 copy-done.7
  36.5 1.5 %collective-permute-start.2 = (f32[128,2048]{1,0:T(8,128)}, f32[128,2048]{1,0:T(8,128)}, u32[]{:S(2)}, u32[]{:S(2)}) collective-permute-start(f32[128,2048]{1,0:T(8,128)} %get-tuple-element.12), channel_id=1, source_target_pairs={{0,1},{1,0},{2,3},{3,2},{4,5},{5,4},{6,7},{7,6},{8,9},{9,8},{10,11... | collective-permute-start | bytes 3145736 | tf_op jit(solution)/shard_map/ppermute | solution.py:20
  38.1 1.3 %collective-permute-start.4 = (bf16[128,2048]{1,0:T(8,128)(2,1)}, bf16[128,2048]{1,0:T(8,128)(2,1)S(1)}, u32[]{:S(2)}, u32[]{:S(2)}) collective-permute-start(bf16[128,2048]{1,0:T(8,128)(2,1)} %get-tuple-element.13), channel_id=1, source_target_pairs={{0,4},{4,8},{8,12},{12,14},{14,10},{10,6},{6,2},{2,0},{1,5},{5,9},... | collective-permute-start | bytes 1572872 | tf_op jit(solution)/shard_map/ppermute | solution.py:173
  39.5 1.3 %collective-permute-start.1 = (bf16[128,2048]{1,0:T(8,128)(2,1)}, bf16[128,2048]{1,0:T(8,128)(2,1)}, u32[]{:S(2)}, u32[]{:S(2)}) collective-permute-start(bf16[128,2048]{1,0:T(8,128)(2,1)} %get-tuple-element.9), channel_id=1, source_target_pairs={{16,0},{17,1},{18,2},{19,3},{20,4},{21,5},{22,6},{23,7},{24,8},{25... | collective-permute-start | bytes 1572872 | tf_op jit(solution)/shard_map/ppermute | solution.py:157
  41.0 2.5 %broadcast_in_dim.20 = bf16[1024,2048]{1,0:T(8,128)(2,1)} broadcast(bf16[]{:T(256)} %constant.138.clone.1), dimensions={} | broadcast | bytes 4194306 | tf_op jit(solution)/shard_map/broadcast_in_dim | solution.py:191
  43.5 1.9 %constant_dynamic-update-slice_fusion.8 = bf16[1024,2048]{1,0:T(8,128)(2,1)} fusion(bf16[1024,2048]{1,0:T(8,128)(2,1)} %broadcast_in_dim.20, bf16[128,2048]{1,0:T(8,128)(2,1)} %get-tuple-element.13, s32[]{:T(128)S(6)} %select_n.166), kind=kLoop, calls=%fused_computation.27 | loop fusion | bytes 1048580 | tf_op jit(solution)/shard_map/dynamic_update_slice | solution.py:194
  45.4 6.6 %collective-permute-done.4 = bf16[128,2048]{1,0:T(8,128)(2,1)S(1)} collective-permute-done((bf16[128,2048]{1,0:T(8,128)(2,1)}, bf16[128,2048]{1,0:T(8,128)(2,1)S(1)}, u32[]{:S(2)}, u32[]{:S(2)}) %collective-permute-start.4) | collective-permute-done | bytes 524320 | tf_op jit(solution)/shard_map/ppermute | solution.py:173
  51.9 1.3 %collective-permute-start.5 = (bf16[128,2048]{1,0:T(8,128)(2,1)S(1)}, bf16[128,2048]{1,0:T(8,128)(2,1)}, u32[]{:S(2)}, u32[]{:S(2)}) collective-permute-start(bf16[128,2048]{1,0:T(8,128)(2,1)S(1)} %collective-permute-done.4), channel_id=1, source_target_pairs={{0,4},{4,8},{8,12},{12,14},{14,10},{10,6},{6,2},{2,0},{1,5},{5,9},... | collective-permute-start | bytes 1572872 | tf_op jit(solution)/shard_map/ppermute | solution.py:173
  53.2 0.2 collective-permute-start.7
  53.4 1.5 %collective-permute-done.1 = bf16[128,2048]{1,0:T(8,128)(2,1)} collective-permute-done((bf16[128,2048]{1,0:T(8,128)(2,1)}, bf16[128,2048]{1,0:T(8,128)(2,1)}, u32[]{:S(2)}, u32[]{:S(2)}) %collective-permute-start.1) | collective-permute-done | bytes 524320 | tf_op jit(solution)/shard_map/ppermute | solution.py:157
  54.9 1.9 %broadcast_select_fusion = (bf16[128,2048]{1,0:T(8,128)(2,1)}, bf16[128,2048]{1,0:T(8,128)(2,1)S(1)}) fusion(bf16[128,2048]{1,0:T(8,128)(2,1)} %collective-permute-done.1, bf16[128,2048]{1,0:T(8,128)(2,1)} %get-tuple-element.9, pred[]{:T(512)S(6)} %eq.49, bf16[128,2048]{1,0:T(8,128)(2,1)S(1)} %copy-done.8), kind=kLoop, calls=%fused_computation.8 | loop fusion | flops 524288 | bytes 2621441 | tf_op jit(solution)/shard_map/jit(_where)/select_n | solution.py:158
  56.9 1.3 %add_convert_fusion = bf16[128,2048]{1,0:T(8,128)(2,1)S(1)} fusion(f32[128,2048]{1,0:T(8,128)S(1)} %get-tuple-element.11, f32[128,2048]{1,0:T(8,128)} %collective-permute-done.2), kind=kLoop, calls=%fused_computation.4 | loop fusion | flops 524288 | bytes 2621440 | tf_op jit(solution)/shard_map/convert_element_type | solution.py:159
  58.2 1.3 %collective-permute-start.3 = (bf16[8,8,2048]{2,1,0:T(8,128)(2,1)S(1)}, bf16[8,8,2048]{2,1,0:T(8,128)(2,1)S(1)}, u32[]{:S(2)}, u32[]{:S(2)}) collective-permute-start(bf16[8,8,2048]{2,1,0:T(8,128)(2,1)S(1)} %slice_bitcast_fusion.1), channel_id=1, source_target_pairs={{16,0},{17,1},{18,2},{19,3},{20,4},{21,5},{22,6},{23,7},{24,8},{25... | collective-permute-start | bytes 786440 | tf_op jit(solution)/shard_map/ppermute | solution.py:160
  59.5 0.8 constant_dynamic-update-slice_fusion.7
  60.4 1.9 %constant_dynamic-update-slice_fusion.6 = bf16[1024,2048]{1,0:T(8,128)(2,1)} fusion(bf16[1024,2048]{1,0:T(8,128)(2,1)} %constant_dynamic-update-slice_fusion.7, bf16[128,2048]{1,0:T(8,128)(2,1)} %collective-permute-done.6, s32[]{:T(128)S(6)} %select_n.170), kind=kLoop, calls=%fused_computation.25 | loop fusion | bytes 1048580 | tf_op jit(solution)/shard_map/dynamic_update_slice | solution.py:194
  62.3 2.5 %collective-permute-done.5 = bf16[128,2048]{1,0:T(8,128)(2,1)} collective-permute-done((bf16[128,2048]{1,0:T(8,128)(2,1)S(1)}, bf16[128,2048]{1,0:T(8,128)(2,1)}, u32[]{:S(2)}, u32[]{:S(2)}) %collective-permute-start.5) | collective-permute-done | bytes 524320 | tf_op jit(solution)/shard_map/ppermute | solution.py:173
  64.8 1.3 %collective-permute-start.8 = (bf16[128,2048]{1,0:T(8,128)(2,1)}, bf16[128,2048]{1,0:T(8,128)(2,1)S(1)}, u32[]{:S(2)}, u32[]{:S(2)}) collective-permute-start(bf16[128,2048]{1,0:T(8,128)(2,1)} %collective-permute-done.5), channel_id=1, source_target_pairs={{0,4},{4,8},{8,12},{12,14},{14,10},{10,6},{6,2},{2,0},{1,5},{5,9},... | collective-permute-start | bytes 1572872 | tf_op jit(solution)/shard_map/ppermute | solution.py:173
  66.3 0.4 collective-permute-done.3
  66.8 0.9 pad_maximum_fusion
  67.7 5.6 %all-to-all-start = ((bf16[8,192,256]{2,1,0:T(8,128)(2,1)}), bf16[8,192,256]{2,1,0:T(8,128)(2,1)S(1)}, u32[]{:S(2)}, u32[]{:S(2)}) async-start(bf16[8,192,256]{2,1,0:T(8,128)(2,1)} %pad_maximum_fusion), calls=%async_computation | async-start | bytes 1572864 | tf_op jit(solution)/shard_map/all_to_all | solution.py:182
  73.3 1.9 %constant_dynamic-update-slice_fusion.5 = bf16[1024,2048]{1,0:T(8,128)(2,1)} fusion(bf16[1024,2048]{1,0:T(8,128)(2,1)} %constant_dynamic-update-slice_fusion.6, bf16[128,2048]{1,0:T(8,128)(2,1)} %collective-permute-done.5, s32[]{:T(128)S(6)} %select_n.172), kind=kLoop, calls=%fused_computation.24 | loop fusion | bytes 1048580 | tf_op jit(solution)/shard_map/dynamic_update_slice | solution.py:194
  75.2 1.9 %constant_dynamic-update-slice_fusion.4 = bf16[1024,2048]{1,0:T(8,128)(2,1)} fusion(bf16[1024,2048]{1,0:T(8,128)(2,1)} %constant_dynamic-update-slice_fusion.5, bf16[128,2048]{1,0:T(8,128)(2,1)} %collective-permute-done.7, s32[]{:T(128)S(6)} %select_n.174), kind=kLoop, calls=%fused_computation.23 | loop fusion | bytes 1048580 | tf_op jit(solution)/shard_map/dynamic_update_slice | solution.py:194
  77.1 1.4 %collective-permute-start.10 = (bf16[64,2048]{1,0:T(8,128)(2,1)S(1)}, bf16[64,2048]{1,0:T(8,128)(2,1)S(1)}, u32[]{:S(2)}, u32[]{:S(2)}) collective-permute-start(bf16[64,2048]{1,0:T(8,128)(2,1)S(1)} %slice.35), channel_id=1, source_target_pairs={{0,4},{4,8},{8,12},{12,14},{14,10},{10,6},{6,2},{2,0},{1,5},{5,9},... | collective-permute-start | bytes 786440 | tf_op jit(solution)/shard_map/ppermute | solution.py:189
  78.5 1.0 slice.36
  79.5 0.2 collective-permute-start.11
  79.6 0.8 constant_dynamic-update-slice_fusion.3
  80.5 1.9 %constant_dynamic-update-slice_fusion.2 = bf16[1024,2048]{1,0:T(8,128)(2,1)} fusion(bf16[1024,2048]{1,0:T(8,128)(2,1)} %constant_dynamic-update-slice_fusion.3, bf16[128,2048]{1,0:T(8,128)(2,1)} %collective-permute-done.9, s32[]{:T(128)S(6)} %select_n.178), kind=kLoop, calls=%fused_computation.21 | loop fusion | bytes 1048580 | tf_op jit(solution)/shard_map/dynamic_update_slice | solution.py:194
  82.3 16.1 %collective-permute-done.10 = bf16[64,2048]{1,0:T(8,128)(2,1)S(1)} collective-permute-done((bf16[64,2048]{1,0:T(8,128)(2,1)S(1)}, bf16[64,2048]{1,0:T(8,128)(2,1)S(1)}, u32[]{:S(2)}, u32[]{:S(2)}) %collective-permute-start.10) | collective-permute-done | bytes 262176 | tf_op jit(solution)/shard_map/ppermute | solution.py:189
  98.5 0.7 constant_dynamic-update-slice_fusion.1
  99.2 1.2 %collective-permute-done.11 = bf16[64,2048]{1,0:T(8,128)(2,1)S(1)} collective-permute-done((bf16[64,2048]{1,0:T(8,128)(2,1)S(1)}, bf16[64,2048]{1,0:T(8,128)(2,1)S(1)}, u32[]{:S(2)}, u32[]{:S(2)}) %collective-permute-start.11) | collective-permute-done | bytes 262176 | tf_op jit(solution)/shard_map/ppermute | solution.py:190
  100.4 0.7 constant_dynamic-update-slice_fusion
  101.2 2.9 %fusion.8 = f32[128,2048]{1,0:T(8,128)S(1)} fusion(bf16[1024,128]{1,0:T(8,128)(2,1)S(1)} %bitcast.52, bf16[1024,2048]{1,0:T(8,128)(2,1)} %constant_dynamic-update-slice_fusion), kind=kOutput, calls=%fused_computation.49 | convolution fusion | flops 536870912 | bytes 5505024 | tf_op jit(solution)/shard_map/dot_general | solution.py:16
  104.1 2.8 %collective-permute-start.12 = (f32[128,2048]{1,0:T(8,128)S(1)}, f32[128,2048]{1,0:T(8,128)S(1)}, u32[]{:S(2)}, u32[]{:S(2)}) collective-permute-start(f32[128,2048]{1,0:T(8,128)S(1)} %fusion.8), channel_id=1, source_target_pairs={{0,1},{1,0},{2,3},{3,2},{4,5},{5,4},{6,7},{7,6},{8,9},{9,8},{10,11... | collective-permute-start | bytes 3145736 | tf_op jit(solution)/shard_map/ppermute | solution.py:20
  107.0 0.6 broadcast_multiply_fusion
  107.6 1.6 %collective-permute-done.12 = f32[128,2048]{1,0:T(8,128)S(1)} collective-permute-done((f32[128,2048]{1,0:T(8,128)S(1)}, f32[128,2048]{1,0:T(8,128)S(1)}, u32[]{:S(2)}, u32[]{:S(2)}) %collective-permute-start.12) | collective-permute-done | bytes 1048608 | tf_op jit(solution)/shard_map/ppermute | solution.py:20
  109.2 3.9 %fusion.1 = f32[1,128,2048]{2,1,0:T(8,128)} fusion(f32[128,2048]{1,0:T(8,128)S(1)} %collective-permute-done.12, bf16[1024,128]{1,0:T(8,128)(2,1)S(1)} %bitcast.50, bf16[1024,2048]{1,0:T(8,128)(2,1)} %constant_dynamic-update-slice_fusion), kind=kOutput, calls=%fused_computation.2 | convolution fusion | flops 537395200 | bytes 6553600 | tf_op jit(solution)/shard_map/dot_general | solution.py:16
  (30 shorter events, 0.7 us)
Async XLA Ops:
  0.6 10.6 %copy-start = (bf16[256,2048]{1,0:T(8,128)(2,1)S(1)}, bf16[256,2048]{1,0:T(8,128)(2,1)}, u32[]{:S(2)}) copy-start(bf16[256,2048]{1,0:T(8,128)(2,1)} %param.6) | copy-start | bytes 3145732
  0.6 3.5 %copy-start.1 = (bf16[1,2048,2048]{2,1,0:T(8,128)(2,1)S(1)}, bf16[1,2048,2048]{2,1,0:T(8,128)(2,1)}, u32[]{:S(2)}) copy-start(bf16[1,2048,2048]{2,1,0:T(8,128)(2,1)} %param.5) | copy-start | bytes 25165828
  4.1 1.0 copy-start.3
  5.2 6.1 %copy-start.9 = (s32[128]{0:T(128)S(1)}, s32[128]{0:T(128)}, u32[]{:S(2)}) copy-start(s32[128]{0:T(128)} %param.7) | copy-start | bytes 1540
  5.2 17.4 %copy-start.4 = (bf16[1,128,2048]{2,1,0:T(8,128)(2,1)S(1)}, bf16[1,128,2048]{2,1,0:T(8,128)(2,1)}, u32[]{:S(2)}) copy-start(bf16[1,128,2048]{2,1,0:T(8,128)(2,1)} %param.4) | copy-start | bytes 1572868
  8.1 13.7 %collective-permute-start = (bf16[2,128,1024]{2,1,0:T(8,128)(2,1)S(1)}, bf16[2,128,1024]{2,1,0:T(8,128)(2,1)S(1)}, u32[]{:S(2)}, u32[]{:S(2)}) collective-permute-start(bf16[2,128,1024]{2,1,0:T(8,128)(2,1)S(1)} %shard_map.67), channel_id=1, source_target_pairs={{0,16},{1,17},{2,18},{3,19},{4,20},{5,21},{6,22},{7,23},{8,24},{9,... | collective-permute-start | bytes 1572872 | tf_op jit(solution)/shard_map/ppermute | solution.py:151
  21.8 0.8 copy-start.5
  22.6 3.4 %copy-start.2 = (bf16[1,2048,2048]{2,1,0:T(8,128)(2,1)S(1)}, bf16[1,2048,2048]{2,1,0:T(8,128)(2,1)}, u32[]{:S(2)}) copy-start(bf16[1,2048,2048]{2,1,0:T(8,128)(2,1)} %param.5) | copy-start | bytes 25165828
  25.9 1.0 copy-start.6
  35.7 0.8 copy-start.7
  36.5 18.4 %copy-start.8 = (bf16[128,2048]{1,0:T(8,128)(2,1)S(1)}, bf16[128,2048]{1,0:T(8,128)(2,1)}, u32[]{:S(2)}) copy-start(bf16[128,2048]{1,0:T(8,128)(2,1)} %copy-done.7) | copy-start | bytes 1572868
  36.5 20.3 %collective-permute-start.2 = (f32[128,2048]{1,0:T(8,128)}, f32[128,2048]{1,0:T(8,128)}, u32[]{:S(2)}, u32[]{:S(2)}) collective-permute-start(f32[128,2048]{1,0:T(8,128)} %get-tuple-element.12), channel_id=1, source_target_pairs={{0,1},{1,0},{2,3},{3,2},{4,5},{5,4},{6,7},{7,6},{8,9},{9,8},{10,11... | collective-permute-start | bytes 3145736 | tf_op jit(solution)/shard_map/ppermute | solution.py:20
  38.1 13.9 %collective-permute-start.4 = (bf16[128,2048]{1,0:T(8,128)(2,1)}, bf16[128,2048]{1,0:T(8,128)(2,1)S(1)}, u32[]{:S(2)}, u32[]{:S(2)}) collective-permute-start(bf16[128,2048]{1,0:T(8,128)(2,1)} %get-tuple-element.13), channel_id=1, source_target_pairs={{0,4},{4,8},{8,12},{12,14},{14,10},{10,6},{6,2},{2,0},{1,5},{5,9},... | collective-permute-start | bytes 1572872 | tf_op jit(solution)/shard_map/ppermute | solution.py:173
  39.4 13.9 %collective-permute-start.6 = (bf16[128,2048]{1,0:T(8,128)(2,1)}, bf16[128,2048]{1,0:T(8,128)(2,1)}, u32[]{:S(2)}, u32[]{:S(2)}) collective-permute-start(bf16[128,2048]{1,0:T(8,128)(2,1)} %get-tuple-element.13), channel_id=1, source_target_pairs={{4,0},{8,4},{12,8},{14,12},{10,14},{6,10},{2,6},{0,2},{5,1},{9,5},... | collective-permute-start | bytes 1572872 | tf_op jit(solution)/shard_map/ppermute | solution.py:174
  39.5 15.4 %collective-permute-start.1 = (bf16[128,2048]{1,0:T(8,128)(2,1)}, bf16[128,2048]{1,0:T(8,128)(2,1)}, u32[]{:S(2)}, u32[]{:S(2)}) collective-permute-start(bf16[128,2048]{1,0:T(8,128)(2,1)} %get-tuple-element.9), channel_id=1, source_target_pairs={{16,0},{17,1},{18,2},{19,3},{20,4},{21,5},{22,6},{23,7},{24,8},{25... | collective-permute-start | bytes 1572872 | tf_op jit(solution)/shard_map/ppermute | solution.py:157
  51.9 12.9 %collective-permute-start.5 = (bf16[128,2048]{1,0:T(8,128)(2,1)S(1)}, bf16[128,2048]{1,0:T(8,128)(2,1)}, u32[]{:S(2)}, u32[]{:S(2)}) collective-permute-start(bf16[128,2048]{1,0:T(8,128)(2,1)S(1)} %collective-permute-done.4), channel_id=1, source_target_pairs={{0,4},{4,8},{8,12},{12,14},{14,10},{10,6},{6,2},{2,0},{1,5},{5,9},... | collective-permute-start | bytes 1572872 | tf_op jit(solution)/shard_map/ppermute | solution.py:173
  53.2 12.9 %collective-permute-start.7 = (bf16[128,2048]{1,0:T(8,128)(2,1)}, bf16[128,2048]{1,0:T(8,128)(2,1)}, u32[]{:S(2)}, u32[]{:S(2)}) collective-permute-start(bf16[128,2048]{1,0:T(8,128)(2,1)} %collective-permute-done.6), channel_id=1, source_target_pairs={{4,0},{8,4},{12,8},{14,12},{10,14},{6,10},{2,6},{0,2},{5,1},{9,5},... | collective-permute-start | bytes 1572872 | tf_op jit(solution)/shard_map/ppermute | solution.py:174
  58.2 8.5 %collective-permute-start.3 = (bf16[8,8,2048]{2,1,0:T(8,128)(2,1)S(1)}, bf16[8,8,2048]{2,1,0:T(8,128)(2,1)S(1)}, u32[]{:S(2)}, u32[]{:S(2)}) collective-permute-start(bf16[8,8,2048]{2,1,0:T(8,128)(2,1)S(1)} %slice_bitcast_fusion.1), channel_id=1, source_target_pairs={{16,0},{17,1},{18,2},{19,3},{20,4},{21,5},{22,6},{23,7},{24,8},{25... | collective-permute-start | bytes 786440 | tf_op jit(solution)/shard_map/ppermute | solution.py:160
  64.8 12.2 %collective-permute-start.8 = (bf16[128,2048]{1,0:T(8,128)(2,1)}, bf16[128,2048]{1,0:T(8,128)(2,1)S(1)}, u32[]{:S(2)}, u32[]{:S(2)}) collective-permute-start(bf16[128,2048]{1,0:T(8,128)(2,1)} %collective-permute-done.5), channel_id=1, source_target_pairs={{0,4},{4,8},{8,12},{12,14},{14,10},{10,6},{6,2},{2,0},{1,5},{5,9},... | collective-permute-start | bytes 1572872 | tf_op jit(solution)/shard_map/ppermute | solution.py:173
  66.1 12.4 %collective-permute-start.9 = (bf16[128,2048]{1,0:T(8,128)(2,1)}, bf16[128,2048]{1,0:T(8,128)(2,1)}, u32[]{:S(2)}, u32[]{:S(2)}) collective-permute-start(bf16[128,2048]{1,0:T(8,128)(2,1)} %collective-permute-done.7), channel_id=1, source_target_pairs={{4,0},{8,4},{12,8},{14,12},{10,14},{6,10},{2,6},{0,2},{5,1},{9,5},... | collective-permute-start | bytes 1572872 | tf_op jit(solution)/shard_map/ppermute | solution.py:174
  67.7 33.4 %all-to-all-start = ((bf16[8,192,256]{2,1,0:T(8,128)(2,1)}), bf16[8,192,256]{2,1,0:T(8,128)(2,1)S(1)}, u32[]{:S(2)}, u32[]{:S(2)}) async-start(bf16[8,192,256]{2,1,0:T(8,128)(2,1)} %pad_maximum_fusion), calls=%async_computation | async-start | bytes 1572864 | tf_op jit(solution)/shard_map/all_to_all | solution.py:182
  77.1 21.4 %collective-permute-start.10 = (bf16[64,2048]{1,0:T(8,128)(2,1)S(1)}, bf16[64,2048]{1,0:T(8,128)(2,1)S(1)}, u32[]{:S(2)}, u32[]{:S(2)}) collective-permute-start(bf16[64,2048]{1,0:T(8,128)(2,1)S(1)} %slice.35), channel_id=1, source_target_pairs={{0,4},{4,8},{8,12},{12,14},{14,10},{10,6},{6,2},{2,0},{1,5},{5,9},... | collective-permute-start | bytes 786440 | tf_op jit(solution)/shard_map/ppermute | solution.py:189
  79.5 20.9 %collective-permute-start.11 = (bf16[64,2048]{1,0:T(8,128)(2,1)S(1)}, bf16[64,2048]{1,0:T(8,128)(2,1)S(1)}, u32[]{:S(2)}, u32[]{:S(2)}) collective-permute-start(bf16[64,2048]{1,0:T(8,128)(2,1)S(1)} %slice.36), channel_id=1, source_target_pairs={{4,0},{8,4},{12,8},{14,12},{10,14},{6,10},{2,6},{0,2},{5,1},{9,5},... | collective-permute-start | bytes 786440 | tf_op jit(solution)/shard_map/ppermute | solution.py:190
  104.1 5.1 %collective-permute-start.12 = (f32[128,2048]{1,0:T(8,128)S(1)}, f32[128,2048]{1,0:T(8,128)S(1)}, u32[]{:S(2)}, u32[]{:S(2)}) collective-permute-start(f32[128,2048]{1,0:T(8,128)S(1)} %fusion.8), channel_id=1, source_target_pairs={{0,1},{1,0},{2,3},{3,2},{4,5},{5,4},{6,7},{7,6},{8,9},{9,8},{10,11... | collective-permute-start | bytes 3145736 | tf_op jit(solution)/shard_map/ppermute | solution.py:20

commit v5 on v4

--- a/solution.py
+++ b/solution.py
@@ -196,7 +196,8 @@
     give = jnp.where(core == 0, upper, lower).reshape(chips * rows_dev, cols // 2)
     keep = jnp.where(core == 0, lower, upper).reshape(chips * rows_dev, cols // 2)
     got = swap_core(dot(give, right_all, 0, 0))
-    weight_grad = (dot(keep, right_all, 0, 0) + got) * (1.0 / jnp.sqrt(F32(total_rows)))
+    own = lax.optimization_barrier(dot(keep, right_all, 0, 0))
+    weight_grad = (own + got) * (1.0 / jnp.sqrt(F32(total_rows)))
     return weight_grad[None], relation_grad, query_grad
 
 

time: 115 us -> 113 us (0.983)
  waiting for transfers between devices: 37.8 us -> 36.2 us
    ppermute x2, waiting for transfers between devices: 1.61 us -> 0.01 us  [swap_core(): return lax.ppermute(block, 'core', [(0, 1), (1, 0)])]
  transfers between devices with their start and end apart: 14 -> 14, of which waited for: 8 -> 7; matrix products, arithmetic and copies ran while one was open for 21% -> 24% of each run, Pallas kernels for 0% -> 0%
where the time goes in v5:
time: 113 us; the launch traced here: 112 us
  waiting for transfers between devices  36.2 us (32%)
  local copies, waits for them, and re-layouts  28.8 us (25%)
  starting transfers between devices  21.7 us (19%)
  Pallas kernels  11.6 us (10%)
  matrix products  6.2 us (5%)
  other arithmetic  6.18 us (5%)
    ppermute x1, waiting for transfers between devices, local(): blocks.append((lax.ppermute(fwd[:mid], 'chip', up), chips // 2, 0))  16.1 us
    dynamic_update_slice x9, local copies, waits for them, and re-layouts, local(): right_all = lax.dynamic_update_slice_in_dim(right_all, block, start, 0)  12.5 us
    unnamed x20, local copies, waits for them, and re-layouts  10.5 us
    ppermute x3, waiting for transfers between devices, local(): fwd = lax.ppermute(fwd, 'chip', up)  9.13 us
    pallas_call x1, Pallas kernels, trail(): pl.pallas_call(trail_body, out_shape=(jax.ShapeDtypeStruct((rows_dev, hid...  8.75 us
    ppermute x1, waiting for transfers between devices, local(): query = lax.ppermute(own_query, 'hop', [(0, 1)])  7.79 us
    dot_general x3, matrix products, dot(): lax.dot_general(a, b, (((ca,), (cb,)), ((), ())), preferred_element_type=...  6.2 us
    all_to_all x1, starting transfers between devices, local(): received = lax.all_to_all(sent, 'chip', 0, 0, tiled=True)  5.61 us
  transfers between devices with their start and end apart: 14, of which 7 were waited for; matrix products, arithmetic and copies ran while one was open for 24% of the time, Pallas kernels for 0%

profile of v5, /device:TPU:9, one launch (start us, length us, event | category | flops | bytes accessed | tf_op | source)
XLA Modules:
  0.0 111.7 jit_solution(17221684094147587098)
XLA Ops:
  0.7 3.5 %copy-done.1 = bf16[1,2048,2048]{2,1,0:T(8,128)(2,1)S(1)} copy-done((bf16[1,2048,2048]{2,1,0:T(8,128)(2,1)S(1)}, bf16[1,2048,2048]{2,1,0:T(8,128)(2,1)}, u32[]{:S(2)}) %copy-start.1) | copy-done | bytes 8388632
  4.1 1.0 copy-done.3
  5.2 2.9 %shard_map.67 = bf16[2,128,1024]{2,1,0:T(8,128)(2,1)S(1)} custom-call(bf16[128,2048]{1,0:T(8,128)(2,1)S(1)} %bitcast.42, bf16[2048,2048]{1,0:T(8,128)(2,1)S(1)} %bitcast.40), custom_call_target="tpu_custom_call" | custom-call | flops 1073741824 | bytes 8388608 | tf_op jit(solution)/shard_map/pallas_call | solution.py:43
  8.1 3.2 %collective-permute-start = (bf16[2,128,1024]{2,1,0:T(8,128)(2,1)S(1)}, bf16[2,128,1024]{2,1,0:T(8,128)(2,1)S(1)}, u32[]{:S(2)}, u32[]{:S(2)}) collective-permute-start(bf16[2,128,1024]{2,1,0:T(8,128)(2,1)S(1)} %shard_map.67), channel_id=1, source_target_pairs={{0,16},{1,17},{2,18},{3,19},{4,20},{5,21},{6,22},{7,23},{8,24},{9,... | collective-permute-start | bytes 1572872 | tf_op jit(solution)/shard_map/ppermute | solution.py:151
  11.2 0.3 convolution_convert_fusion
  11.6 1.0 copy.9
  12.6 1.2 %copy.10 = bf16[128,2,1024]{2,0,1:T(8,128)(2,1)S(1)} copy(bf16[128,2,1024]{0,2,1:T(8,128)(2,1)} %bitcast.48) | data formatting | bytes 1048576 | tf_op jit(solution)/shard_map/reshape | solution.py:153
  14.0 7.8 %collective-permute-done.query = bf16[2,128,1024]{2,1,0:T(8,128)(2,1)S(1)} collective-permute-done((bf16[2,128,1024]{2,1,0:T(8,128)(2,1)S(1)}, bf16[2,128,1024]{2,1,0:T(8,128)(2,1)S(1)}, u32[]{:S(2)}, u32[]{:S(2)}) %collective-permute-start) | collective-permute-done | bytes 524320 | tf_op jit(solution)/shard_map/ppermute | solution.py:151
  21.8 0.8 copy-done.5
  22.6 3.4 %copy-done.2 = bf16[1,2048,2048]{2,1,0:T(8,128)(2,1)S(1)} copy-done((bf16[1,2048,2048]{2,1,0:T(8,128)(2,1)S(1)}, bf16[1,2048,2048]{2,1,0:T(8,128)(2,1)}, u32[]{:S(2)}) %copy-start.2) | copy-done | bytes 8388632
  26.0 1.0 copy-done.6
  27.0 8.8 %shard_map.68 = (bf16[128,2048]{1,0:T(8,128)(2,1)}, bf16[128,2048]{1,0:T(8,128)(2,1)}, f32[128,2048]{1,0:T(8,128)}, f32[128,2048]{1,0:T(8,128)S(1)}, bf16[128,2048]{1,0:T(8,128)(2,1)S(1)}) custom-call(s32[1]{0:T(128)} %bitcast.first, bf16[2,128,1024]{2,1,0:T(8,128)(2,1)S(1)} %copy-done.6, bf16[128,2048]{1,0:T(8,128)(2,1)S(1)} %bitcast.43, ...), custom_call_target="tpu_custom_call" | custom-call | flops 2415919104 | bytes 16777216 | tf_op jit(solution)/shard_map/pallas_call | solution.py:105
  35.7 0.8 copy-done.7
  36.5 1.5 %collective-permute-start.2 = (f32[128,2048]{1,0:T(8,128)}, f32[128,2048]{1,0:T(8,128)}, u32[]{:S(2)}, u32[]{:S(2)}) collective-permute-start(f32[128,2048]{1,0:T(8,128)} %get-tuple-element.12), channel_id=1, source_target_pairs={{0,1},{1,0},{2,3},{3,2},{4,5},{5,4},{6,7},{7,6},{8,9},{9,8},{10,11... | collective-permute-start | bytes 3145736 | tf_op jit(solution)/shard_map/ppermute | solution.py:20
  38.1 1.3 %collective-permute-start.4 = (bf16[128,2048]{1,0:T(8,128)(2,1)}, bf16[128,2048]{1,0:T(8,128)(2,1)S(1)}, u32[]{:S(2)}, u32[]{:S(2)}) collective-permute-start(bf16[128,2048]{1,0:T(8,128)(2,1)} %get-tuple-element.13), channel_id=1, source_target_pairs={{0,4},{4,8},{8,12},{12,14},{14,10},{10,6},{6,2},{2,0},{1,5},{5,9},... | collective-permute-start | bytes 1572872 | tf_op jit(solution)/shard_map/ppermute | solution.py:173
  39.5 1.3 %collective-permute-start.1 = (bf16[128,2048]{1,0:T(8,128)(2,1)}, bf16[128,2048]{1,0:T(8,128)(2,1)}, u32[]{:S(2)}, u32[]{:S(2)}) collective-permute-start(bf16[128,2048]{1,0:T(8,128)(2,1)} %get-tuple-element.9), channel_id=1, source_target_pairs={{16,0},{17,1},{18,2},{19,3},{20,4},{21,5},{22,6},{23,7},{24,8},{25... | collective-permute-start | bytes 1572872 | tf_op jit(solution)/shard_map/ppermute | solution.py:157
  41.0 2.5 %broadcast_in_dim.20 = bf16[1024,2048]{1,0:T(8,128)(2,1)} broadcast(bf16[]{:T(256)} %constant.138.clone.1), dimensions={} | broadcast | bytes 4194306 | tf_op jit(solution)/shard_map/broadcast_in_dim | solution.py:191
  43.5 1.9 %constant_dynamic-update-slice_fusion.8 = bf16[1024,2048]{1,0:T(8,128)(2,1)} fusion(bf16[1024,2048]{1,0:T(8,128)(2,1)} %broadcast_in_dim.20, bf16[128,2048]{1,0:T(8,128)(2,1)} %get-tuple-element.13, s32[]{:T(128)S(6)} %select_n.166), kind=kLoop, calls=%fused_computation.25 | loop fusion | bytes 1048580 | tf_op jit(solution)/shard_map/dynamic_update_slice | solution.py:194
  45.4 6.6 %collective-permute-done.4 = bf16[128,2048]{1,0:T(8,128)(2,1)S(1)} collective-permute-done((bf16[128,2048]{1,0:T(8,128)(2,1)}, bf16[128,2048]{1,0:T(8,128)(2,1)S(1)}, u32[]{:S(2)}, u32[]{:S(2)}) %collective-permute-start.4) | collective-permute-done | bytes 524320 | tf_op jit(solution)/shard_map/ppermute | solution.py:173
  51.9 1.3 %collective-permute-start.5 = (bf16[128,2048]{1,0:T(8,128)(2,1)S(1)}, bf16[128,2048]{1,0:T(8,128)(2,1)}, u32[]{:S(2)}, u32[]{:S(2)}) collective-permute-start(bf16[128,2048]{1,0:T(8,128)(2,1)S(1)} %collective-permute-done.4), channel_id=1, source_target_pairs={{0,4},{4,8},{8,12},{12,14},{14,10},{10,6},{6,2},{2,0},{1,5},{5,9},... | collective-permute-start | bytes 1572872 | tf_op jit(solution)/shard_map/ppermute | solution.py:173
  53.4 1.5 %collective-permute-done.1 = bf16[128,2048]{1,0:T(8,128)(2,1)} collective-permute-done((bf16[128,2048]{1,0:T(8,128)(2,1)}, bf16[128,2048]{1,0:T(8,128)(2,1)}, u32[]{:S(2)}, u32[]{:S(2)}) %collective-permute-start.1) | collective-permute-done | bytes 524320 | tf_op jit(solution)/shard_map/ppermute | solution.py:157
  54.9 1.9 %broadcast_select_fusion = (bf16[128,2048]{1,0:T(8,128)(2,1)}, bf16[128,2048]{1,0:T(8,128)(2,1)S(1)}) fusion(bf16[128,2048]{1,0:T(8,128)(2,1)} %collective-permute-done.1, bf16[128,2048]{1,0:T(8,128)(2,1)} %get-tuple-element.9, pred[]{:T(512)S(6)} %eq.49, bf16[128,2048]{1,0:T(8,128)(2,1)S(1)} %copy-done.8), kind=kLoop, calls=%fused_computation.6 | loop fusion | flops 524288 | bytes 2621441 | tf_op jit(solution)/shard_map/jit(_where)/select_n | solution.py:158
  56.9 1.3 %add_convert_fusion = bf16[128,2048]{1,0:T(8,128)(2,1)S(1)} fusion(f32[128,2048]{1,0:T(8,128)S(1)} %get-tuple-element.11, f32[128,2048]{1,0:T(8,128)} %collective-permute-done.2), kind=kLoop, calls=%fused_computation.2 | loop fusion | flops 524288 | bytes 2621440 | tf_op jit(solution)/shard_map/convert_element_type | solution.py:159
  58.2 1.3 %collective-permute-start.3 = (bf16[8,8,2048]{2,1,0:T(8,128)(2,1)S(1)}, bf16[8,8,2048]{2,1,0:T(8,128)(2,1)S(1)}, u32[]{:S(2)}, u32[]{:S(2)}) collective-permute-start(bf16[8,8,2048]{2,1,0:T(8,128)(2,1)S(1)} %slice_bitcast_fusion.1), channel_id=1, source_target_pairs={{16,0},{17,1},{18,2},{19,3},{20,4},{21,5},{22,6},{23,7},{24,8},{25... | collective-permute-start | bytes 786440 | tf_op jit(solution)/shard_map/ppermute | solution.py:160
  59.5 0.8 constant_dynamic-update-slice_fusion.7
  60.4 1.9 %constant_dynamic-update-slice_fusion.6 = bf16[1024,2048]{1,0:T(8,128)(2,1)} fusion(bf16[1024,2048]{1,0:T(8,128)(2,1)} %constant_dynamic-update-slice_fusion.7, bf16[128,2048]{1,0:T(8,128)(2,1)} %collective-permute-done.6, s32[]{:T(128)S(6)} %select_n.170), kind=kLoop, calls=%fused_computation.23 | loop fusion | bytes 1048580 | tf_op jit(solution)/shard_map/dynamic_update_slice | solution.py:194
  62.3 2.5 %collective-permute-done.5 = bf16[128,2048]{1,0:T(8,128)(2,1)} collective-permute-done((bf16[128,2048]{1,0:T(8,128)(2,1)S(1)}, bf16[128,2048]{1,0:T(8,128)(2,1)}, u32[]{:S(2)}, u32[]{:S(2)}) %collective-permute-start.5) | collective-permute-done | bytes 524320 | tf_op jit(solution)/shard_map/ppermute | solution.py:173
  64.8 1.3 %collective-permute-start.8 = (bf16[128,2048]{1,0:T(8,128)(2,1)}, bf16[128,2048]{1,0:T(8,128)(2,1)S(1)}, u32[]{:S(2)}, u32[]{:S(2)}) collective-permute-start(bf16[128,2048]{1,0:T(8,128)(2,1)} %collective-permute-done.5), channel_id=1, source_target_pairs={{0,4},{4,8},{8,12},{12,14},{14,10},{10,6},{6,2},{2,0},{1,5},{5,9},... | collective-permute-start | bytes 1572872 | tf_op jit(solution)/shard_map/ppermute | solution.py:173
  66.1 0.2 collective-permute-start.9
  66.3 0.4 collective-permute-done.3
  66.8 0.9 pad_maximum_fusion
  67.7 5.6 %all-to-all-start = ((bf16[8,192,256]{2,1,0:T(8,128)(2,1)}), bf16[8,192,256]{2,1,0:T(8,128)(2,1)S(1)}, u32[]{:S(2)}, u32[]{:S(2)}) async-start(bf16[8,192,256]{2,1,0:T(8,128)(2,1)} %pad_maximum_fusion), calls=%async_computation | async-start | bytes 1572864 | tf_op jit(solution)/shard_map/all_to_all | solution.py:182
  73.3 1.9 %constant_dynamic-update-slice_fusion.5 = bf16[1024,2048]{1,0:T(8,128)(2,1)} fusion(bf16[1024,2048]{1,0:T(8,128)(2,1)} %constant_dynamic-update-slice_fusion.6, bf16[128,2048]{1,0:T(8,128)(2,1)} %collective-permute-done.5, s32[]{:T(128)S(6)} %select_n.172), kind=kLoop, calls=%fused_computation.22 | loop fusion | bytes 1048580 | tf_op jit(solution)/shard_map/dynamic_update_slice | solution.py:194
  75.2 1.9 %constant_dynamic-update-slice_fusion.4 = bf16[1024,2048]{1,0:T(8,128)(2,1)} fusion(bf16[1024,2048]{1,0:T(8,128)(2,1)} %constant_dynamic-update-slice_fusion.5, bf16[128,2048]{1,0:T(8,128)(2,1)} %collective-permute-done.7, s32[]{:T(128)S(6)} %select_n.174), kind=kLoop, calls=%fused_computation.21 | loop fusion | bytes 1048580 | tf_op jit(solution)/shard_map/dynamic_update_slice | solution.py:194
  77.1 1.4 %collective-permute-start.10 = (bf16[64,2048]{1,0:T(8,128)(2,1)S(1)}, bf16[64,2048]{1,0:T(8,128)(2,1)S(1)}, u32[]{:S(2)}, u32[]{:S(2)}) collective-permute-start(bf16[64,2048]{1,0:T(8,128)(2,1)S(1)} %slice.35), channel_id=1, source_target_pairs={{0,4},{4,8},{8,12},{12,14},{14,10},{10,6},{6,2},{2,0},{1,5},{5,9},... | collective-permute-start | bytes 786440 | tf_op jit(solution)/shard_map/ppermute | solution.py:189
  78.5 1.0 slice.36
  79.5 0.2 collective-permute-start.11
  79.6 0.8 constant_dynamic-update-slice_fusion.3
  80.5 1.9 %constant_dynamic-update-slice_fusion.2 = bf16[1024,2048]{1,0:T(8,128)(2,1)} fusion(bf16[1024,2048]{1,0:T(8,128)(2,1)} %constant_dynamic-update-slice_fusion.3, bf16[128,2048]{1,0:T(8,128)(2,1)} %collective-permute-done.9, s32[]{:T(128)S(6)} %select_n.178), kind=kLoop, calls=%fused_computation.19 | loop fusion | bytes 1048580 | tf_op jit(solution)/shard_map/dynamic_update_slice | solution.py:194
  82.3 16.1 %collective-permute-done.10 = bf16[64,2048]{1,0:T(8,128)(2,1)S(1)} collective-permute-done((bf16[64,2048]{1,0:T(8,128)(2,1)S(1)}, bf16[64,2048]{1,0:T(8,128)(2,1)S(1)}, u32[]{:S(2)}, u32[]{:S(2)}) %collective-permute-start.10) | collective-permute-done | bytes 262176 | tf_op jit(solution)/shard_map/ppermute | solution.py:189
  98.5 0.7 constant_dynamic-update-slice_fusion.1
  99.2 1.2 %collective-permute-done.11 = bf16[64,2048]{1,0:T(8,128)(2,1)S(1)} collective-permute-done((bf16[64,2048]{1,0:T(8,128)(2,1)S(1)}, bf16[64,2048]{1,0:T(8,128)(2,1)S(1)}, u32[]{:S(2)}, u32[]{:S(2)}) %collective-permute-start.11) | collective-permute-done | bytes 262176 | tf_op jit(solution)/shard_map/ppermute | solution.py:190
  100.4 0.7 constant_dynamic-update-slice_fusion
  101.2 2.9 %fusion.7 = f32[128,2048]{1,0:T(8,128)S(1)} fusion(bf16[1024,128]{1,0:T(8,128)(2,1)S(1)} %bitcast.52, bf16[1024,2048]{1,0:T(8,128)(2,1)} %constant_dynamic-update-slice_fusion), kind=kOutput, calls=%fused_computation.48 | convolution fusion | flops 536870912 | bytes 5505024 | tf_op jit(solution)/shard_map/dot_general | solution.py:16
  104.1 2.8 %collective-permute-start.12 = (f32[128,2048]{1,0:T(8,128)S(1)}, f32[128,2048]{1,0:T(8,128)S(1)}, u32[]{:S(2)}, u32[]{:S(2)}) collective-permute-start(f32[128,2048]{1,0:T(8,128)S(1)} %fusion.7), channel_id=1, source_target_pairs={{0,1},{1,0},{2,3},{3,2},{4,5},{5,4},{6,7},{7,6},{8,9},{9,8},{10,11... | collective-permute-start | bytes 3145736 | tf_op jit(solution)/shard_map/ppermute | solution.py:20
  106.9 2.9 %fusion.6 = f32[128,2048]{1,0:T(8,128)S(1)} fusion(bf16[1024,128]{1,0:T(8,128)(2,1)S(1)} %bitcast.51, bf16[1024,2048]{1,0:T(8,128)(2,1)} %constant_dynamic-update-slice_fusion), kind=kOutput, calls=%fused_computation.47 | convolution fusion | flops 536870912 | bytes 5505024 | tf_op jit(solution)/shard_map/dot_general | solution.py:16
  109.9 0.6 broadcast_multiply_fusion
  110.5 1.1 %multiply_bitcast_fusion = f32[1,128,2048]{2,1,0:T(8,128)} fusion(f32[128,2048]{1,0:T(8,128)S(1)} %fusion.6, f32[128,2048]{1,0:T(8,128)S(1)} %collective-permute-done.12), kind=kLoop, calls=%fused_computation.1 | loop fusion | flops 524288 | bytes 3145728 | tf_op jit(solution)/shard_map/broadcast_in_dim | solution.py:201
  (31 shorter events, 0.7 us)
Async XLA Ops:
  0.6 10.6 %copy-start = (bf16[256,2048]{1,0:T(8,128)(2,1)S(1)}, bf16[256,2048]{1,0:T(8,128)(2,1)}, u32[]{:S(2)}) copy-start(bf16[256,2048]{1,0:T(8,128)(2,1)} %param.6) | copy-start | bytes 3145732
  0.6 3.5 %copy-start.1 = (bf16[1,2048,2048]{2,1,0:T(8,128)(2,1)S(1)}, bf16[1,2048,2048]{2,1,0:T(8,128)(2,1)}, u32[]{:S(2)}) copy-start(bf16[1,2048,2048]{2,1,0:T(8,128)(2,1)} %param.5) | copy-start | bytes 25165828
  4.1 1.0 copy-start.3
  5.2 6.1 %copy-start.9 = (s32[128]{0:T(128)S(1)}, s32[128]{0:T(128)}, u32[]{:S(2)}) copy-start(s32[128]{0:T(128)} %param.7) | copy-start | bytes 1540
  5.2 17.4 %copy-start.4 = (bf16[1,128,2048]{2,1,0:T(8,128)(2,1)S(1)}, bf16[1,128,2048]{2,1,0:T(8,128)(2,1)}, u32[]{:S(2)}) copy-start(bf16[1,128,2048]{2,1,0:T(8,128)(2,1)} %param.4) | copy-start | bytes 1572868
  8.1 13.7 %collective-permute-start = (bf16[2,128,1024]{2,1,0:T(8,128)(2,1)S(1)}, bf16[2,128,1024]{2,1,0:T(8,128)(2,1)S(1)}, u32[]{:S(2)}, u32[]{:S(2)}) collective-permute-start(bf16[2,128,1024]{2,1,0:T(8,128)(2,1)S(1)} %shard_map.67), channel_id=1, source_target_pairs={{0,16},{1,17},{2,18},{3,19},{4,20},{5,21},{6,22},{7,23},{8,24},{9,... | collective-permute-start | bytes 1572872 | tf_op jit(solution)/shard_map/ppermute | solution.py:151
  21.8 0.8 copy-start.5
  22.6 3.4 %copy-start.2 = (bf16[1,2048,2048]{2,1,0:T(8,128)(2,1)S(1)}, bf16[1,2048,2048]{2,1,0:T(8,128)(2,1)}, u32[]{:S(2)}) copy-start(bf16[1,2048,2048]{2,1,0:T(8,128)(2,1)} %param.5) | copy-start | bytes 25165828
  25.9 1.0 copy-start.6
  35.7 0.8 copy-start.7
  36.5 18.4 %copy-start.8 = (bf16[128,2048]{1,0:T(8,128)(2,1)S(1)}, bf16[128,2048]{1,0:T(8,128)(2,1)}, u32[]{:S(2)}) copy-start(bf16[128,2048]{1,0:T(8,128)(2,1)} %copy-done.7) | copy-start | bytes 1572868
  36.5 20.3 %collective-permute-start.2 = (f32[128,2048]{1,0:T(8,128)}, f32[128,2048]{1,0:T(8,128)}, u32[]{:S(2)}, u32[]{:S(2)}) collective-permute-start(f32[128,2048]{1,0:T(8,128)} %get-tuple-element.12), channel_id=1, source_target_pairs={{0,1},{1,0},{2,3},{3,2},{4,5},{5,4},{6,7},{7,6},{8,9},{9,8},{10,11... | collective-permute-start | bytes 3145736 | tf_op jit(solution)/shard_map/ppermute | solution.py:20
  38.1 13.9 %collective-permute-start.4 = (bf16[128,2048]{1,0:T(8,128)(2,1)}, bf16[128,2048]{1,0:T(8,128)(2,1)S(1)}, u32[]{:S(2)}, u32[]{:S(2)}) collective-permute-start(bf16[128,2048]{1,0:T(8,128)(2,1)} %get-tuple-element.13), channel_id=1, source_target_pairs={{0,4},{4,8},{8,12},{12,14},{14,10},{10,6},{6,2},{2,0},{1,5},{5,9},... | collective-permute-start | bytes 1572872 | tf_op jit(solution)/shard_map/ppermute | solution.py:173
  39.4 13.9 %collective-permute-start.6 = (bf16[128,2048]{1,0:T(8,128)(2,1)}, bf16[128,2048]{1,0:T(8,128)(2,1)}, u32[]{:S(2)}, u32[]{:S(2)}) collective-permute-start(bf16[128,2048]{1,0:T(8,128)(2,1)} %get-tuple-element.13), channel_id=1, source_target_pairs={{4,0},{8,4},{12,8},{14,12},{10,14},{6,10},{2,6},{0,2},{5,1},{9,5},... | collective-permute-start | bytes 1572872 | tf_op jit(solution)/shard_map/ppermute | solution.py:174
  39.5 15.4 %collective-permute-start.1 = (bf16[128,2048]{1,0:T(8,128)(2,1)}, bf16[128,2048]{1,0:T(8,128)(2,1)}, u32[]{:S(2)}, u32[]{:S(2)}) collective-permute-start(bf16[128,2048]{1,0:T(8,128)(2,1)} %get-tuple-element.9), channel_id=1, source_target_pairs={{16,0},{17,1},{18,2},{19,3},{20,4},{21,5},{22,6},{23,7},{24,8},{25... | collective-permute-start | bytes 1572872 | tf_op jit(solution)/shard_map/ppermute | solution.py:157
  51.9 12.9 %collective-permute-start.5 = (bf16[128,2048]{1,0:T(8,128)(2,1)S(1)}, bf16[128,2048]{1,0:T(8,128)(2,1)}, u32[]{:S(2)}, u32[]{:S(2)}) collective-permute-start(bf16[128,2048]{1,0:T(8,128)(2,1)S(1)} %collective-permute-done.4), channel_id=1, source_target_pairs={{0,4},{4,8},{8,12},{12,14},{14,10},{10,6},{6,2},{2,0},{1,5},{5,9},... | collective-permute-start | bytes 1572872 | tf_op jit(solution)/shard_map/ppermute | solution.py:173
  53.2 12.9 %collective-permute-start.7 = (bf16[128,2048]{1,0:T(8,128)(2,1)}, bf16[128,2048]{1,0:T(8,128)(2,1)}, u32[]{:S(2)}, u32[]{:S(2)}) collective-permute-start(bf16[128,2048]{1,0:T(8,128)(2,1)} %collective-permute-done.6), channel_id=1, source_target_pairs={{4,0},{8,4},{12,8},{14,12},{10,14},{6,10},{2,6},{0,2},{5,1},{9,5},... | collective-permute-start | bytes 1572872 | tf_op jit(solution)/shard_map/ppermute | solution.py:174
  58.2 8.5 %collective-permute-start.3 = (bf16[8,8,2048]{2,1,0:T(8,128)(2,1)S(1)}, bf16[8,8,2048]{2,1,0:T(8,128)(2,1)S(1)}, u32[]{:S(2)}, u32[]{:S(2)}) collective-permute-start(bf16[8,8,2048]{2,1,0:T(8,128)(2,1)S(1)} %slice_bitcast_fusion.1), channel_id=1, source_target_pairs={{16,0},{17,1},{18,2},{19,3},{20,4},{21,5},{22,6},{23,7},{24,8},{25... | collective-permute-start | bytes 786440 | tf_op jit(solution)/shard_map/ppermute | solution.py:160
  64.8 12.2 %collective-permute-start.8 = (bf16[128,2048]{1,0:T(8,128)(2,1)}, bf16[128,2048]{1,0:T(8,128)(2,1)S(1)}, u32[]{:S(2)}, u32[]{:S(2)}) collective-permute-start(bf16[128,2048]{1,0:T(8,128)(2,1)} %collective-permute-done.5), channel_id=1, source_target_pairs={{0,4},{4,8},{8,12},{12,14},{14,10},{10,6},{6,2},{2,0},{1,5},{5,9},... | collective-permute-start | bytes 1572872 | tf_op jit(solution)/shard_map/ppermute | solution.py:173
  66.1 12.4 %collective-permute-start.9 = (bf16[128,2048]{1,0:T(8,128)(2,1)}, bf16[128,2048]{1,0:T(8,128)(2,1)}, u32[]{:S(2)}, u32[]{:S(2)}) collective-permute-start(bf16[128,2048]{1,0:T(8,128)(2,1)} %collective-permute-done.7), channel_id=1, source_target_pairs={{4,0},{8,4},{12,8},{14,12},{10,14},{6,10},{2,6},{0,2},{5,1},{9,5},... | collective-permute-start | bytes 1572872 | tf_op jit(solution)/shard_map/ppermute | solution.py:174
  67.7 33.4 %all-to-all-start = ((bf16[8,192,256]{2,1,0:T(8,128)(2,1)}), bf16[8,192,256]{2,1,0:T(8,128)(2,1)S(1)}, u32[]{:S(2)}, u32[]{:S(2)}) async-start(bf16[8,192,256]{2,1,0:T(8,128)(2,1)} %pad_maximum_fusion), calls=%async_computation | async-start | bytes 1572864 | tf_op jit(solution)/shard_map/all_to_all | solution.py:182
  77.1 21.4 %collective-permute-start.10 = (bf16[64,2048]{1,0:T(8,128)(2,1)S(1)}, bf16[64,2048]{1,0:T(8,128)(2,1)S(1)}, u32[]{:S(2)}, u32[]{:S(2)}) collective-permute-start(bf16[64,2048]{1,0:T(8,128)(2,1)S(1)} %slice.35), channel_id=1, source_target_pairs={{0,4},{4,8},{8,12},{12,14},{14,10},{10,6},{6,2},{2,0},{1,5},{5,9},... | collective-permute-start | bytes 786440 | tf_op jit(solution)/shard_map/ppermute | solution.py:189
  79.5 20.9 %collective-permute-start.11 = (bf16[64,2048]{1,0:T(8,128)(2,1)S(1)}, bf16[64,2048]{1,0:T(8,128)(2,1)S(1)}, u32[]{:S(2)}, u32[]{:S(2)}) collective-permute-start(bf16[64,2048]{1,0:T(8,128)(2,1)S(1)} %slice.36), channel_id=1, source_target_pairs={{4,0},{8,4},{12,8},{14,12},{10,14},{6,10},{2,6},{0,2},{5,1},{9,5},... | collective-permute-start | bytes 786440 | tf_op jit(solution)/shard_map/ppermute | solution.py:190
  104.1 6.4 %collective-permute-start.12 = (f32[128,2048]{1,0:T(8,128)S(1)}, f32[128,2048]{1,0:T(8,128)S(1)}, u32[]{:S(2)}, u32[]{:S(2)}) collective-permute-start(f32[128,2048]{1,0:T(8,128)S(1)} %fusion.7), channel_id=1, source_target_pairs={{0,1},{1,0},{2,3},{3,2},{4,5},{5,4},{6,7},{7,6},{8,9},{9,8},{10,11... | collective-permute-start | bytes 3145736 | tf_op jit(solution)/shard_map/ppermute | solution.py:20

commit v6 on v5

--- a/solution.py
+++ b/solution.py
@@ -188,7 +188,7 @@
         mid = rows_dev // 2
         blocks.append((lax.ppermute(fwd[:mid], "chip", up), chips // 2, 0))
         blocks.append((lax.ppermute(bwd[mid:], "chip", down), chips // 2, mid))
-    right_all = jnp.zeros((chips * rows_dev, width), BF16)
+    right_all, _ = lax.optimization_barrier((jnp.zeros((chips * rows_dev, width), BF16), rel_chip))
     for block, step, base in blocks:
         start = chip_at(place + step) * rows_dev + base
         right_all = lax.dynamic_update_slice_in_dim(right_all, block, start, 0)

time: 113 us -> 121 us (1.071)
  waiting for transfers between devices: 36.2 us -> 47.1 us
  other arithmetic: 6.18 us -> 4.95 us
    ppermute x1, waiting for transfers between devices: 1.5 us -> 13.1 us  [local(): query_back = lax.ppermute(grad_query, 'hop', [(1, 0)])]
    ppermute x1, waiting for transfers between devices: 16.1 us -> 14.7 us  [local(): blocks.append((lax.ppermute(fwd[:mid], 'chip', up), chips // 2, 0))]
    convert_element_type x1, other arithmetic: 1.34 us -> 0.1 us  [local(): (rel_keep + swap_core(rel_give)).astype(BF16)]
    unnamed x20 -> x18, local copies, waits for them, and re-layouts: 10.5 us -> 10.5 us
  transfers between devices with their start and end apart: 14 -> 14, of which waited for: 7 -> 5; matrix products, arithmetic and copies ran while one was open for 24% -> 20% of each run, Pallas kernels for 0% -> 0%
where the time goes in v6:
time: 121 us; the launch traced here: 120 us
  waiting for transfers between devices  47.1 us (39%)
  local copies, waits for them, and re-layouts  27.9 us (23%)
  starting transfers between devices  21.6 us (18%)
  Pallas kernels  11.6 us (10%)
  matrix products  6.2 us (5%)
  other arithmetic  4.95 us (4%)
    ppermute x1, waiting for transfers between devices, local(): blocks.append((lax.ppermute(fwd[:mid], 'chip', up), chips // 2, 0))  14.7 us
    ppermute x1, waiting for transfers between devices, local(): query_back = lax.ppermute(grad_query, 'hop', [(1, 0)])  13.1 us
    dynamic_update_slice x9, local copies, waits for them, and re-layouts, local(): right_all = lax.dynamic_update_slice_in_dim(right_all, block, start, 0)  12.6 us
    unnamed x18, local copies, waits for them, and re-layouts  10.5 us
    ppermute x3, waiting for transfers between devices, local(): fwd = lax.ppermute(fwd, 'chip', up)  10.1 us
    pallas_call x1, Pallas kernels, trail(): pl.pallas_call(trail_body, out_shape=(jax.ShapeDtypeStruct((rows_dev, hid...  8.75 us
    ppermute x1, waiting for transfers between devices, local(): query = lax.ppermute(own_query, 'hop', [(0, 1)])  7.79 us
    dot_general x3, matrix products, dot(): lax.dot_general(a, b, (((ca,), (cb,)), ((), ())), preferred_element_type=...  6.2 us
  transfers between devices with their start and end apart: 14, of which 5 were waited for; matrix products, arithmetic and copies ran while one was open for 20% of the time, Pallas kernels for 0%

profile of v6, /device:TPU:9, one launch (start us, length us, event | category | flops | bytes accessed | tf_op | source)
XLA Modules:
  0.0 120.2 jit_solution(16132172227046940018)
XLA Ops:
  0.7 3.5 %copy-done.1 = bf16[1,2048,2048]{2,1,0:T(8,128)(2,1)S(1)} copy-done((bf16[1,2048,2048]{2,1,0:T(8,128)(2,1)S(1)}, bf16[1,2048,2048]{2,1,0:T(8,128)(2,1)}, u32[]{:S(2)}) %copy-start.1) | copy-done | bytes 8388632
  4.1 1.0 copy-done.3
  5.2 2.9 %shard_map.67 = bf16[2,128,1024]{2,1,0:T(8,128)(2,1)S(1)} custom-call(bf16[128,2048]{1,0:T(8,128)(2,1)S(1)} %bitcast.42, bf16[2048,2048]{1,0:T(8,128)(2,1)S(1)} %bitcast.40), custom_call_target="tpu_custom_call" | custom-call | flops 1073741824 | bytes 8388608 | tf_op jit(solution)/shard_map/pallas_call | solution.py:43
  8.1 3.2 %collective-permute-start = (bf16[2,128,1024]{2,1,0:T(8,128)(2,1)S(1)}, bf16[2,128,1024]{2,1,0:T(8,128)(2,1)S(1)}, u32[]{:S(2)}, u32[]{:S(2)}) collective-permute-start(bf16[2,128,1024]{2,1,0:T(8,128)(2,1)S(1)} %shard_map.67), channel_id=1, source_target_pairs={{0,16},{1,17},{2,18},{3,19},{4,20},{5,21},{6,22},{7,23},{8,24},{9,... | collective-permute-start | bytes 1572872 | tf_op jit(solution)/shard_map/ppermute | solution.py:151
  11.2 0.3 convolution_convert_fusion
  11.6 1.0 copy.9
  12.6 1.2 %copy.10 = bf16[128,2,1024]{2,0,1:T(8,128)(2,1)S(1)} copy(bf16[128,2,1024]{0,2,1:T(8,128)(2,1)} %bitcast.48) | data formatting | bytes 1048576 | tf_op jit(solution)/shard_map/reshape | solution.py:153
  13.9 0.1 compare_convert_fusion.onehot
  14.0 7.8 %collective-permute-done.query = bf16[2,128,1024]{2,1,0:T(8,128)(2,1)S(1)} collective-permute-done((bf16[2,128,1024]{2,1,0:T(8,128)(2,1)S(1)}, bf16[2,128,1024]{2,1,0:T(8,128)(2,1)S(1)}, u32[]{:S(2)}, u32[]{:S(2)}) %collective-permute-start) | collective-permute-done | bytes 524320 | tf_op jit(solution)/shard_map/ppermute | solution.py:151
  21.8 0.8 copy-done.5
  22.6 3.4 %copy-done.2 = bf16[1,2048,2048]{2,1,0:T(8,128)(2,1)S(1)} copy-done((bf16[1,2048,2048]{2,1,0:T(8,128)(2,1)S(1)}, bf16[1,2048,2048]{2,1,0:T(8,128)(2,1)}, u32[]{:S(2)}) %copy-start.2) | copy-done | bytes 8388632
  26.0 1.0 copy-done.6
  27.0 8.8 %shard_map.68 = (bf16[128,2048]{1,0:T(8,128)(2,1)}, bf16[128,2048]{1,0:T(8,128)(2,1)}, f32[128,2048]{1,0:T(8,128)}, f32[128,2048]{1,0:T(8,128)S(1)}, bf16[128,2048]{1,0:T(8,128)(2,1)S(1)}) custom-call(s32[1]{0:T(128)} %bitcast.first, bf16[2,128,1024]{2,1,0:T(8,128)(2,1)S(1)} %copy-done.6, bf16[128,2048]{1,0:T(8,128)(2,1)S(1)} %bitcast.43, ...), custom_call_target="tpu_custom_call" | custom-call | flops 2415919104 | bytes 16777216 | tf_op jit(solution)/shard_map/pallas_call | solution.py:105
  35.7 0.8 copy-done.7
  36.6 1.5 %collective-permute-start.2 = (f32[128,2048]{1,0:T(8,128)}, f32[128,2048]{1,0:T(8,128)S(1)}, u32[]{:S(2)}, u32[]{:S(2)}) collective-permute-start(f32[128,2048]{1,0:T(8,128)} %get-tuple-element.13), channel_id=1, source_target_pairs={{0,1},{1,0},{2,3},{3,2},{4,5},{5,4},{6,7},{7,6},{8,9},{9,8},{10,11... | collective-permute-start | bytes 3145736 | tf_op jit(solution)/shard_map/ppermute | solution.py:20
  38.1 1.3 %collective-permute-start.1 = (bf16[128,2048]{1,0:T(8,128)(2,1)}, bf16[128,2048]{1,0:T(8,128)(2,1)}, u32[]{:S(2)}, u32[]{:S(2)}) collective-permute-start(bf16[128,2048]{1,0:T(8,128)(2,1)} %get-tuple-element.10), channel_id=1, source_target_pairs={{16,0},{17,1},{18,2},{19,3},{20,4},{21,5},{22,6},{23,7},{24,8},{25... | collective-permute-start | bytes 1572872 | tf_op jit(solution)/shard_map/ppermute | solution.py:157
  39.4 1.3 %collective-permute-start.4 = (bf16[128,2048]{1,0:T(8,128)(2,1)}, bf16[128,2048]{1,0:T(8,128)(2,1)}, u32[]{:S(2)}, u32[]{:S(2)}) collective-permute-start(bf16[128,2048]{1,0:T(8,128)(2,1)} %get-tuple-element.14), channel_id=1, source_target_pairs={{0,4},{4,8},{8,12},{12,14},{14,10},{10,6},{6,2},{2,0},{1,5},{5,9},... | collective-permute-start | bytes 1572872 | tf_op jit(solution)/shard_map/ppermute | solution.py:173
  40.7 0.2 collective-permute-start.6
  40.9 13.1 %collective-permute-done.1 = bf16[128,2048]{1,0:T(8,128)(2,1)} collective-permute-done((bf16[128,2048]{1,0:T(8,128)(2,1)}, bf16[128,2048]{1,0:T(8,128)(2,1)}, u32[]{:S(2)}, u32[]{:S(2)}) %collective-permute-start.1) | collective-permute-done | bytes 524320 | tf_op jit(solution)/shard_map/ppermute | solution.py:157
  54.0 1.9 %broadcast_select_fusion = (bf16[128,2048]{1,0:T(8,128)(2,1)}, bf16[128,2048]{1,0:T(8,128)(2,1)S(1)}) fusion(bf16[128,2048]{1,0:T(8,128)(2,1)} %collective-permute-done.1, bf16[128,2048]{1,0:T(8,128)(2,1)} %get-tuple-element.10, pred[]{:T(512)S(6)} %eq.49, bf16[128,2048]{1,0:T(8,128)(2,1)} %copy-done.7), kind=kLoop, calls=%fused_computation.6 | loop fusion | flops 524288 | bytes 2621441 | tf_op jit(solution)/shard_map/jit(_where)/select_n | solution.py:158
  56.0 1.3 %collective-permute-start.5 = (bf16[128,2048]{1,0:T(8,128)(2,1)}, bf16[128,2048]{1,0:T(8,128)(2,1)}, u32[]{:S(2)}, u32[]{:S(2)}) collective-permute-start(bf16[128,2048]{1,0:T(8,128)(2,1)} %collective-permute-done.4), channel_id=1, source_target_pairs={{0,4},{4,8},{8,12},{12,14},{14,10},{10,6},{6,2},{2,0},{1,5},{5,9},... | collective-permute-start | bytes 1572872 | tf_op jit(solution)/shard_map/ppermute | solution.py:173
  57.3 0.2 collective-permute-start.7
  57.5 0.1 add_convert_fusion
  57.7 1.3 %collective-permute-start.3 = (bf16[8,8,2048]{2,1,0:T(8,128)(2,1)S(1)}, bf16[8,8,2048]{2,1,0:T(8,128)(2,1)S(1)}, u32[]{:S(2)}, u32[]{:S(2)}) collective-permute-start(bf16[8,8,2048]{2,1,0:T(8,128)(2,1)S(1)} %slice_bitcast_fusion.1), channel_id=1, source_target_pairs={{16,0},{17,1},{18,2},{19,3},{20,4},{21,5},{22,6},{23,7},{24,8},{25... | collective-permute-start | bytes 786440 | tf_op jit(solution)/shard_map/ppermute | solution.py:160
  59.0 10.1 %collective-permute-done.5 = bf16[128,2048]{1,0:T(8,128)(2,1)} collective-permute-done((bf16[128,2048]{1,0:T(8,128)(2,1)}, bf16[128,2048]{1,0:T(8,128)(2,1)}, u32[]{:S(2)}, u32[]{:S(2)}) %collective-permute-start.5) | collective-permute-done | bytes 524320 | tf_op jit(solution)/shard_map/ppermute | solution.py:173
  69.1 1.3 %collective-permute-start.8 = (bf16[128,2048]{1,0:T(8,128)(2,1)}, bf16[128,2048]{1,0:T(8,128)(2,1)S(1)}, u32[]{:S(2)}, u32[]{:S(2)}) collective-permute-start(bf16[128,2048]{1,0:T(8,128)(2,1)} %collective-permute-done.5), channel_id=1, source_target_pairs={{0,4},{4,8},{8,12},{12,14},{14,10},{10,6},{6,2},{2,0},{1,5},{5,9},... | collective-permute-start | bytes 1572872 | tf_op jit(solution)/shard_map/ppermute | solution.py:173
  70.4 2.5 %broadcast_in_dim.20 = bf16[1024,2048]{1,0:T(8,128)(2,1)} broadcast(bf16[]{:T(256)} %constant.138.clone.1), dimensions={} | broadcast | bytes 4194306 | tf_op jit(solution)/shard_map/broadcast_in_dim | solution.py:191
  72.8 1.9 %constant_dynamic-update-slice_fusion.8 = bf16[1024,2048]{1,0:T(8,128)(2,1)} fusion(bf16[1024,2048]{1,0:T(8,128)(2,1)} %broadcast_in_dim.20, bf16[128,2048]{1,0:T(8,128)(2,1)} %get-tuple-element.14, s32[]{:T(128)S(6)} %select_n.166), kind=kLoop, calls=%fused_computation.25 | loop fusion | bytes 1048580 | tf_op jit(solution)/shard_map/dynamic_update_slice | solution.py:194
  74.7 0.2 collective-permute-start.9
  74.9 1.9 %constant_dynamic-update-slice_fusion.7 = bf16[1024,2048]{1,0:T(8,128)(2,1)} fusion(bf16[1024,2048]{1,0:T(8,128)(2,1)} %constant_dynamic-update-slice_fusion.8, bf16[128,2048]{1,0:T(8,128)(2,1)} %collective-permute-done.4, s32[]{:T(128)S(6)} %select_n.168), kind=kLoop, calls=%fused_computation.24 | loop fusion | bytes 1048580 | tf_op jit(solution)/shard_map/dynamic_update_slice | solution.py:194
  76.8 1.9 %constant_dynamic-update-slice_fusion.6 = bf16[1024,2048]{1,0:T(8,128)(2,1)} fusion(bf16[1024,2048]{1,0:T(8,128)(2,1)} %constant_dynamic-update-slice_fusion.7, bf16[128,2048]{1,0:T(8,128)(2,1)} %collective-permute-done.6, s32[]{:T(128)S(6)} %select_n.170), kind=kLoop, calls=%fused_computation.23 | loop fusion | bytes 1048580 | tf_op jit(solution)/shard_map/dynamic_update_slice | solution.py:194
  78.7 0.9 pad_maximum_fusion
  79.7 5.7 %all-to-all-start = ((bf16[8,192,256]{2,1,0:T(8,128)(2,1)}), bf16[8,192,256]{2,1,0:T(8,128)(2,1)S(1)}, u32[]{:S(2)}, u32[]{:S(2)}) async-start(bf16[8,192,256]{2,1,0:T(8,128)(2,1)} %pad_maximum_fusion), calls=%async_computation | async-start | bytes 1572864 | tf_op jit(solution)/shard_map/all_to_all | solution.py:182
  85.4 1.9 %constant_dynamic-update-slice_fusion.5 = bf16[1024,2048]{1,0:T(8,128)(2,1)} fusion(bf16[1024,2048]{1,0:T(8,128)(2,1)} %constant_dynamic-update-slice_fusion.6, bf16[128,2048]{1,0:T(8,128)(2,1)} %collective-permute-done.5, s32[]{:T(128)S(6)} %select_n.172), kind=kLoop, calls=%fused_computation.22 | loop fusion | bytes 1048580 | tf_op jit(solution)/shard_map/dynamic_update_slice | solution.py:194
  87.3 1.9 %constant_dynamic-update-slice_fusion.4 = bf16[1024,2048]{1,0:T(8,128)(2,1)} fusion(bf16[1024,2048]{1,0:T(8,128)(2,1)} %constant_dynamic-update-slice_fusion.5, bf16[128,2048]{1,0:T(8,128)(2,1)} %collective-permute-done.7, s32[]{:T(128)S(6)} %select_n.174), kind=kLoop, calls=%fused_computation.21 | loop fusion | bytes 1048580 | tf_op jit(solution)/shard_map/dynamic_update_slice | solution.py:194
  89.2 1.2 %collective-permute-start.10 = (bf16[64,2048]{1,0:T(8,128)(2,1)S(1)}, bf16[64,2048]{1,0:T(8,128)(2,1)S(1)}, u32[]{:S(2)}, u32[]{:S(2)}) collective-permute-start(bf16[64,2048]{1,0:T(8,128)(2,1)S(1)} %slice.35), channel_id=1, source_target_pairs={{0,4},{4,8},{8,12},{12,14},{14,10},{10,6},{6,2},{2,0},{1,5},{5,9},... | collective-permute-start | bytes 786440 | tf_op jit(solution)/shard_map/ppermute | solution.py:189
  90.4 0.3 collective-permute-start.11
  90.8 0.8 constant_dynamic-update-slice_fusion.3
  91.6 0.8 constant_dynamic-update-slice_fusion.2
  92.4 14.7 %collective-permute-done.10 = bf16[64,2048]{1,0:T(8,128)(2,1)S(1)} collective-permute-done((bf16[64,2048]{1,0:T(8,128)(2,1)S(1)}, bf16[64,2048]{1,0:T(8,128)(2,1)S(1)}, u32[]{:S(2)}, u32[]{:S(2)}) %collective-permute-start.10) | collective-permute-done | bytes 262176 | tf_op jit(solution)/shard_map/ppermute | solution.py:189
  107.1 0.7 constant_dynamic-update-slice_fusion.1
  107.8 1.4 %collective-permute-done.11 = bf16[64,2048]{1,0:T(8,128)(2,1)S(1)} collective-permute-done((bf16[64,2048]{1,0:T(8,128)(2,1)S(1)}, bf16[64,2048]{1,0:T(8,128)(2,1)S(1)}, u32[]{:S(2)}, u32[]{:S(2)}) %collective-permute-start.11) | collective-permute-done | bytes 262176 | tf_op jit(solution)/shard_map/ppermute | solution.py:190
  109.2 0.7 constant_dynamic-update-slice_fusion
  110.0 2.9 %fusion.7 = f32[128,2048]{1,0:T(8,128)S(1)} fusion(bf16[1024,128]{1,0:T(8,128)(2,1)S(1)} %bitcast.52, bf16[1024,2048]{1,0:T(8,128)(2,1)} %constant_dynamic-update-slice_fusion), kind=kOutput, calls=%fused_computation.48 | convolution fusion | flops 536870912 | bytes 5505024 | tf_op jit(solution)/shard_map/dot_general | solution.py:16
  112.9 2.6 %collective-permute-start.12 = (f32[128,2048]{1,0:T(8,128)S(1)}, f32[128,2048]{1,0:T(8,128)S(1)}, u32[]{:S(2)}, u32[]{:S(2)}) collective-permute-start(f32[128,2048]{1,0:T(8,128)S(1)} %fusion.7), channel_id=1, source_target_pairs={{0,1},{1,0},{2,3},{3,2},{4,5},{5,4},{6,7},{7,6},{8,9},{9,8},{10,11... | collective-permute-start | bytes 3145736 | tf_op jit(solution)/shard_map/ppermute | solution.py:20
  115.5 2.9 %fusion.6 = f32[128,2048]{1,0:T(8,128)S(1)} fusion(bf16[1024,128]{1,0:T(8,128)(2,1)S(1)} %bitcast.51, bf16[1024,2048]{1,0:T(8,128)(2,1)} %constant_dynamic-update-slice_fusion), kind=kOutput, calls=%fused_computation.47 | convolution fusion | flops 536870912 | bytes 5505024 | tf_op jit(solution)/shard_map/dot_general | solution.py:16
  118.5 0.6 broadcast_multiply_fusion
  119.1 1.1 multiply_bitcast_fusion
  (29 shorter events, 0.3 us)
Async XLA Ops:
  0.6 10.6 %copy-start = (bf16[256,2048]{1,0:T(8,128)(2,1)S(1)}, bf16[256,2048]{1,0:T(8,128)(2,1)}, u32[]{:S(2)}) copy-start(bf16[256,2048]{1,0:T(8,128)(2,1)} %param.6) | copy-start | bytes 3145732
  0.6 3.5 %copy-start.1 = (bf16[1,2048,2048]{2,1,0:T(8,128)(2,1)S(1)}, bf16[1,2048,2048]{2,1,0:T(8,128)(2,1)}, u32[]{:S(2)}) copy-start(bf16[1,2048,2048]{2,1,0:T(8,128)(2,1)} %param.5) | copy-start | bytes 25165828
  4.1 1.0 copy-start.3
  5.2 6.1 %copy-start.8 = (s32[128]{0:T(128)S(1)}, s32[128]{0:T(128)}, u32[]{:S(2)}) copy-start(s32[128]{0:T(128)} %param.7) | copy-start | bytes 1540
  5.2 17.4 %copy-start.4 = (bf16[1,128,2048]{2,1,0:T(8,128)(2,1)S(1)}, bf16[1,128,2048]{2,1,0:T(8,128)(2,1)}, u32[]{:S(2)}) copy-start(bf16[1,128,2048]{2,1,0:T(8,128)(2,1)} %param.4) | copy-start | bytes 1572868
  8.1 13.7 %collective-permute-start = (bf16[2,128,1024]{2,1,0:T(8,128)(2,1)S(1)}, bf16[2,128,1024]{2,1,0:T(8,128)(2,1)S(1)}, u32[]{:S(2)}, u32[]{:S(2)}) collective-permute-start(bf16[2,128,1024]{2,1,0:T(8,128)(2,1)S(1)} %shard_map.67), channel_id=1, source_target_pairs={{0,16},{1,17},{2,18},{3,19},{4,20},{5,21},{6,22},{7,23},{8,24},{9,... | collective-permute-start | bytes 1572872 | tf_op jit(solution)/shard_map/ppermute | solution.py:151
  21.8 0.8 copy-start.5
  22.6 3.4 %copy-start.2 = (bf16[1,2048,2048]{2,1,0:T(8,128)(2,1)S(1)}, bf16[1,2048,2048]{2,1,0:T(8,128)(2,1)}, u32[]{:S(2)}) copy-start(bf16[1,2048,2048]{2,1,0:T(8,128)(2,1)} %param.5) | copy-start | bytes 25165828
  25.9 1.0 copy-start.6
  35.7 0.8 copy-start.7
  36.6 21.0 %collective-permute-start.2 = (f32[128,2048]{1,0:T(8,128)}, f32[128,2048]{1,0:T(8,128)S(1)}, u32[]{:S(2)}, u32[]{:S(2)}) collective-permute-start(f32[128,2048]{1,0:T(8,128)} %get-tuple-element.13), channel_id=1, source_target_pairs={{0,1},{1,0},{2,3},{3,2},{4,5},{5,4},{6,7},{7,6},{8,9},{9,8},{10,11... | collective-permute-start | bytes 3145736 | tf_op jit(solution)/shard_map/ppermute | solution.py:20
  38.1 15.9 %collective-permute-start.1 = (bf16[128,2048]{1,0:T(8,128)(2,1)}, bf16[128,2048]{1,0:T(8,128)(2,1)}, u32[]{:S(2)}, u32[]{:S(2)}) collective-permute-start(bf16[128,2048]{1,0:T(8,128)(2,1)} %get-tuple-element.10), channel_id=1, source_target_pairs={{16,0},{17,1},{18,2},{19,3},{20,4},{21,5},{22,6},{23,7},{24,8},{25... | collective-permute-start | bytes 1572872 | tf_op jit(solution)/shard_map/ppermute | solution.py:157
  39.4 16.6 %collective-permute-start.4 = (bf16[128,2048]{1,0:T(8,128)(2,1)}, bf16[128,2048]{1,0:T(8,128)(2,1)}, u32[]{:S(2)}, u32[]{:S(2)}) collective-permute-start(bf16[128,2048]{1,0:T(8,128)(2,1)} %get-tuple-element.14), channel_id=1, source_target_pairs={{0,4},{4,8},{8,12},{12,14},{14,10},{10,6},{6,2},{2,0},{1,5},{5,9},... | collective-permute-start | bytes 1572872 | tf_op jit(solution)/shard_map/ppermute | solution.py:173
  40.7 16.6 %collective-permute-start.6 = (bf16[128,2048]{1,0:T(8,128)(2,1)}, bf16[128,2048]{1,0:T(8,128)(2,1)}, u32[]{:S(2)}, u32[]{:S(2)}) collective-permute-start(bf16[128,2048]{1,0:T(8,128)(2,1)} %get-tuple-element.14), channel_id=1, source_target_pairs={{4,0},{8,4},{12,8},{14,12},{10,14},{6,10},{2,6},{0,2},{5,1},{9,5},... | collective-permute-start | bytes 1572872 | tf_op jit(solution)/shard_map/ppermute | solution.py:174
  56.0 13.1 %collective-permute-start.5 = (bf16[128,2048]{1,0:T(8,128)(2,1)}, bf16[128,2048]{1,0:T(8,128)(2,1)}, u32[]{:S(2)}, u32[]{:S(2)}) collective-permute-start(bf16[128,2048]{1,0:T(8,128)(2,1)} %collective-permute-done.4), channel_id=1, source_target_pairs={{0,4},{4,8},{8,12},{12,14},{14,10},{10,6},{6,2},{2,0},{1,5},{5,9},... | collective-permute-start | bytes 1572872 | tf_op jit(solution)/shard_map/ppermute | solution.py:173
  57.3 17.4 %collective-permute-start.7 = (bf16[128,2048]{1,0:T(8,128)(2,1)}, bf16[128,2048]{1,0:T(8,128)(2,1)}, u32[]{:S(2)}, u32[]{:S(2)}) collective-permute-start(bf16[128,2048]{1,0:T(8,128)(2,1)} %collective-permute-done.6), channel_id=1, source_target_pairs={{4,0},{8,4},{12,8},{14,12},{10,14},{6,10},{2,6},{0,2},{5,1},{9,5},... | collective-permute-start | bytes 1572872 | tf_op jit(solution)/shard_map/ppermute | solution.py:174
  57.7 21.0 %collective-permute-start.3 = (bf16[8,8,2048]{2,1,0:T(8,128)(2,1)S(1)}, bf16[8,8,2048]{2,1,0:T(8,128)(2,1)S(1)}, u32[]{:S(2)}, u32[]{:S(2)}) collective-permute-start(bf16[8,8,2048]{2,1,0:T(8,128)(2,1)S(1)} %slice_bitcast_fusion.1), channel_id=1, source_target_pairs={{16,0},{17,1},{18,2},{19,3},{20,4},{21,5},{22,6},{23,7},{24,8},{25... | collective-permute-start | bytes 786440 | tf_op jit(solution)/shard_map/ppermute | solution.py:160
  69.1 20.1 %collective-permute-start.8 = (bf16[128,2048]{1,0:T(8,128)(2,1)}, bf16[128,2048]{1,0:T(8,128)(2,1)S(1)}, u32[]{:S(2)}, u32[]{:S(2)}) collective-permute-start(bf16[128,2048]{1,0:T(8,128)(2,1)} %collective-permute-done.5), channel_id=1, source_target_pairs={{0,4},{4,8},{8,12},{12,14},{14,10},{10,6},{6,2},{2,0},{1,5},{5,9},... | collective-permute-start | bytes 1572872 | tf_op jit(solution)/shard_map/ppermute | solution.py:173
  74.7 15.7 %collective-permute-start.9 = (bf16[128,2048]{1,0:T(8,128)(2,1)}, bf16[128,2048]{1,0:T(8,128)(2,1)S(1)}, u32[]{:S(2)}, u32[]{:S(2)}) collective-permute-start(bf16[128,2048]{1,0:T(8,128)(2,1)} %collective-permute-done.7), channel_id=1, source_target_pairs={{4,0},{8,4},{12,8},{14,12},{10,14},{6,10},{2,6},{0,2},{5,1},{9,5},... | collective-permute-start | bytes 1572872 | tf_op jit(solution)/shard_map/ppermute | solution.py:174
  79.7 30.3 %all-to-all-start = ((bf16[8,192,256]{2,1,0:T(8,128)(2,1)}), bf16[8,192,256]{2,1,0:T(8,128)(2,1)S(1)}, u32[]{:S(2)}, u32[]{:S(2)}) async-start(bf16[8,192,256]{2,1,0:T(8,128)(2,1)} %pad_maximum_fusion), calls=%async_computation | async-start | bytes 1572864 | tf_op jit(solution)/shard_map/all_to_all | solution.py:182
  89.2 17.9 %collective-permute-start.10 = (bf16[64,2048]{1,0:T(8,128)(2,1)S(1)}, bf16[64,2048]{1,0:T(8,128)(2,1)S(1)}, u32[]{:S(2)}, u32[]{:S(2)}) collective-permute-start(bf16[64,2048]{1,0:T(8,128)(2,1)S(1)} %slice.35), channel_id=1, source_target_pairs={{0,4},{4,8},{8,12},{12,14},{14,10},{10,6},{6,2},{2,0},{1,5},{5,9},... | collective-permute-start | bytes 786440 | tf_op jit(solution)/shard_map/ppermute | solution.py:189
  90.4 18.8 %collective-permute-start.11 = (bf16[64,2048]{1,0:T(8,128)(2,1)S(1)}, bf16[64,2048]{1,0:T(8,128)(2,1)S(1)}, u32[]{:S(2)}, u32[]{:S(2)}) collective-permute-start(bf16[64,2048]{1,0:T(8,128)(2,1)S(1)} %slice.36), channel_id=1, source_target_pairs={{4,0},{8,4},{12,8},{14,12},{10,14},{6,10},{2,6},{0,2},{5,1},{9,5},... | collective-permute-start | bytes 786440 | tf_op jit(solution)/shard_map/ppermute | solution.py:190
  112.9 6.2 %collective-permute-start.12 = (f32[128,2048]{1,0:T(8,128)S(1)}, f32[128,2048]{1,0:T(8,128)S(1)}, u32[]{:S(2)}, u32[]{:S(2)}) collective-permute-start(f32[128,2048]{1,0:T(8,128)S(1)} %fusion.7), channel_id=1, source_target_pairs={{0,1},{1,0},{2,3},{3,2},{4,5},{5,4},{6,7},{7,6},{8,9},{9,8},{10,11... | collective-permute-start | bytes 3145736 | tf_op jit(solution)/shard_map/ppermute | solution.py:20

commit v7 on v5

--- a/solution.py
+++ b/solution.py
@@ -155,8 +155,9 @@
         first.astype(jnp.int32).reshape(1), query, rows, weight, rel, onehot_t
     )
     query_back = lax.ppermute(grad_query, "hop", [(1, 0)])
+    rel_chip = (rel_keep + swap_core(rel_give)).astype(BF16).reshape(chips, 2, owned, width)
+    query_back, _ = lax.optimization_barrier((query_back, rel_chip))
     query_grad = jnp.where(first, query_back, grad_query)
-    rel_chip = (rel_keep + swap_core(rel_give)).astype(BF16).reshape(chips, 2, owned, width)
     rel_back = lax.ppermute(rel_chip[:, 0], "hop", [(1, 0)])
 
     def chip_at(place):

time: 113 us -> 113 us (level)
  waiting for transfers between devices: 36.2 us -> 44.5 us
  local copies, waits for them, and re-layouts: 28.8 us -> 24.4 us
  other arithmetic: 6.18 us -> 3.9 us
  matrix products: 6.2 us -> 4.16 us
    ppermute x3, waiting for transfers between devices: 9.13 us -> 16.3 us  [local(): fwd = lax.ppermute(fwd, 'chip', up)]
    dynamic_update_slice x9, local copies, waits for them, and re-layouts: 12.5 us -> 10.2 us  [local(): right_all = lax.dynamic_update_slice_in_dim(right_all, block, start, 0)]
    ppermute x1, waiting for transfers between devices: 16.1 us -> 18.3 us  [local(): blocks.append((lax.ppermute(fwd[:mid], 'chip', up), chips // 2, 0))]
    dot_general x3, matrix products: 6.2 us -> 4.16 us  [dot(): lax.dot_general(a, b, (((ca,), (cb,)), ((), ())), preferred_element_type=...]
    broadcast_in_dim x1, local copies, waits for them, and re-layouts: 2.47 us -> 0.51 us  [local(): right_all = jnp.zeros((chips * rows_dev, width), BF16)]
    ppermute x1, waiting for transfers between devices: 1.5 us -> 0.01 us  [local(): query_back = lax.ppermute(grad_query, 'hop', [(1, 0)])]
    convert_element_type x1, other arithmetic: 1.34 us -> 0.11 us  [local(): (rel_keep + swap_core(rel_give)).astype(BF16)]
    unnamed x20 -> x28, local copies, waits for them, and re-layouts: 10.5 us -> 11.4 us
  transfers between devices with their start and end apart: 14 -> 14, of which waited for: 7 -> 6; matrix products, arithmetic and copies ran while one was open for 24% -> 15% of each run, Pallas kernels for 0% -> 0%
where the time goes in v7:
time: 113 us; the launch traced here: 111 us
  waiting for transfers between devices  44.5 us (39%)
  local copies, waits for them, and re-layouts  24.4 us (22%)
  starting transfers between devices  21.9 us (19%)
  Pallas kernels  11.6 us (10%)
  matrix products  4.16 us (4%)
  other arithmetic  3.9 us (3%)
    ppermute x1, waiting for transfers between devices, local(): blocks.append((lax.ppermute(fwd[:mid], 'chip', up), chips // 2, 0))  18.3 us
    ppermute x3, waiting for transfers between devices, local(): fwd = lax.ppermute(fwd, 'chip', up)  16.3 us
    unnamed x28, local copies, waits for them, and re-layouts  11.4 us
    dynamic_update_slice x9, local copies, waits for them, and re-layouts, local(): right_all = lax.dynamic_update_slice_in_dim(right_all, block, start, 0)  10.2 us
    pallas_call x1, Pallas kernels, trail(): pl.pallas_call(trail_body, out_shape=(jax.ShapeDtypeStruct((rows_dev, hid...  8.75 us
    ppermute x1, waiting for transfers between devices, local(): query = lax.ppermute(own_query, 'hop', [(0, 1)])  7.79 us
    all_to_all x1, starting transfers between devices, local(): received = lax.all_to_all(sent, 'chip', 0, 0, tiled=True)  5.71 us
    ppermute x2, starting transfers between devices, swap_core(): return lax.ppermute(block, 'core', [(0, 1), (1, 0)])  4.48 us
  transfers between devices with their start and end apart: 14, of which 6 were waited for; matrix products, arithmetic and copies ran while one was open for 15% of the time, Pallas kernels for 0%

profile of v7, /device:TPU:9, one launch (start us, length us, event | category | flops | bytes accessed | tf_op | source)
XLA Modules:
  0.0 111.4 jit_solution(250795145131881064)
XLA Ops:
  0.7 3.5 %copy-done.1 = bf16[1,2048,2048]{2,1,0:T(8,128)(2,1)S(1)} copy-done((bf16[1,2048,2048]{2,1,0:T(8,128)(2,1)S(1)}, bf16[1,2048,2048]{2,1,0:T(8,128)(2,1)}, u32[]{:S(2)}) %copy-start.1) | copy-done | bytes 8388632
  4.1 1.0 copy-done.3
  5.2 2.9 %shard_map.67 = bf16[2,128,1024]{2,1,0:T(8,128)(2,1)S(1)} custom-call(bf16[128,2048]{1,0:T(8,128)(2,1)S(1)} %bitcast.42, bf16[2048,2048]{1,0:T(8,128)(2,1)S(1)} %bitcast.40), custom_call_target="tpu_custom_call" | custom-call | flops 1073741824 | bytes 8388608 | tf_op jit(solution)/shard_map/pallas_call | solution.py:43
  8.1 3.2 %collective-permute-start = (bf16[2,128,1024]{2,1,0:T(8,128)(2,1)S(1)}, bf16[2,128,1024]{2,1,0:T(8,128)(2,1)S(1)}, u32[]{:S(2)}, u32[]{:S(2)}) collective-permute-start(bf16[2,128,1024]{2,1,0:T(8,128)(2,1)S(1)} %shard_map.67), channel_id=1, source_target_pairs={{0,16},{1,17},{2,18},{3,19},{4,20},{5,21},{6,22},{7,23},{8,24},{9,... | collective-permute-start | bytes 1572872 | tf_op jit(solution)/shard_map/ppermute | solution.py:151
  11.2 0.3 convolution_convert_fusion
  11.6 1.0 copy.9
  12.6 1.2 %copy.10 = bf16[128,2,1024]{2,0,1:T(8,128)(2,1)S(1)} copy(bf16[128,2,1024]{0,2,1:T(8,128)(2,1)} %bitcast.48) | data formatting | bytes 1048576 | tf_op jit(solution)/shard_map/reshape | solution.py:153
  14.0 7.8 %collective-permute-done.query = bf16[2,128,1024]{2,1,0:T(8,128)(2,1)S(1)} collective-permute-done((bf16[2,128,1024]{2,1,0:T(8,128)(2,1)S(1)}, bf16[2,128,1024]{2,1,0:T(8,128)(2,1)S(1)}, u32[]{:S(2)}, u32[]{:S(2)}) %collective-permute-start) | collective-permute-done | bytes 524320 | tf_op jit(solution)/shard_map/ppermute | solution.py:151
  21.8 0.8 copy-done.5
  22.6 3.4 %copy-done.2 = bf16[1,2048,2048]{2,1,0:T(8,128)(2,1)S(1)} copy-done((bf16[1,2048,2048]{2,1,0:T(8,128)(2,1)S(1)}, bf16[1,2048,2048]{2,1,0:T(8,128)(2,1)}, u32[]{:S(2)}) %copy-start.2) | copy-done | bytes 8388632
  26.0 1.0 copy-done.6
  27.0 8.8 %shard_map.68 = (bf16[128,2048]{1,0:T(8,128)(2,1)}, bf16[128,2048]{1,0:T(8,128)(2,1)S(1)}, f32[128,2048]{1,0:T(8,128)}, f32[128,2048]{1,0:T(8,128)S(1)}, bf16[128,2048]{1,0:T(8,128)(2,1)S(1)}) custom-call(s32[1]{0:T(128)} %bitcast.first, bf16[2,128,1024]{2,1,0:T(8,128)(2,1)S(1)} %copy-done.6, bf16[128,2048]{1,0:T(8,128)(2,1)S(1)} %bitcast.43, ...), custom_call_target="tpu_custom_call" | custom-call | flops 2415919104 | bytes 16777216 | tf_op jit(solution)/shard_map/pallas_call | solution.py:105
  35.7 0.8 copy-done.7
  36.5 0.8 copy-done.9
  37.4 1.5 %collective-permute-start.2 = (f32[128,2048]{1,0:T(8,128)}, f32[128,2048]{1,0:T(8,128)S(1)}, u32[]{:S(2)}, u32[]{:S(2)}) collective-permute-start(f32[128,2048]{1,0:T(8,128)} %get-tuple-element.12), channel_id=1, source_target_pairs={{0,1},{1,0},{2,3},{3,2},{4,5},{5,4},{6,7},{7,6},{8,9},{9,8},{10,11... | collective-permute-start | bytes 3145736 | tf_op jit(solution)/shard_map/ppermute | solution.py:20
  38.9 1.3 %collective-permute-start.4 = (bf16[128,2048]{1,0:T(8,128)(2,1)}, bf16[128,2048]{1,0:T(8,128)(2,1)}, u32[]{:S(2)}, u32[]{:S(2)}) collective-permute-start(bf16[128,2048]{1,0:T(8,128)(2,1)} %get-tuple-element.15), channel_id=1, source_target_pairs={{0,4},{4,8},{8,12},{12,14},{14,10},{10,6},{6,2},{2,0},{1,5},{5,9},... | collective-permute-start | bytes 1572872 | tf_op jit(solution)/shard_map/ppermute | solution.py:174
  40.2 0.2 collective-permute-start.6
  40.4 1.3 %collective-permute-start.1 = (bf16[128,2048]{1,0:T(8,128)(2,1)}, bf16[128,2048]{1,0:T(8,128)(2,1)S(1)}, u32[]{:S(2)}, u32[]{:S(2)}) collective-permute-start(bf16[128,2048]{1,0:T(8,128)(2,1)} %copy-done.7), channel_id=1, source_target_pairs={{16,0},{17,1},{18,2},{19,3},{20,4},{21,5},{22,6},{23,7},{24,8},{25... | collective-permute-start | bytes 1572872 | tf_op jit(solution)/shard_map/ppermute | solution.py:157
  41.6 0.5 broadcast_in_dim.20
  42.2 1.2 %constant_dynamic-update-slice_fusion.8 = bf16[1024,2048]{1,0:T(8,128)(2,1)S(1)} fusion(bf16[1024,2048]{1,0:T(8,128)(2,1)S(1)} %broadcast_in_dim.20, bf16[128,2048]{1,0:T(8,128)(2,1)} %get-tuple-element.15, s32[]{:T(128)S(6)} %select_n.166), kind=kLoop, calls=%fused_computation.25 | loop fusion | bytes 1048580 | tf_op jit(solution)/shard_map/dynamic_update_slice | solution.py:195
  43.4 9.4 %collective-permute-done.4 = bf16[128,2048]{1,0:T(8,128)(2,1)} collective-permute-done((bf16[128,2048]{1,0:T(8,128)(2,1)}, bf16[128,2048]{1,0:T(8,128)(2,1)}, u32[]{:S(2)}, u32[]{:S(2)}) %collective-permute-start.4) | collective-permute-done | bytes 524320 | tf_op jit(solution)/shard_map/ppermute | solution.py:174
  52.8 1.3 %collective-permute-start.5 = (bf16[128,2048]{1,0:T(8,128)(2,1)}, bf16[128,2048]{1,0:T(8,128)(2,1)}, u32[]{:S(2)}, u32[]{:S(2)}) collective-permute-start(bf16[128,2048]{1,0:T(8,128)(2,1)} %collective-permute-done.4), channel_id=1, source_target_pairs={{0,4},{4,8},{8,12},{12,14},{14,10},{10,6},{6,2},{2,0},{1,5},{5,9},... | collective-permute-start | bytes 1572872 | tf_op jit(solution)/shard_map/ppermute | solution.py:174
  54.1 0.2 collective-permute-start.7
  54.2 1.1 constant_dynamic-update-slice_fusion.7
  55.3 1.1 constant_dynamic-update-slice_fusion.6
  56.6 1.3 %collective-permute-start.3 = (bf16[8,8,2048]{2,1,0:T(8,128)(2,1)S(1)}, bf16[8,8,2048]{2,1,0:T(8,128)(2,1)S(1)}, u32[]{:S(2)}, u32[]{:S(2)}) collective-permute-start(bf16[8,8,2048]{2,1,0:T(8,128)(2,1)S(1)} %slice_bitcast_fusion.1), channel_id=1, source_target_pairs={{16,0},{17,1},{18,2},{19,3},{20,4},{21,5},{22,6},{23,7},{24,8},{25... | collective-permute-start | bytes 786440 | tf_op jit(solution)/shard_map/ppermute | solution.py:161
  57.9 0.9 broadcast_select_fusion
  58.8 6.9 %collective-permute-done.5 = bf16[128,2048]{1,0:T(8,128)(2,1)} collective-permute-done((bf16[128,2048]{1,0:T(8,128)(2,1)}, bf16[128,2048]{1,0:T(8,128)(2,1)}, u32[]{:S(2)}, u32[]{:S(2)}) %collective-permute-start.5) | collective-permute-done | bytes 524320 | tf_op jit(solution)/shard_map/ppermute | solution.py:174
  65.7 1.3 %collective-permute-start.8 = (bf16[128,2048]{1,0:T(8,128)(2,1)}, bf16[128,2048]{1,0:T(8,128)(2,1)S(1)}, u32[]{:S(2)}, u32[]{:S(2)}) collective-permute-start(bf16[128,2048]{1,0:T(8,128)(2,1)} %collective-permute-done.5), channel_id=1, source_target_pairs={{0,4},{4,8},{8,12},{12,14},{14,10},{10,6},{6,2},{2,0},{1,5},{5,9},... | collective-permute-start | bytes 1572872 | tf_op jit(solution)/shard_map/ppermute | solution.py:174
  67.0 0.2 collective-permute-start.9
  67.3 0.9 pad_maximum_fusion
  68.2 5.7 %all-to-all-start = ((bf16[8,192,256]{2,1,0:T(8,128)(2,1)}), bf16[8,192,256]{2,1,0:T(8,128)(2,1)S(1)}, u32[]{:S(2)}, u32[]{:S(2)}) async-start(bf16[8,192,256]{2,1,0:T(8,128)(2,1)} %pad_maximum_fusion), calls=%async_computation | async-start | bytes 1572864 | tf_op jit(solution)/shard_map/all_to_all | solution.py:183
  73.9 1.9 %constant_dynamic-update-slice_fusion.5 = bf16[1024,2048]{1,0:T(8,128)(2,1)} fusion(bf16[1024,2048]{1,0:T(8,128)(2,1)} %copy-done.11, bf16[128,2048]{1,0:T(8,128)(2,1)} %collective-permute-done.5, s32[]{:T(128)S(6)} %select_n.172), kind=kLoop, calls=%fused_computation.22 | loop fusion | bytes 1048580 | tf_op jit(solution)/shard_map/dynamic_update_slice | solution.py:195
  75.8 1.9 %constant_dynamic-update-slice_fusion.4 = bf16[1024,2048]{1,0:T(8,128)(2,1)} fusion(bf16[1024,2048]{1,0:T(8,128)(2,1)} %constant_dynamic-update-slice_fusion.5, bf16[128,2048]{1,0:T(8,128)(2,1)} %collective-permute-done.7, s32[]{:T(128)S(6)} %select_n.174), kind=kLoop, calls=%fused_computation.21 | loop fusion | bytes 1048580 | tf_op jit(solution)/shard_map/dynamic_update_slice | solution.py:195
  77.7 1.4 %collective-permute-start.10 = (bf16[64,2048]{1,0:T(8,128)(2,1)S(1)}, bf16[64,2048]{1,0:T(8,128)(2,1)S(1)}, u32[]{:S(2)}, u32[]{:S(2)}) collective-permute-start(bf16[64,2048]{1,0:T(8,128)(2,1)S(1)} %slice.35), channel_id=1, source_target_pairs={{0,4},{4,8},{8,12},{12,14},{14,10},{10,6},{6,2},{2,0},{1,5},{5,9},... | collective-permute-start | bytes 786440 | tf_op jit(solution)/shard_map/ppermute | solution.py:190
  79.2 0.1 collective-permute-start.11
  79.3 0.8 constant_dynamic-update-slice_fusion.3
  80.2 0.8 constant_dynamic-update-slice_fusion.2
  81.0 18.3 %collective-permute-done.10 = bf16[64,2048]{1,0:T(8,128)(2,1)S(1)} collective-permute-done((bf16[64,2048]{1,0:T(8,128)(2,1)S(1)}, bf16[64,2048]{1,0:T(8,128)(2,1)S(1)}, u32[]{:S(2)}, u32[]{:S(2)}) %collective-permute-start.10) | collective-permute-done | bytes 262176 | tf_op jit(solution)/shard_map/ppermute | solution.py:190
  99.3 0.7 constant_dynamic-update-slice_fusion.1
  100.0 1.2 %collective-permute-done.11 = bf16[64,2048]{1,0:T(8,128)(2,1)S(1)} collective-permute-done((bf16[64,2048]{1,0:T(8,128)(2,1)S(1)}, bf16[64,2048]{1,0:T(8,128)(2,1)S(1)}, u32[]{:S(2)}, u32[]{:S(2)}) %collective-permute-start.11) | collective-permute-done | bytes 262176 | tf_op jit(solution)/shard_map/ppermute | solution.py:191
  101.2 0.7 constant_dynamic-update-slice_fusion
  102.0 3.1 %fusion.7 = f32[128,2048]{1,0:T(8,128)S(1)} fusion(bf16[1024,128]{1,0:T(8,128)(2,1)S(1)} %bitcast.52, bf16[1024,2048]{1,0:T(8,128)(2,1)} %constant_dynamic-update-slice_fusion), kind=kOutput, calls=%fused_computation.48 | convolution fusion | flops 536870912 | bytes 5505024 | tf_op jit(solution)/shard_map/dot_general | solution.py:16
  105.0 2.9 %collective-permute-start.12 = (f32[128,2048]{1,0:T(8,128)S(1)}, f32[128,2048]{1,0:T(8,128)S(1)}, u32[]{:S(2)}, u32[]{:S(2)}) collective-permute-start(f32[128,2048]{1,0:T(8,128)S(1)} %fusion.7), channel_id=1, source_target_pairs={{0,1},{1,0},{2,3},{3,2},{4,5},{5,4},{6,7},{7,6},{8,9},{9,8},{10,11... | collective-permute-start | bytes 3145736 | tf_op jit(solution)/shard_map/ppermute | solution.py:20
  108.0 0.7 fusion.6
  108.8 0.6 broadcast_multiply_fusion
  109.4 0.9 collective-permute-done.12
  110.3 1.1 %multiply_bitcast_fusion = f32[1,128,2048]{2,1,0:T(8,128)} fusion(f32[128,2048]{1,0:T(8,128)S(1)} %fusion.6, f32[128,2048]{1,0:T(8,128)S(1)} %collective-permute-done.12), kind=kLoop, calls=%fused_computation.1 | loop fusion | flops 524288 | bytes 3145728 | tf_op jit(solution)/shard_map/broadcast_in_dim | solution.py:202
  (39 shorter events, 0.5 us)
Async XLA Ops:
  0.6 10.6 %copy-start = (bf16[256,2048]{1,0:T(8,128)(2,1)S(1)}, bf16[256,2048]{1,0:T(8,128)(2,1)}, u32[]{:S(2)}) copy-start(bf16[256,2048]{1,0:T(8,128)(2,1)} %param.6) | copy-start | bytes 3145732
  0.6 3.5 %copy-start.1 = (bf16[1,2048,2048]{2,1,0:T(8,128)(2,1)S(1)}, bf16[1,2048,2048]{2,1,0:T(8,128)(2,1)}, u32[]{:S(2)}) copy-start(bf16[1,2048,2048]{2,1,0:T(8,128)(2,1)} %param.5) | copy-start | bytes 25165828
  4.1 1.0 copy-start.3
  5.2 6.1 %copy-start.13 = (s32[128]{0:T(128)S(1)}, s32[128]{0:T(128)}, u32[]{:S(2)}) copy-start(s32[128]{0:T(128)} %param.7) | copy-start | bytes 1540
  5.2 17.4 %copy-start.4 = (bf16[1,128,2048]{2,1,0:T(8,128)(2,1)S(1)}, bf16[1,128,2048]{2,1,0:T(8,128)(2,1)}, u32[]{:S(2)}) copy-start(bf16[1,128,2048]{2,1,0:T(8,128)(2,1)} %param.4) | copy-start | bytes 1572868
  8.1 13.7 %collective-permute-start = (bf16[2,128,1024]{2,1,0:T(8,128)(2,1)S(1)}, bf16[2,128,1024]{2,1,0:T(8,128)(2,1)S(1)}, u32[]{:S(2)}, u32[]{:S(2)}) collective-permute-start(bf16[2,128,1024]{2,1,0:T(8,128)(2,1)S(1)} %shard_map.67), channel_id=1, source_target_pairs={{0,16},{1,17},{2,18},{3,19},{4,20},{5,21},{6,22},{7,23},{8,24},{9,... | collective-permute-start | bytes 1572872 | tf_op jit(solution)/shard_map/ppermute | solution.py:151
  21.8 0.8 copy-start.5
  22.6 3.4 %copy-start.2 = (bf16[1,2048,2048]{2,1,0:T(8,128)(2,1)S(1)}, bf16[1,2048,2048]{2,1,0:T(8,128)(2,1)}, u32[]{:S(2)}) copy-start(bf16[1,2048,2048]{2,1,0:T(8,128)(2,1)} %param.5) | copy-start | bytes 25165828
  25.9 1.0 copy-start.6
  35.7 0.8 copy-start.7
  36.5 0.8 copy-start.9
  37.4 19.1 %collective-permute-start.2 = (f32[128,2048]{1,0:T(8,128)}, f32[128,2048]{1,0:T(8,128)S(1)}, u32[]{:S(2)}, u32[]{:S(2)}) collective-permute-start(f32[128,2048]{1,0:T(8,128)} %get-tuple-element.12), channel_id=1, source_target_pairs={{0,1},{1,0},{2,3},{3,2},{4,5},{5,4},{6,7},{7,6},{8,9},{9,8},{10,11... | collective-permute-start | bytes 3145736 | tf_op jit(solution)/shard_map/ppermute | solution.py:20
  38.9 13.9 %collective-permute-start.4 = (bf16[128,2048]{1,0:T(8,128)(2,1)}, bf16[128,2048]{1,0:T(8,128)(2,1)}, u32[]{:S(2)}, u32[]{:S(2)}) collective-permute-start(bf16[128,2048]{1,0:T(8,128)(2,1)} %get-tuple-element.15), channel_id=1, source_target_pairs={{0,4},{4,8},{8,12},{12,14},{14,10},{10,6},{6,2},{2,0},{1,5},{5,9},... | collective-permute-start | bytes 1572872 | tf_op jit(solution)/shard_map/ppermute | solution.py:174
  40.2 13.9 %collective-permute-start.6 = (bf16[128,2048]{1,0:T(8,128)(2,1)}, bf16[128,2048]{1,0:T(8,128)(2,1)}, u32[]{:S(2)}, u32[]{:S(2)}) collective-permute-start(bf16[128,2048]{1,0:T(8,128)(2,1)} %get-tuple-element.15), channel_id=1, source_target_pairs={{4,0},{8,4},{12,8},{14,12},{10,14},{6,10},{2,6},{0,2},{5,1},{9,5},... | collective-permute-start | bytes 1572872 | tf_op jit(solution)/shard_map/ppermute | solution.py:175
  40.4 17.5 %collective-permute-start.1 = (bf16[128,2048]{1,0:T(8,128)(2,1)}, bf16[128,2048]{1,0:T(8,128)(2,1)S(1)}, u32[]{:S(2)}, u32[]{:S(2)}) collective-permute-start(bf16[128,2048]{1,0:T(8,128)(2,1)} %copy-done.7), channel_id=1, source_target_pairs={{16,0},{17,1},{18,2},{19,3},{20,4},{21,5},{22,6},{23,7},{24,8},{25... | collective-permute-start | bytes 1572872 | tf_op jit(solution)/shard_map/ppermute | solution.py:157
  42.2 15.7 %copy-start.8 = (bf16[128,2048]{1,0:T(8,128)(2,1)S(1)}, bf16[128,2048]{1,0:T(8,128)(2,1)}, u32[]{:S(2)}) copy-start(bf16[128,2048]{1,0:T(8,128)(2,1)} %copy-done.7) | copy-start | bytes 1572868
  42.2 15.7 %copy-start.10 = (bf16[128,2048]{1,0:T(8,128)(2,1)S(1)}, bf16[128,2048]{1,0:T(8,128)(2,1)}, u32[]{:S(2)}) copy-start(bf16[128,2048]{1,0:T(8,128)(2,1)} %copy-done.9) | copy-start | bytes 1572868
  52.8 13.0 %collective-permute-start.5 = (bf16[128,2048]{1,0:T(8,128)(2,1)}, bf16[128,2048]{1,0:T(8,128)(2,1)}, u32[]{:S(2)}, u32[]{:S(2)}) collective-permute-start(bf16[128,2048]{1,0:T(8,128)(2,1)} %collective-permute-done.4), channel_id=1, source_target_pairs={{0,4},{4,8},{8,12},{12,14},{14,10},{10,6},{6,2},{2,0},{1,5},{5,9},... | collective-permute-start | bytes 1572872 | tf_op jit(solution)/shard_map/ppermute | solution.py:174
  54.1 13.0 %collective-permute-start.7 = (bf16[128,2048]{1,0:T(8,128)(2,1)}, bf16[128,2048]{1,0:T(8,128)(2,1)}, u32[]{:S(2)}, u32[]{:S(2)}) collective-permute-start(bf16[128,2048]{1,0:T(8,128)(2,1)} %collective-permute-done.6), channel_id=1, source_target_pairs={{4,0},{8,4},{12,8},{14,12},{10,14},{6,10},{2,6},{0,2},{5,1},{9,5},... | collective-permute-start | bytes 1572872 | tf_op jit(solution)/shard_map/ppermute | solution.py:175
  56.4 2.4 %copy-start.11 = (bf16[1024,2048]{1,0:T(8,128)(2,1)}, bf16[1024,2048]{1,0:T(8,128)(2,1)S(1)}, u32[]{:S(2)}) copy-start(bf16[1024,2048]{1,0:T(8,128)(2,1)S(1)} %constant_dynamic-update-slice_fusion.6) | copy-start | bytes 12582916
  56.6 10.7 %collective-permute-start.3 = (bf16[8,8,2048]{2,1,0:T(8,128)(2,1)S(1)}, bf16[8,8,2048]{2,1,0:T(8,128)(2,1)S(1)}, u32[]{:S(2)}, u32[]{:S(2)}) collective-permute-start(bf16[8,8,2048]{2,1,0:T(8,128)(2,1)S(1)} %slice_bitcast_fusion.1), channel_id=1, source_target_pairs={{16,0},{17,1},{18,2},{19,3},{20,4},{21,5},{22,6},{23,7},{24,8},{25... | collective-permute-start | bytes 786440 | tf_op jit(solution)/shard_map/ppermute | solution.py:161
  65.7 12.0 %collective-permute-start.8 = (bf16[128,2048]{1,0:T(8,128)(2,1)}, bf16[128,2048]{1,0:T(8,128)(2,1)S(1)}, u32[]{:S(2)}, u32[]{:S(2)}) collective-permute-start(bf16[128,2048]{1,0:T(8,128)(2,1)} %collective-permute-done.5), channel_id=1, source_target_pairs={{0,4},{4,8},{8,12},{12,14},{14,10},{10,6},{6,2},{2,0},{1,5},{5,9},... | collective-permute-start | bytes 1572872 | tf_op jit(solution)/shard_map/ppermute | solution.py:174
  67.0 12.1 %collective-permute-start.9 = (bf16[128,2048]{1,0:T(8,128)(2,1)}, bf16[128,2048]{1,0:T(8,128)(2,1)S(1)}, u32[]{:S(2)}, u32[]{:S(2)}) collective-permute-start(bf16[128,2048]{1,0:T(8,128)(2,1)} %collective-permute-done.7), channel_id=1, source_target_pairs={{4,0},{8,4},{12,8},{14,12},{10,14},{6,10},{2,6},{0,2},{5,1},{9,5},... | collective-permute-start | bytes 1572872 | tf_op jit(solution)/shard_map/ppermute | solution.py:175
  68.2 33.7 %all-to-all-start = ((bf16[8,192,256]{2,1,0:T(8,128)(2,1)}), bf16[8,192,256]{2,1,0:T(8,128)(2,1)S(1)}, u32[]{:S(2)}, u32[]{:S(2)}) async-start(bf16[8,192,256]{2,1,0:T(8,128)(2,1)} %pad_maximum_fusion), calls=%async_computation | async-start | bytes 1572864 | tf_op jit(solution)/shard_map/all_to_all | solution.py:183
  77.7 21.5 %collective-permute-start.10 = (bf16[64,2048]{1,0:T(8,128)(2,1)S(1)}, bf16[64,2048]{1,0:T(8,128)(2,1)S(1)}, u32[]{:S(2)}, u32[]{:S(2)}) collective-permute-start(bf16[64,2048]{1,0:T(8,128)(2,1)S(1)} %slice.35), channel_id=1, source_target_pairs={{0,4},{4,8},{8,12},{12,14},{14,10},{10,6},{6,2},{2,0},{1,5},{5,9},... | collective-permute-start | bytes 786440 | tf_op jit(solution)/shard_map/ppermute | solution.py:190
  79.2 22.0 %collective-permute-start.11 = (bf16[64,2048]{1,0:T(8,128)(2,1)S(1)}, bf16[64,2048]{1,0:T(8,128)(2,1)S(1)}, u32[]{:S(2)}, u32[]{:S(2)}) collective-permute-start(bf16[64,2048]{1,0:T(8,128)(2,1)S(1)} %slice.36), channel_id=1, source_target_pairs={{4,0},{8,4},{12,8},{14,12},{10,14},{6,10},{2,6},{0,2},{5,1},{9,5},... | collective-permute-start | bytes 786440 | tf_op jit(solution)/shard_map/ppermute | solution.py:191
  101.9 6.1 %copy-start.12 = (bf16[1024,2048]{1,0:T(8,128)(2,1)S(1)}, bf16[1024,2048]{1,0:T(8,128)(2,1)}, u32[]{:S(2)}) copy-start(bf16[1024,2048]{1,0:T(8,128)(2,1)} %constant_dynamic-update-slice_fusion) | copy-start | bytes 12582916
  105.0 5.2 %collective-permute-start.12 = (f32[128,2048]{1,0:T(8,128)S(1)}, f32[128,2048]{1,0:T(8,128)S(1)}, u32[]{:S(2)}, u32[]{:S(2)}) collective-permute-start(f32[128,2048]{1,0:T(8,128)S(1)} %fusion.7), channel_id=1, source_target_pairs={{0,1},{1,0},{2,3},{3,2},{4,5},{5,4},{6,7},{7,6},{8,9},{9,8},{10,11... | collective-permute-start | bytes 3145736 | tf_op jit(solution)/shard_map/ppermute | solution.py:20

commit v8 on v7

--- a/solution.py
+++ b/solution.py
@@ -9,7 +9,7 @@
 F32 = jnp.float32
 BF16 = jnp.bfloat16
 TILE = 256
-GRANT = 16 * 1024 * 1024
+GRANT = 8 * 1024 * 1024
 
 
 def dot(a, b, ca, cb):

time: 113 us -> 113 us (level)
  no operation moved by 1% of the time
where the time goes in v8:
time: 113 us; the launch traced here: 111 us
  waiting for transfers between devices  44.5 us (39%)
  local copies, waits for them, and re-layouts  24.4 us (22%)
  starting transfers between devices  21.9 us (19%)
  Pallas kernels  11.7 us (10%)
  matrix products  4.16 us (4%)
  other arithmetic  3.9 us (3%)
    ppermute x1, waiting for transfers between devices, local(): blocks.append((lax.ppermute(fwd[:mid], 'chip', up), chips // 2, 0))  18.3 us
    ppermute x3, waiting for transfers between devices, local(): fwd = lax.ppermute(fwd, 'chip', up)  16.3 us
    unnamed x28, local copies, waits for them, and re-layouts  11.4 us
    dynamic_update_slice x9, local copies, waits for them, and re-layouts, local(): right_all = lax.dynamic_update_slice_in_dim(right_all, block, start, 0)  10.2 us
    pallas_call x1, Pallas kernels, trail(): pl.pallas_call(trail_body, out_shape=(jax.ShapeDtypeStruct((rows_dev, hid...  8.78 us
    ppermute x1, waiting for transfers between devices, local(): query = lax.ppermute(own_query, 'hop', [(0, 1)])  7.79 us
    all_to_all x1, starting transfers between devices, local(): received = lax.all_to_all(sent, 'chip', 0, 0, tiled=True)  5.71 us
    ppermute x2, starting transfers between devices, swap_core(): return lax.ppermute(block, 'core', [(0, 1), (1, 0)])  4.47 us
  transfers between devices with their start and end apart: 14, of which 6 were waited for; matrix products, arithmetic and copies ran while one was open for 15% of the time, Pallas kernels for 0%

profile of v8, /device:TPU:9, one launch (start us, length us, event | category | flops | bytes accessed | tf_op | source)
XLA Modules:
  0.0 111.4 jit_solution(5399422834221742382)
XLA Ops:
  0.7 3.5 %copy-done.1 = bf16[1,2048,2048]{2,1,0:T(8,128)(2,1)S(1)} copy-done((bf16[1,2048,2048]{2,1,0:T(8,128)(2,1)S(1)}, bf16[1,2048,2048]{2,1,0:T(8,128)(2,1)}, u32[]{:S(2)}) %copy-start.1) | copy-done | bytes 8388632
  4.1 1.0 copy-done.3
  5.2 2.9 %shard_map.67 = bf16[2,128,1024]{2,1,0:T(8,128)(2,1)S(1)} custom-call(bf16[128,2048]{1,0:T(8,128)(2,1)S(1)} %bitcast.42, bf16[2048,2048]{1,0:T(8,128)(2,1)S(1)} %bitcast.40), custom_call_target="tpu_custom_call" | custom-call | flops 1073741824 | bytes 8388608 | tf_op jit(solution)/shard_map/pallas_call | solution.py:43
  8.1 3.2 %collective-permute-start = (bf16[2,128,1024]{2,1,0:T(8,128)(2,1)S(1)}, bf16[2,128,1024]{2,1,0:T(8,128)(2,1)S(1)}, u32[]{:S(2)}, u32[]{:S(2)}) collective-permute-start(bf16[2,128,1024]{2,1,0:T(8,128)(2,1)S(1)} %shard_map.67), channel_id=1, source_target_pairs={{0,16},{1,17},{2,18},{3,19},{4,20},{5,21},{6,22},{7,23},{8,24},{9,... | collective-permute-start | bytes 1572872 | tf_op jit(solution)/shard_map/ppermute | solution.py:151
  11.2 0.3 convolution_convert_fusion
  11.6 1.0 copy.9
  12.6 1.2 %copy.10 = bf16[128,2,1024]{2,0,1:T(8,128)(2,1)S(1)} copy(bf16[128,2,1024]{0,2,1:T(8,128)(2,1)} %bitcast.48) | data formatting | bytes 1048576 | tf_op jit(solution)/shard_map/reshape | solution.py:153
  14.0 7.8 %collective-permute-done.query = bf16[2,128,1024]{2,1,0:T(8,128)(2,1)S(1)} collective-permute-done((bf16[2,128,1024]{2,1,0:T(8,128)(2,1)S(1)}, bf16[2,128,1024]{2,1,0:T(8,128)(2,1)S(1)}, u32[]{:S(2)}, u32[]{:S(2)}) %collective-permute-start) | collective-permute-done | bytes 524320 | tf_op jit(solution)/shard_map/ppermute | solution.py:151
  21.8 0.8 copy-done.5
  22.6 3.4 %copy-done.2 = bf16[1,2048,2048]{2,1,0:T(8,128)(2,1)S(1)} copy-done((bf16[1,2048,2048]{2,1,0:T(8,128)(2,1)S(1)}, bf16[1,2048,2048]{2,1,0:T(8,128)(2,1)}, u32[]{:S(2)}) %copy-start.2) | copy-done | bytes 8388632
  26.0 1.0 copy-done.6
  27.0 8.8 %shard_map.68 = (bf16[128,2048]{1,0:T(8,128)(2,1)}, bf16[128,2048]{1,0:T(8,128)(2,1)S(1)}, f32[128,2048]{1,0:T(8,128)}, f32[128,2048]{1,0:T(8,128)S(1)}, bf16[128,2048]{1,0:T(8,128)(2,1)S(1)}) custom-call(s32[1]{0:T(128)} %bitcast.first, bf16[2,128,1024]{2,1,0:T(8,128)(2,1)S(1)} %copy-done.6, bf16[128,2048]{1,0:T(8,128)(2,1)S(1)} %bitcast.43, ...), custom_call_target="tpu_custom_call" | custom-call | flops 2415919104 | bytes 16777216 | tf_op jit(solution)/shard_map/pallas_call | solution.py:105
  35.8 0.8 copy-done.7
  36.6 0.8 copy-done.9
  37.4 1.5 %collective-permute-start.2 = (f32[128,2048]{1,0:T(8,128)}, f32[128,2048]{1,0:T(8,128)S(1)}, u32[]{:S(2)}, u32[]{:S(2)}) collective-permute-start(f32[128,2048]{1,0:T(8,128)} %get-tuple-element.12), channel_id=1, source_target_pairs={{0,1},{1,0},{2,3},{3,2},{4,5},{5,4},{6,7},{7,6},{8,9},{9,8},{10,11... | collective-permute-start | bytes 3145736 | tf_op jit(solution)/shard_map/ppermute | solution.py:20
  38.9 1.3 %collective-permute-start.4 = (bf16[128,2048]{1,0:T(8,128)(2,1)}, bf16[128,2048]{1,0:T(8,128)(2,1)}, u32[]{:S(2)}, u32[]{:S(2)}) collective-permute-start(bf16[128,2048]{1,0:T(8,128)(2,1)} %get-tuple-element.15), channel_id=1, source_target_pairs={{0,4},{4,8},{8,12},{12,14},{14,10},{10,6},{6,2},{2,0},{1,5},{5,9},... | collective-permute-start | bytes 1572872 | tf_op jit(solution)/shard_map/ppermute | solution.py:174
  40.2 0.2 collective-permute-start.6
  40.4 1.3 %collective-permute-start.1 = (bf16[128,2048]{1,0:T(8,128)(2,1)}, bf16[128,2048]{1,0:T(8,128)(2,1)S(1)}, u32[]{:S(2)}, u32[]{:S(2)}) collective-permute-start(bf16[128,2048]{1,0:T(8,128)(2,1)} %copy-done.7), channel_id=1, source_target_pairs={{16,0},{17,1},{18,2},{19,3},{20,4},{21,5},{22,6},{23,7},{24,8},{25... | collective-permute-start | bytes 1572872 | tf_op jit(solution)/shard_map/ppermute | solution.py:157
  41.7 0.5 broadcast_in_dim.20
  42.2 1.2 %constant_dynamic-update-slice_fusion.8 = bf16[1024,2048]{1,0:T(8,128)(2,1)S(1)} fusion(bf16[1024,2048]{1,0:T(8,128)(2,1)S(1)} %broadcast_in_dim.20, bf16[128,2048]{1,0:T(8,128)(2,1)} %get-tuple-element.15, s32[]{:T(128)S(6)} %select_n.166), kind=kLoop, calls=%fused_computation.25 | loop fusion | bytes 1048580 | tf_op jit(solution)/shard_map/dynamic_update_slice | solution.py:195
  43.4 9.4 %collective-permute-done.4 = bf16[128,2048]{1,0:T(8,128)(2,1)} collective-permute-done((bf16[128,2048]{1,0:T(8,128)(2,1)}, bf16[128,2048]{1,0:T(8,128)(2,1)}, u32[]{:S(2)}, u32[]{:S(2)}) %collective-permute-start.4) | collective-permute-done | bytes 524320 | tf_op jit(solution)/shard_map/ppermute | solution.py:174
  52.8 1.3 %collective-permute-start.5 = (bf16[128,2048]{1,0:T(8,128)(2,1)}, bf16[128,2048]{1,0:T(8,128)(2,1)}, u32[]{:S(2)}, u32[]{:S(2)}) collective-permute-start(bf16[128,2048]{1,0:T(8,128)(2,1)} %collective-permute-done.4), channel_id=1, source_target_pairs={{0,4},{4,8},{8,12},{12,14},{14,10},{10,6},{6,2},{2,0},{1,5},{5,9},... | collective-permute-start | bytes 1572872 | tf_op jit(solution)/shard_map/ppermute | solution.py:174
  54.1 0.2 collective-permute-start.7
  54.3 1.1 constant_dynamic-update-slice_fusion.7
  55.3 1.1 constant_dynamic-update-slice_fusion.6
  56.6 1.3 %collective-permute-start.3 = (bf16[8,8,2048]{2,1,0:T(8,128)(2,1)S(1)}, bf16[8,8,2048]{2,1,0:T(8,128)(2,1)S(1)}, u32[]{:S(2)}, u32[]{:S(2)}) collective-permute-start(bf16[8,8,2048]{2,1,0:T(8,128)(2,1)S(1)} %slice_bitcast_fusion.1), channel_id=1, source_target_pairs={{16,0},{17,1},{18,2},{19,3},{20,4},{21,5},{22,6},{23,7},{24,8},{25... | collective-permute-start | bytes 786440 | tf_op jit(solution)/shard_map/ppermute | solution.py:161
  57.9 0.9 broadcast_select_fusion
  58.8 6.9 %collective-permute-done.5 = bf16[128,2048]{1,0:T(8,128)(2,1)} collective-permute-done((bf16[128,2048]{1,0:T(8,128)(2,1)}, bf16[128,2048]{1,0:T(8,128)(2,1)}, u32[]{:S(2)}, u32[]{:S(2)}) %collective-permute-start.5) | collective-permute-done | bytes 524320 | tf_op jit(solution)/shard_map/ppermute | solution.py:174
  65.8 1.3 %collective-permute-start.8 = (bf16[128,2048]{1,0:T(8,128)(2,1)}, bf16[128,2048]{1,0:T(8,128)(2,1)S(1)}, u32[]{:S(2)}, u32[]{:S(2)}) collective-permute-start(bf16[128,2048]{1,0:T(8,128)(2,1)} %collective-permute-done.5), channel_id=1, source_target_pairs={{0,4},{4,8},{8,12},{12,14},{14,10},{10,6},{6,2},{2,0},{1,5},{5,9},... | collective-permute-start | bytes 1572872 | tf_op jit(solution)/shard_map/ppermute | solution.py:174
  67.1 0.2 collective-permute-start.9
  67.3 0.9 pad_maximum_fusion
  68.2 5.7 %all-to-all-start = ((bf16[8,192,256]{2,1,0:T(8,128)(2,1)}), bf16[8,192,256]{2,1,0:T(8,128)(2,1)S(1)}, u32[]{:S(2)}, u32[]{:S(2)}) async-start(bf16[8,192,256]{2,1,0:T(8,128)(2,1)} %pad_maximum_fusion), calls=%async_computation | async-start | bytes 1572864 | tf_op jit(solution)/shard_map/all_to_all | solution.py:183
  73.9 1.9 %constant_dynamic-update-slice_fusion.5 = bf16[1024,2048]{1,0:T(8,128)(2,1)} fusion(bf16[1024,2048]{1,0:T(8,128)(2,1)} %copy-done.11, bf16[128,2048]{1,0:T(8,128)(2,1)} %collective-permute-done.5, s32[]{:T(128)S(6)} %select_n.172), kind=kLoop, calls=%fused_computation.22 | loop fusion | bytes 1048580 | tf_op jit(solution)/shard_map/dynamic_update_slice | solution.py:195
  75.8 1.9 %constant_dynamic-update-slice_fusion.4 = bf16[1024,2048]{1,0:T(8,128)(2,1)} fusion(bf16[1024,2048]{1,0:T(8,128)(2,1)} %constant_dynamic-update-slice_fusion.5, bf16[128,2048]{1,0:T(8,128)(2,1)} %collective-permute-done.7, s32[]{:T(128)S(6)} %select_n.174), kind=kLoop, calls=%fused_computation.21 | loop fusion | bytes 1048580 | tf_op jit(solution)/shard_map/dynamic_update_slice | solution.py:195
  77.7 1.4 %collective-permute-start.10 = (bf16[64,2048]{1,0:T(8,128)(2,1)S(1)}, bf16[64,2048]{1,0:T(8,128)(2,1)S(1)}, u32[]{:S(2)}, u32[]{:S(2)}) collective-permute-start(bf16[64,2048]{1,0:T(8,128)(2,1)S(1)} %slice.35), channel_id=1, source_target_pairs={{0,4},{4,8},{8,12},{12,14},{14,10},{10,6},{6,2},{2,0},{1,5},{5,9},... | collective-permute-start | bytes 786440 | tf_op jit(solution)/shard_map/ppermute | solution.py:190
  79.2 0.1 collective-permute-start.11
  79.3 0.8 constant_dynamic-update-slice_fusion.3
  80.2 0.8 constant_dynamic-update-slice_fusion.2
  81.0 18.3 %collective-permute-done.10 = bf16[64,2048]{1,0:T(8,128)(2,1)S(1)} collective-permute-done((bf16[64,2048]{1,0:T(8,128)(2,1)S(1)}, bf16[64,2048]{1,0:T(8,128)(2,1)S(1)}, u32[]{:S(2)}, u32[]{:S(2)}) %collective-permute-start.10) | collective-permute-done | bytes 262176 | tf_op jit(solution)/shard_map/ppermute | solution.py:190
  99.3 0.7 constant_dynamic-update-slice_fusion.1
  100.0 1.2 %collective-permute-done.11 = bf16[64,2048]{1,0:T(8,128)(2,1)S(1)} collective-permute-done((bf16[64,2048]{1,0:T(8,128)(2,1)S(1)}, bf16[64,2048]{1,0:T(8,128)(2,1)S(1)}, u32[]{:S(2)}, u32[]{:S(2)}) %collective-permute-start.11) | collective-permute-done | bytes 262176 | tf_op jit(solution)/shard_map/ppermute | solution.py:191
  101.2 0.7 constant_dynamic-update-slice_fusion
  102.0 3.1 %fusion.7 = f32[128,2048]{1,0:T(8,128)S(1)} fusion(bf16[1024,128]{1,0:T(8,128)(2,1)S(1)} %bitcast.52, bf16[1024,2048]{1,0:T(8,128)(2,1)} %constant_dynamic-update-slice_fusion), kind=kOutput, calls=%fused_computation.48 | convolution fusion | flops 536870912 | bytes 5505024 | tf_op jit(solution)/shard_map/dot_general | solution.py:16
  105.1 2.9 %collective-permute-start.12 = (f32[128,2048]{1,0:T(8,128)S(1)}, f32[128,2048]{1,0:T(8,128)S(1)}, u32[]{:S(2)}, u32[]{:S(2)}) collective-permute-start(f32[128,2048]{1,0:T(8,128)S(1)} %fusion.7), channel_id=1, source_target_pairs={{0,1},{1,0},{2,3},{3,2},{4,5},{5,4},{6,7},{7,6},{8,9},{9,8},{10,11... | collective-permute-start | bytes 3145736 | tf_op jit(solution)/shard_map/ppermute | solution.py:20
  108.0 0.7 fusion.6
  108.8 0.6 broadcast_multiply_fusion
  109.4 0.9 collective-permute-done.12
  110.3 1.1 %multiply_bitcast_fusion = f32[1,128,2048]{2,1,0:T(8,128)} fusion(f32[128,2048]{1,0:T(8,128)S(1)} %fusion.6, f32[128,2048]{1,0:T(8,128)S(1)} %collective-permute-done.12), kind=kLoop, calls=%fused_computation.1 | loop fusion | flops 524288 | bytes 3145728 | tf_op jit(solution)/shard_map/broadcast_in_dim | solution.py:202
  (39 shorter events, 0.5 us)
Async XLA Ops:
  0.6 10.6 %copy-start = (bf16[256,2048]{1,0:T(8,128)(2,1)S(1)}, bf16[256,2048]{1,0:T(8,128)(2,1)}, u32[]{:S(2)}) copy-start(bf16[256,2048]{1,0:T(8,128)(2,1)} %param.6) | copy-start | bytes 3145732
  0.6 3.5 %copy-start.1 = (bf16[1,2048,2048]{2,1,0:T(8,128)(2,1)S(1)}, bf16[1,2048,2048]{2,1,0:T(8,128)(2,1)}, u32[]{:S(2)}) copy-start(bf16[1,2048,2048]{2,1,0:T(8,128)(2,1)} %param.5) | copy-start | bytes 25165828
  4.1 1.0 copy-start.3
  5.2 6.1 %copy-start.13 = (s32[128]{0:T(128)S(1)}, s32[128]{0:T(128)}, u32[]{:S(2)}) copy-start(s32[128]{0:T(128)} %param.7) | copy-start | bytes 1540
  5.2 17.4 %copy-start.4 = (bf16[1,128,2048]{2,1,0:T(8,128)(2,1)S(1)}, bf16[1,128,2048]{2,1,0:T(8,128)(2,1)}, u32[]{:S(2)}) copy-start(bf16[1,128,2048]{2,1,0:T(8,128)(2,1)} %param.4) | copy-start | bytes 1572868
  8.1 13.7 %collective-permute-start = (bf16[2,128,1024]{2,1,0:T(8,128)(2,1)S(1)}, bf16[2,128,1024]{2,1,0:T(8,128)(2,1)S(1)}, u32[]{:S(2)}, u32[]{:S(2)}) collective-permute-start(bf16[2,128,1024]{2,1,0:T(8,128)(2,1)S(1)} %shard_map.67), channel_id=1, source_target_pairs={{0,16},{1,17},{2,18},{3,19},{4,20},{5,21},{6,22},{7,23},{8,24},{9,... | collective-permute-start | bytes 1572872 | tf_op jit(solution)/shard_map/ppermute | solution.py:151
  21.8 0.8 copy-start.5
  22.6 3.4 %copy-start.2 = (bf16[1,2048,2048]{2,1,0:T(8,128)(2,1)S(1)}, bf16[1,2048,2048]{2,1,0:T(8,128)(2,1)}, u32[]{:S(2)}) copy-start(bf16[1,2048,2048]{2,1,0:T(8,128)(2,1)} %param.5) | copy-start | bytes 25165828
  25.9 1.0 copy-start.6
  35.8 0.8 copy-start.7
  36.6 0.8 copy-start.9
  37.4 19.1 %collective-permute-start.2 = (f32[128,2048]{1,0:T(8,128)}, f32[128,2048]{1,0:T(8,128)S(1)}, u32[]{:S(2)}, u32[]{:S(2)}) collective-permute-start(f32[128,2048]{1,0:T(8,128)} %get-tuple-element.12), channel_id=1, source_target_pairs={{0,1},{1,0},{2,3},{3,2},{4,5},{5,4},{6,7},{7,6},{8,9},{9,8},{10,11... | collective-permute-start | bytes 3145736 | tf_op jit(solution)/shard_map/ppermute | solution.py:20
  38.9 13.9 %collective-permute-start.4 = (bf16[128,2048]{1,0:T(8,128)(2,1)}, bf16[128,2048]{1,0:T(8,128)(2,1)}, u32[]{:S(2)}, u32[]{:S(2)}) collective-permute-start(bf16[128,2048]{1,0:T(8,128)(2,1)} %get-tuple-element.15), channel_id=1, source_target_pairs={{0,4},{4,8},{8,12},{12,14},{14,10},{10,6},{6,2},{2,0},{1,5},{5,9},... | collective-permute-start | bytes 1572872 | tf_op jit(solution)/shard_map/ppermute | solution.py:174
  40.2 13.9 %collective-permute-start.6 = (bf16[128,2048]{1,0:T(8,128)(2,1)}, bf16[128,2048]{1,0:T(8,128)(2,1)}, u32[]{:S(2)}, u32[]{:S(2)}) collective-permute-start(bf16[128,2048]{1,0:T(8,128)(2,1)} %get-tuple-element.15), channel_id=1, source_target_pairs={{4,0},{8,4},{12,8},{14,12},{10,14},{6,10},{2,6},{0,2},{5,1},{9,5},... | collective-permute-start | bytes 1572872 | tf_op jit(solution)/shard_map/ppermute | solution.py:175
  40.4 17.5 %collective-permute-start.1 = (bf16[128,2048]{1,0:T(8,128)(2,1)}, bf16[128,2048]{1,0:T(8,128)(2,1)S(1)}, u32[]{:S(2)}, u32[]{:S(2)}) collective-permute-start(bf16[128,2048]{1,0:T(8,128)(2,1)} %copy-done.7), channel_id=1, source_target_pairs={{16,0},{17,1},{18,2},{19,3},{20,4},{21,5},{22,6},{23,7},{24,8},{25... | collective-permute-start | bytes 1572872 | tf_op jit(solution)/shard_map/ppermute | solution.py:157
  42.2 15.7 %copy-start.8 = (bf16[128,2048]{1,0:T(8,128)(2,1)S(1)}, bf16[128,2048]{1,0:T(8,128)(2,1)}, u32[]{:S(2)}) copy-start(bf16[128,2048]{1,0:T(8,128)(2,1)} %copy-done.7) | copy-start | bytes 1572868
  42.2 15.7 %copy-start.10 = (bf16[128,2048]{1,0:T(8,128)(2,1)S(1)}, bf16[128,2048]{1,0:T(8,128)(2,1)}, u32[]{:S(2)}) copy-start(bf16[128,2048]{1,0:T(8,128)(2,1)} %copy-done.9) | copy-start | bytes 1572868
  52.8 13.0 %collective-permute-start.5 = (bf16[128,2048]{1,0:T(8,128)(2,1)}, bf16[128,2048]{1,0:T(8,128)(2,1)}, u32[]{:S(2)}, u32[]{:S(2)}) collective-permute-start(bf16[128,2048]{1,0:T(8,128)(2,1)} %collective-permute-done.4), channel_id=1, source_target_pairs={{0,4},{4,8},{8,12},{12,14},{14,10},{10,6},{6,2},{2,0},{1,5},{5,9},... | collective-permute-start | bytes 1572872 | tf_op jit(solution)/shard_map/ppermute | solution.py:174
  54.1 13.0 %collective-permute-start.7 = (bf16[128,2048]{1,0:T(8,128)(2,1)}, bf16[128,2048]{1,0:T(8,128)(2,1)}, u32[]{:S(2)}, u32[]{:S(2)}) collective-permute-start(bf16[128,2048]{1,0:T(8,128)(2,1)} %collective-permute-done.6), channel_id=1, source_target_pairs={{4,0},{8,4},{12,8},{14,12},{10,14},{6,10},{2,6},{0,2},{5,1},{9,5},... | collective-permute-start | bytes 1572872 | tf_op jit(solution)/shard_map/ppermute | solution.py:175
  56.4 2.4 %copy-start.11 = (bf16[1024,2048]{1,0:T(8,128)(2,1)}, bf16[1024,2048]{1,0:T(8,128)(2,1)S(1)}, u32[]{:S(2)}) copy-start(bf16[1024,2048]{1,0:T(8,128)(2,1)S(1)} %constant_dynamic-update-slice_fusion.6) | copy-start | bytes 12582916
  56.6 10.7 %collective-permute-start.3 = (bf16[8,8,2048]{2,1,0:T(8,128)(2,1)S(1)}, bf16[8,8,2048]{2,1,0:T(8,128)(2,1)S(1)}, u32[]{:S(2)}, u32[]{:S(2)}) collective-permute-start(bf16[8,8,2048]{2,1,0:T(8,128)(2,1)S(1)} %slice_bitcast_fusion.1), channel_id=1, source_target_pairs={{16,0},{17,1},{18,2},{19,3},{20,4},{21,5},{22,6},{23,7},{24,8},{25... | collective-permute-start | bytes 786440 | tf_op jit(solution)/shard_map/ppermute | solution.py:161
  65.8 12.0 %collective-permute-start.8 = (bf16[128,2048]{1,0:T(8,128)(2,1)}, bf16[128,2048]{1,0:T(8,128)(2,1)S(1)}, u32[]{:S(2)}, u32[]{:S(2)}) collective-permute-start(bf16[128,2048]{1,0:T(8,128)(2,1)} %collective-permute-done.5), channel_id=1, source_target_pairs={{0,4},{4,8},{8,12},{12,14},{14,10},{10,6},{6,2},{2,0},{1,5},{5,9},... | collective-permute-start | bytes 1572872 | tf_op jit(solution)/shard_map/ppermute | solution.py:174
  67.1 12.1 %collective-permute-start.9 = (bf16[128,2048]{1,0:T(8,128)(2,1)}, bf16[128,2048]{1,0:T(8,128)(2,1)S(1)}, u32[]{:S(2)}, u32[]{:S(2)}) collective-permute-start(bf16[128,2048]{1,0:T(8,128)(2,1)} %collective-permute-done.7), channel_id=1, source_target_pairs={{4,0},{8,4},{12,8},{14,12},{10,14},{6,10},{2,6},{0,2},{5,1},{9,5},... | collective-permute-start | bytes 1572872 | tf_op jit(solution)/shard_map/ppermute | solution.py:175
  68.2 33.7 %all-to-all-start = ((bf16[8,192,256]{2,1,0:T(8,128)(2,1)}), bf16[8,192,256]{2,1,0:T(8,128)(2,1)S(1)}, u32[]{:S(2)}, u32[]{:S(2)}) async-start(bf16[8,192,256]{2,1,0:T(8,128)(2,1)} %pad_maximum_fusion), calls=%async_computation | async-start | bytes 1572864 | tf_op jit(solution)/shard_map/all_to_all | solution.py:183
  77.7 21.5 %collective-permute-start.10 = (bf16[64,2048]{1,0:T(8,128)(2,1)S(1)}, bf16[64,2048]{1,0:T(8,128)(2,1)S(1)}, u32[]{:S(2)}, u32[]{:S(2)}) collective-permute-start(bf16[64,2048]{1,0:T(8,128)(2,1)S(1)} %slice.35), channel_id=1, source_target_pairs={{0,4},{4,8},{8,12},{12,14},{14,10},{10,6},{6,2},{2,0},{1,5},{5,9},... | collective-permute-start | bytes 786440 | tf_op jit(solution)/shard_map/ppermute | solution.py:190
  79.2 22.0 %collective-permute-start.11 = (bf16[64,2048]{1,0:T(8,128)(2,1)S(1)}, bf16[64,2048]{1,0:T(8,128)(2,1)S(1)}, u32[]{:S(2)}, u32[]{:S(2)}) collective-permute-start(bf16[64,2048]{1,0:T(8,128)(2,1)S(1)} %slice.36), channel_id=1, source_target_pairs={{4,0},{8,4},{12,8},{14,12},{10,14},{6,10},{2,6},{0,2},{5,1},{9,5},... | collective-permute-start | bytes 786440 | tf_op jit(solution)/shard_map/ppermute | solution.py:191
  101.9 6.1 %copy-start.12 = (bf16[1024,2048]{1,0:T(8,128)(2,1)S(1)}, bf16[1024,2048]{1,0:T(8,128)(2,1)}, u32[]{:S(2)}) copy-start(bf16[1024,2048]{1,0:T(8,128)(2,1)} %constant_dynamic-update-slice_fusion) | copy-start | bytes 12582916
  105.1 5.2 %collective-permute-start.12 = (f32[128,2048]{1,0:T(8,128)S(1)}, f32[128,2048]{1,0:T(8,128)S(1)}, u32[]{:S(2)}, u32[]{:S(2)}) collective-permute-start(f32[128,2048]{1,0:T(8,128)S(1)} %fusion.7), channel_id=1, source_target_pairs={{0,1},{1,0},{2,3},{3,2},{4,5},{5,4},{6,7},{7,6},{8,9},{9,8},{10,11... | collective-permute-start | bytes 3145736 | tf_op jit(solution)/shard_map/ppermute | solution.py:20

commit v9 on v7

--- a/solution.py
+++ b/solution.py
@@ -8,7 +8,7 @@
 
 F32 = jnp.float32
 BF16 = jnp.bfloat16
-TILE = 256
+TILE = 512
 GRANT = 16 * 1024 * 1024
 
 

time: 113 us -> 112 us (level)
  Pallas kernels: 11.6 us -> 10.2 us
    pallas_call x1, Pallas kernels: 8.75 us -> 7.28 us  [trail(): pl.pallas_call(trail_body, out_shape=(jax.ShapeDtypeStruct((rows_dev, hid...]
where the time goes in v9:
time: 112 us; the launch traced here: 110 us
  waiting for transfers between devices  44.5 us (40%)
  local copies, waits for them, and re-layouts  24.4 us (22%)
  starting transfers between devices  21.9 us (20%)
  Pallas kernels  10.2 us (9%)
  matrix products  4.17 us (4%)
  other arithmetic  3.9 us (3%)
    ppermute x1, waiting for transfers between devices, local(): blocks.append((lax.ppermute(fwd[:mid], 'chip', up), chips // 2, 0))  18.3 us
    ppermute x3, waiting for transfers between devices, local(): fwd = lax.ppermute(fwd, 'chip', up)  16.3 us
    unnamed x28, local copies, waits for them, and re-layouts  11.4 us
    dynamic_update_slice x9, local copies, waits for them, and re-layouts, local(): right_all = lax.dynamic_update_slice_in_dim(right_all, block, start, 0)  10.2 us
    ppermute x1, waiting for transfers between devices, local(): query = lax.ppermute(own_query, 'hop', [(0, 1)])  7.79 us
    pallas_call x1, Pallas kernels, trail(): pl.pallas_call(trail_body, out_shape=(jax.ShapeDtypeStruct((rows_dev, hid...  7.28 us
    all_to_all x1, starting transfers between devices, local(): received = lax.all_to_all(sent, 'chip', 0, 0, tiled=True)  5.73 us
    ppermute x2, starting transfers between devices, swap_core(): return lax.ppermute(block, 'core', [(0, 1), (1, 0)])  4.47 us
  transfers between devices with their start and end apart: 14, of which 6 were waited for; matrix products, arithmetic and copies ran while one was open for 15% of the time, Pallas kernels for 0%

profile of v9, /device:TPU:9, one launch (start us, length us, event | category | flops | bytes accessed | tf_op | source)
XLA Modules:
  0.0 109.9 jit_solution(3919426894878098535)
XLA Ops:
  0.7 3.5 %copy-done.1 = bf16[1,2048,2048]{2,1,0:T(8,128)(2,1)S(1)} copy-done((bf16[1,2048,2048]{2,1,0:T(8,128)(2,1)S(1)}, bf16[1,2048,2048]{2,1,0:T(8,128)(2,1)}, u32[]{:S(2)}) %copy-start.1) | copy-done | bytes 8388632
  4.1 1.0 copy-done.3
  5.2 2.9 %shard_map.67 = bf16[2,128,1024]{2,1,0:T(8,128)(2,1)S(1)} custom-call(bf16[128,2048]{1,0:T(8,128)(2,1)S(1)} %bitcast.42, bf16[2048,2048]{1,0:T(8,128)(2,1)S(1)} %bitcast.40), custom_call_target="tpu_custom_call" | custom-call | flops 1073741824 | bytes 8388608 | tf_op jit(solution)/shard_map/pallas_call | solution.py:43
  8.1 3.1 %collective-permute-start = (bf16[2,128,1024]{2,1,0:T(8,128)(2,1)S(1)}, bf16[2,128,1024]{2,1,0:T(8,128)(2,1)S(1)}, u32[]{:S(2)}, u32[]{:S(2)}) collective-permute-start(bf16[2,128,1024]{2,1,0:T(8,128)(2,1)S(1)} %shard_map.67), channel_id=1, source_target_pairs={{0,16},{1,17},{2,18},{3,19},{4,20},{5,21},{6,22},{7,23},{8,24},{9,... | collective-permute-start | bytes 1572872 | tf_op jit(solution)/shard_map/ppermute | solution.py:151
  11.2 0.3 convolution_convert_fusion
  11.6 1.0 copy.9
  12.6 1.2 %copy.10 = bf16[128,2,1024]{2,0,1:T(8,128)(2,1)S(1)} copy(bf16[128,2,1024]{0,2,1:T(8,128)(2,1)} %bitcast.48) | data formatting | bytes 1048576 | tf_op jit(solution)/shard_map/reshape | solution.py:153
  14.0 7.8 %collective-permute-done.query = bf16[2,128,1024]{2,1,0:T(8,128)(2,1)S(1)} collective-permute-done((bf16[2,128,1024]{2,1,0:T(8,128)(2,1)S(1)}, bf16[2,128,1024]{2,1,0:T(8,128)(2,1)S(1)}, u32[]{:S(2)}, u32[]{:S(2)}) %collective-permute-start) | collective-permute-done | bytes 524320 | tf_op jit(solution)/shard_map/ppermute | solution.py:151
  21.8 0.8 copy-done.5
  22.6 3.4 %copy-done.2 = bf16[1,2048,2048]{2,1,0:T(8,128)(2,1)S(1)} copy-done((bf16[1,2048,2048]{2,1,0:T(8,128)(2,1)S(1)}, bf16[1,2048,2048]{2,1,0:T(8,128)(2,1)}, u32[]{:S(2)}) %copy-start.2) | copy-done | bytes 8388632
  25.9 1.0 copy-done.6
  27.0 7.3 %shard_map.68 = (bf16[128,2048]{1,0:T(8,128)(2,1)}, bf16[128,2048]{1,0:T(8,128)(2,1)S(1)}, f32[128,2048]{1,0:T(8,128)}, f32[128,2048]{1,0:T(8,128)S(1)}, bf16[128,2048]{1,0:T(8,128)(2,1)S(1)}) custom-call(s32[1]{0:T(128)} %bitcast.first, bf16[2,128,1024]{2,1,0:T(8,128)(2,1)S(1)} %copy-done.6, bf16[128,2048]{1,0:T(8,128)(2,1)S(1)} %bitcast.43, ...), custom_call_target="tpu_custom_call" | custom-call | flops 2415919104 | bytes 16777216 | tf_op jit(solution)/shard_map/pallas_call | solution.py:105
  34.3 0.8 copy-done.7
  35.1 0.8 copy-done.9
  35.9 1.5 %collective-permute-start.2 = (f32[128,2048]{1,0:T(8,128)}, f32[128,2048]{1,0:T(8,128)S(1)}, u32[]{:S(2)}, u32[]{:S(2)}) collective-permute-start(f32[128,2048]{1,0:T(8,128)} %get-tuple-element.12), channel_id=1, source_target_pairs={{0,1},{1,0},{2,3},{3,2},{4,5},{5,4},{6,7},{7,6},{8,9},{9,8},{10,11... | collective-permute-start | bytes 3145736 | tf_op jit(solution)/shard_map/ppermute | solution.py:20
  37.4 1.3 %collective-permute-start.4 = (bf16[128,2048]{1,0:T(8,128)(2,1)}, bf16[128,2048]{1,0:T(8,128)(2,1)}, u32[]{:S(2)}, u32[]{:S(2)}) collective-permute-start(bf16[128,2048]{1,0:T(8,128)(2,1)} %get-tuple-element.15), channel_id=1, source_target_pairs={{0,4},{4,8},{8,12},{12,14},{14,10},{10,6},{6,2},{2,0},{1,5},{5,9},... | collective-permute-start | bytes 1572872 | tf_op jit(solution)/shard_map/ppermute | solution.py:174
  38.7 0.2 collective-permute-start.6
  38.9 1.3 %collective-permute-start.1 = (bf16[128,2048]{1,0:T(8,128)(2,1)}, bf16[128,2048]{1,0:T(8,128)(2,1)S(1)}, u32[]{:S(2)}, u32[]{:S(2)}) collective-permute-start(bf16[128,2048]{1,0:T(8,128)(2,1)} %copy-done.7), channel_id=1, source_target_pairs={{16,0},{17,1},{18,2},{19,3},{20,4},{21,5},{22,6},{23,7},{24,8},{25... | collective-permute-start | bytes 1572872 | tf_op jit(solution)/shard_map/ppermute | solution.py:157
  40.2 0.5 broadcast_in_dim.20
  40.7 1.2 %constant_dynamic-update-slice_fusion.8 = bf16[1024,2048]{1,0:T(8,128)(2,1)S(1)} fusion(bf16[1024,2048]{1,0:T(8,128)(2,1)S(1)} %broadcast_in_dim.20, bf16[128,2048]{1,0:T(8,128)(2,1)} %get-tuple-element.15, s32[]{:T(128)S(6)} %select_n.166), kind=kLoop, calls=%fused_computation.25 | loop fusion | bytes 1048580 | tf_op jit(solution)/shard_map/dynamic_update_slice | solution.py:195
  41.9 9.4 %collective-permute-done.4 = bf16[128,2048]{1,0:T(8,128)(2,1)} collective-permute-done((bf16[128,2048]{1,0:T(8,128)(2,1)}, bf16[128,2048]{1,0:T(8,128)(2,1)}, u32[]{:S(2)}, u32[]{:S(2)}) %collective-permute-start.4) | collective-permute-done | bytes 524320 | tf_op jit(solution)/shard_map/ppermute | solution.py:174
  51.3 1.3 %collective-permute-start.5 = (bf16[128,2048]{1,0:T(8,128)(2,1)}, bf16[128,2048]{1,0:T(8,128)(2,1)}, u32[]{:S(2)}, u32[]{:S(2)}) collective-permute-start(bf16[128,2048]{1,0:T(8,128)(2,1)} %collective-permute-done.4), channel_id=1, source_target_pairs={{0,4},{4,8},{8,12},{12,14},{14,10},{10,6},{6,2},{2,0},{1,5},{5,9},... | collective-permute-start | bytes 1572872 | tf_op jit(solution)/shard_map/ppermute | solution.py:174
  52.6 0.2 collective-permute-start.7
  52.7 1.1 constant_dynamic-update-slice_fusion.7
  53.8 1.1 constant_dynamic-update-slice_fusion.6
  54.9 0.1 add_convert_fusion
  55.1 1.3 %collective-permute-start.3 = (bf16[8,8,2048]{2,1,0:T(8,128)(2,1)S(1)}, bf16[8,8,2048]{2,1,0:T(8,128)(2,1)S(1)}, u32[]{:S(2)}, u32[]{:S(2)}) collective-permute-start(bf16[8,8,2048]{2,1,0:T(8,128)(2,1)S(1)} %slice_bitcast_fusion.1), channel_id=1, source_target_pairs={{16,0},{17,1},{18,2},{19,3},{20,4},{21,5},{22,6},{23,7},{24,8},{25... | collective-permute-start | bytes 786440 | tf_op jit(solution)/shard_map/ppermute | solution.py:161
  56.4 0.9 broadcast_select_fusion
  57.3 6.9 %collective-permute-done.5 = bf16[128,2048]{1,0:T(8,128)(2,1)} collective-permute-done((bf16[128,2048]{1,0:T(8,128)(2,1)}, bf16[128,2048]{1,0:T(8,128)(2,1)}, u32[]{:S(2)}, u32[]{:S(2)}) %collective-permute-start.5) | collective-permute-done | bytes 524320 | tf_op jit(solution)/shard_map/ppermute | solution.py:174
  64.3 1.3 %collective-permute-start.8 = (bf16[128,2048]{1,0:T(8,128)(2,1)}, bf16[128,2048]{1,0:T(8,128)(2,1)S(1)}, u32[]{:S(2)}, u32[]{:S(2)}) collective-permute-start(bf16[128,2048]{1,0:T(8,128)(2,1)} %collective-permute-done.5), channel_id=1, source_target_pairs={{0,4},{4,8},{8,12},{12,14},{14,10},{10,6},{6,2},{2,0},{1,5},{5,9},... | collective-permute-start | bytes 1572872 | tf_op jit(solution)/shard_map/ppermute | solution.py:174
  65.6 0.2 collective-permute-start.9
  65.8 0.9 pad_maximum_fusion
  66.7 5.7 %all-to-all-start = ((bf16[8,192,256]{2,1,0:T(8,128)(2,1)}), bf16[8,192,256]{2,1,0:T(8,128)(2,1)S(1)}, u32[]{:S(2)}, u32[]{:S(2)}) async-start(bf16[8,192,256]{2,1,0:T(8,128)(2,1)} %pad_maximum_fusion), calls=%async_computation | async-start | bytes 1572864 | tf_op jit(solution)/shard_map/all_to_all | solution.py:183
  72.4 1.9 %constant_dynamic-update-slice_fusion.5 = bf16[1024,2048]{1,0:T(8,128)(2,1)} fusion(bf16[1024,2048]{1,0:T(8,128)(2,1)} %copy-done.11, bf16[128,2048]{1,0:T(8,128)(2,1)} %collective-permute-done.5, s32[]{:T(128)S(6)} %select_n.172), kind=kLoop, calls=%fused_computation.22 | loop fusion | bytes 1048580 | tf_op jit(solution)/shard_map/dynamic_update_slice | solution.py:195
  74.3 1.9 %constant_dynamic-update-slice_fusion.4 = bf16[1024,2048]{1,0:T(8,128)(2,1)} fusion(bf16[1024,2048]{1,0:T(8,128)(2,1)} %constant_dynamic-update-slice_fusion.5, bf16[128,2048]{1,0:T(8,128)(2,1)} %collective-permute-done.7, s32[]{:T(128)S(6)} %select_n.174), kind=kLoop, calls=%fused_computation.21 | loop fusion | bytes 1048580 | tf_op jit(solution)/shard_map/dynamic_update_slice | solution.py:195
  76.2 1.5 %collective-permute-start.10 = (bf16[64,2048]{1,0:T(8,128)(2,1)S(1)}, bf16[64,2048]{1,0:T(8,128)(2,1)S(1)}, u32[]{:S(2)}, u32[]{:S(2)}) collective-permute-start(bf16[64,2048]{1,0:T(8,128)(2,1)S(1)} %slice.35), channel_id=1, source_target_pairs={{0,4},{4,8},{8,12},{12,14},{14,10},{10,6},{6,2},{2,0},{1,5},{5,9},... | collective-permute-start | bytes 786440 | tf_op jit(solution)/shard_map/ppermute | solution.py:190
  77.8 0.8 constant_dynamic-update-slice_fusion.3
  78.7 0.8 constant_dynamic-update-slice_fusion.2
  79.5 18.3 %collective-permute-done.10 = bf16[64,2048]{1,0:T(8,128)(2,1)S(1)} collective-permute-done((bf16[64,2048]{1,0:T(8,128)(2,1)S(1)}, bf16[64,2048]{1,0:T(8,128)(2,1)S(1)}, u32[]{:S(2)}, u32[]{:S(2)}) %collective-permute-start.10) | collective-permute-done | bytes 262176 | tf_op jit(solution)/shard_map/ppermute | solution.py:190
  97.8 0.7 constant_dynamic-update-slice_fusion.1
  98.5 1.2 %collective-permute-done.11 = bf16[64,2048]{1,0:T(8,128)(2,1)S(1)} collective-permute-done((bf16[64,2048]{1,0:T(8,128)(2,1)S(1)}, bf16[64,2048]{1,0:T(8,128)(2,1)S(1)}, u32[]{:S(2)}, u32[]{:S(2)}) %collective-permute-start.11) | collective-permute-done | bytes 262176 | tf_op jit(solution)/shard_map/ppermute | solution.py:191
  99.7 0.7 constant_dynamic-update-slice_fusion
  100.5 3.1 %fusion.7 = f32[128,2048]{1,0:T(8,128)S(1)} fusion(bf16[1024,128]{1,0:T(8,128)(2,1)S(1)} %bitcast.52, bf16[1024,2048]{1,0:T(8,128)(2,1)} %constant_dynamic-update-slice_fusion), kind=kOutput, calls=%fused_computation.48 | convolution fusion | flops 536870912 | bytes 5505024 | tf_op jit(solution)/shard_map/dot_general | solution.py:16
  103.6 2.9 %collective-permute-start.12 = (f32[128,2048]{1,0:T(8,128)S(1)}, f32[128,2048]{1,0:T(8,128)S(1)}, u32[]{:S(2)}, u32[]{:S(2)}) collective-permute-start(f32[128,2048]{1,0:T(8,128)S(1)} %fusion.7), channel_id=1, source_target_pairs={{0,1},{1,0},{2,3},{3,2},{4,5},{5,4},{6,7},{7,6},{8,9},{9,8},{10,11... | collective-permute-start | bytes 3145736 | tf_op jit(solution)/shard_map/ppermute | solution.py:20
  106.5 0.7 fusion.6
  107.3 0.6 broadcast_multiply_fusion
  107.9 0.9 collective-permute-done.12
  108.8 1.1 %multiply_bitcast_fusion = f32[1,128,2048]{2,1,0:T(8,128)} fusion(f32[128,2048]{1,0:T(8,128)S(1)} %fusion.6, f32[128,2048]{1,0:T(8,128)S(1)} %collective-permute-done.12), kind=kLoop, calls=%fused_computation.1 | loop fusion | flops 524288 | bytes 3145728 | tf_op jit(solution)/shard_map/broadcast_in_dim | solution.py:202
  (39 shorter events, 0.5 us)
Async XLA Ops:
  0.6 10.6 %copy-start = (bf16[256,2048]{1,0:T(8,128)(2,1)S(1)}, bf16[256,2048]{1,0:T(8,128)(2,1)}, u32[]{:S(2)}) copy-start(bf16[256,2048]{1,0:T(8,128)(2,1)} %param.6) | copy-start | bytes 3145732
  0.6 3.5 %copy-start.1 = (bf16[1,2048,2048]{2,1,0:T(8,128)(2,1)S(1)}, bf16[1,2048,2048]{2,1,0:T(8,128)(2,1)}, u32[]{:S(2)}) copy-start(bf16[1,2048,2048]{2,1,0:T(8,128)(2,1)} %param.5) | copy-start | bytes 25165828
  4.1 1.0 copy-start.3
  5.2 6.1 %copy-start.13 = (s32[128]{0:T(128)S(1)}, s32[128]{0:T(128)}, u32[]{:S(2)}) copy-start(s32[128]{0:T(128)} %param.7) | copy-start | bytes 1540
  5.2 17.4 %copy-start.4 = (bf16[1,128,2048]{2,1,0:T(8,128)(2,1)S(1)}, bf16[1,128,2048]{2,1,0:T(8,128)(2,1)}, u32[]{:S(2)}) copy-start(bf16[1,128,2048]{2,1,0:T(8,128)(2,1)} %param.4) | copy-start | bytes 1572868
  8.1 13.7 %collective-permute-start = (bf16[2,128,1024]{2,1,0:T(8,128)(2,1)S(1)}, bf16[2,128,1024]{2,1,0:T(8,128)(2,1)S(1)}, u32[]{:S(2)}, u32[]{:S(2)}) collective-permute-start(bf16[2,128,1024]{2,1,0:T(8,128)(2,1)S(1)} %shard_map.67), channel_id=1, source_target_pairs={{0,16},{1,17},{2,18},{3,19},{4,20},{5,21},{6,22},{7,23},{8,24},{9,... | collective-permute-start | bytes 1572872 | tf_op jit(solution)/shard_map/ppermute | solution.py:151
  21.8 0.8 copy-start.5
  22.6 3.4 %copy-start.2 = (bf16[1,2048,2048]{2,1,0:T(8,128)(2,1)S(1)}, bf16[1,2048,2048]{2,1,0:T(8,128)(2,1)}, u32[]{:S(2)}) copy-start(bf16[1,2048,2048]{2,1,0:T(8,128)(2,1)} %param.5) | copy-start | bytes 25165828
  25.9 1.0 copy-start.6
  34.3 0.8 copy-start.7
  35.1 0.8 copy-start.9
  35.9 19.1 %collective-permute-start.2 = (f32[128,2048]{1,0:T(8,128)}, f32[128,2048]{1,0:T(8,128)S(1)}, u32[]{:S(2)}, u32[]{:S(2)}) collective-permute-start(f32[128,2048]{1,0:T(8,128)} %get-tuple-element.12), channel_id=1, source_target_pairs={{0,1},{1,0},{2,3},{3,2},{4,5},{5,4},{6,7},{7,6},{8,9},{9,8},{10,11... | collective-permute-start | bytes 3145736 | tf_op jit(solution)/shard_map/ppermute | solution.py:20
  37.4 13.9 %collective-permute-start.4 = (bf16[128,2048]{1,0:T(8,128)(2,1)}, bf16[128,2048]{1,0:T(8,128)(2,1)}, u32[]{:S(2)}, u32[]{:S(2)}) collective-permute-start(bf16[128,2048]{1,0:T(8,128)(2,1)} %get-tuple-element.15), channel_id=1, source_target_pairs={{0,4},{4,8},{8,12},{12,14},{14,10},{10,6},{6,2},{2,0},{1,5},{5,9},... | collective-permute-start | bytes 1572872 | tf_op jit(solution)/shard_map/ppermute | solution.py:174
  38.7 13.9 %collective-permute-start.6 = (bf16[128,2048]{1,0:T(8,128)(2,1)}, bf16[128,2048]{1,0:T(8,128)(2,1)}, u32[]{:S(2)}, u32[]{:S(2)}) collective-permute-start(bf16[128,2048]{1,0:T(8,128)(2,1)} %get-tuple-element.15), channel_id=1, source_target_pairs={{4,0},{8,4},{12,8},{14,12},{10,14},{6,10},{2,6},{0,2},{5,1},{9,5},... | collective-permute-start | bytes 1572872 | tf_op jit(solution)/shard_map/ppermute | solution.py:175
  38.9 17.5 %collective-permute-start.1 = (bf16[128,2048]{1,0:T(8,128)(2,1)}, bf16[128,2048]{1,0:T(8,128)(2,1)S(1)}, u32[]{:S(2)}, u32[]{:S(2)}) collective-permute-start(bf16[128,2048]{1,0:T(8,128)(2,1)} %copy-done.7), channel_id=1, source_target_pairs={{16,0},{17,1},{18,2},{19,3},{20,4},{21,5},{22,6},{23,7},{24,8},{25... | collective-permute-start | bytes 1572872 | tf_op jit(solution)/shard_map/ppermute | solution.py:157
  40.7 15.7 %copy-start.8 = (bf16[128,2048]{1,0:T(8,128)(2,1)S(1)}, bf16[128,2048]{1,0:T(8,128)(2,1)}, u32[]{:S(2)}) copy-start(bf16[128,2048]{1,0:T(8,128)(2,1)} %copy-done.7) | copy-start | bytes 1572868
  40.7 15.7 %copy-start.10 = (bf16[128,2048]{1,0:T(8,128)(2,1)S(1)}, bf16[128,2048]{1,0:T(8,128)(2,1)}, u32[]{:S(2)}) copy-start(bf16[128,2048]{1,0:T(8,128)(2,1)} %copy-done.9) | copy-start | bytes 1572868
  51.3 13.0 %collective-permute-start.5 = (bf16[128,2048]{1,0:T(8,128)(2,1)}, bf16[128,2048]{1,0:T(8,128)(2,1)}, u32[]{:S(2)}, u32[]{:S(2)}) collective-permute-start(bf16[128,2048]{1,0:T(8,128)(2,1)} %collective-permute-done.4), channel_id=1, source_target_pairs={{0,4},{4,8},{8,12},{12,14},{14,10},{10,6},{6,2},{2,0},{1,5},{5,9},... | collective-permute-start | bytes 1572872 | tf_op jit(solution)/shard_map/ppermute | solution.py:174
  52.6 13.0 %collective-permute-start.7 = (bf16[128,2048]{1,0:T(8,128)(2,1)}, bf16[128,2048]{1,0:T(8,128)(2,1)}, u32[]{:S(2)}, u32[]{:S(2)}) collective-permute-start(bf16[128,2048]{1,0:T(8,128)(2,1)} %collective-permute-done.6), channel_id=1, source_target_pairs={{4,0},{8,4},{12,8},{14,12},{10,14},{6,10},{2,6},{0,2},{5,1},{9,5},... | collective-permute-start | bytes 1572872 | tf_op jit(solution)/shard_map/ppermute | solution.py:175
  54.9 2.4 %copy-start.11 = (bf16[1024,2048]{1,0:T(8,128)(2,1)}, bf16[1024,2048]{1,0:T(8,128)(2,1)S(1)}, u32[]{:S(2)}) copy-start(bf16[1024,2048]{1,0:T(8,128)(2,1)S(1)} %constant_dynamic-update-slice_fusion.6) | copy-start | bytes 12582916
  55.1 10.7 %collective-permute-start.3 = (bf16[8,8,2048]{2,1,0:T(8,128)(2,1)S(1)}, bf16[8,8,2048]{2,1,0:T(8,128)(2,1)S(1)}, u32[]{:S(2)}, u32[]{:S(2)}) collective-permute-start(bf16[8,8,2048]{2,1,0:T(8,128)(2,1)S(1)} %slice_bitcast_fusion.1), channel_id=1, source_target_pairs={{16,0},{17,1},{18,2},{19,3},{20,4},{21,5},{22,6},{23,7},{24,8},{25... | collective-permute-start | bytes 786440 | tf_op jit(solution)/shard_map/ppermute | solution.py:161
  64.3 12.0 %collective-permute-start.8 = (bf16[128,2048]{1,0:T(8,128)(2,1)}, bf16[128,2048]{1,0:T(8,128)(2,1)S(1)}, u32[]{:S(2)}, u32[]{:S(2)}) collective-permute-start(bf16[128,2048]{1,0:T(8,128)(2,1)} %collective-permute-done.5), channel_id=1, source_target_pairs={{0,4},{4,8},{8,12},{12,14},{14,10},{10,6},{6,2},{2,0},{1,5},{5,9},... | collective-permute-start | bytes 1572872 | tf_op jit(solution)/shard_map/ppermute | solution.py:174
  65.6 12.1 %collective-permute-start.9 = (bf16[128,2048]{1,0:T(8,128)(2,1)}, bf16[128,2048]{1,0:T(8,128)(2,1)S(1)}, u32[]{:S(2)}, u32[]{:S(2)}) collective-permute-start(bf16[128,2048]{1,0:T(8,128)(2,1)} %collective-permute-done.7), channel_id=1, source_target_pairs={{4,0},{8,4},{12,8},{14,12},{10,14},{6,10},{2,6},{0,2},{5,1},{9,5},... | collective-permute-start | bytes 1572872 | tf_op jit(solution)/shard_map/ppermute | solution.py:175
  66.7 33.7 %all-to-all-start = ((bf16[8,192,256]{2,1,0:T(8,128)(2,1)}), bf16[8,192,256]{2,1,0:T(8,128)(2,1)S(1)}, u32[]{:S(2)}, u32[]{:S(2)}) async-start(bf16[8,192,256]{2,1,0:T(8,128)(2,1)} %pad_maximum_fusion), calls=%async_computation | async-start | bytes 1572864 | tf_op jit(solution)/shard_map/all_to_all | solution.py:183
  76.2 21.5 %collective-permute-start.10 = (bf16[64,2048]{1,0:T(8,128)(2,1)S(1)}, bf16[64,2048]{1,0:T(8,128)(2,1)S(1)}, u32[]{:S(2)}, u32[]{:S(2)}) collective-permute-start(bf16[64,2048]{1,0:T(8,128)(2,1)S(1)} %slice.35), channel_id=1, source_target_pairs={{0,4},{4,8},{8,12},{12,14},{14,10},{10,6},{6,2},{2,0},{1,5},{5,9},... | collective-permute-start | bytes 786440 | tf_op jit(solution)/shard_map/ppermute | solution.py:190
  77.7 22.0 %collective-permute-start.11 = (bf16[64,2048]{1,0:T(8,128)(2,1)S(1)}, bf16[64,2048]{1,0:T(8,128)(2,1)S(1)}, u32[]{:S(2)}, u32[]{:S(2)}) collective-permute-start(bf16[64,2048]{1,0:T(8,128)(2,1)S(1)} %slice.36), channel_id=1, source_target_pairs={{4,0},{8,4},{12,8},{14,12},{10,14},{6,10},{2,6},{0,2},{5,1},{9,5},... | collective-permute-start | bytes 786440 | tf_op jit(solution)/shard_map/ppermute | solution.py:191
  100.4 6.1 %copy-start.12 = (bf16[1024,2048]{1,0:T(8,128)(2,1)S(1)}, bf16[1024,2048]{1,0:T(8,128)(2,1)}, u32[]{:S(2)}) copy-start(bf16[1024,2048]{1,0:T(8,128)(2,1)} %constant_dynamic-update-slice_fusion) | copy-start | bytes 12582916
  103.6 5.2 %collective-permute-start.12 = (f32[128,2048]{1,0:T(8,128)S(1)}, f32[128,2048]{1,0:T(8,128)S(1)}, u32[]{:S(2)}, u32[]{:S(2)}) collective-permute-start(f32[128,2048]{1,0:T(8,128)S(1)} %fusion.7), channel_id=1, source_target_pairs={{0,1},{1,0},{2,3},{3,2},{4,5},{5,4},{6,7},{7,6},{8,9},{9,8},{10,11... | collective-permute-start | bytes 3145736 | tf_op jit(solution)/shard_map/ppermute | solution.py:20
